TPU v7x, 128 devices: a whole 4x4x4 slice. The times are simulated.
128 devices in a mesh: ka: 4 (over x_hi, core), band: 32 (over y, x_lo, z).
Axes of the slice: x: 4 (x_hi: 2, x_lo: 2; x = x_hi * 2 + x_lo), y: 4, z: 4, core: 2. Of those that a mesh axis runs over, the one named last changes fastest.
Arguments:
- occ_orb: float32 [8, 64, 2, 4096], P('ka'), may hold values from -6 to 6
- occ_energy: float32 [8, 64], P('ka'), may hold values from -6 to -0.5
- emp_orb: float32 [8, 64, 2, 4096], P('ka', 'band'), may hold values from -6 to 6
- emp_energy: float32 [8, 64], P('ka', 'band'), may hold values from 0.5 to 8
- gidx: int32 [2048], replicated, may hold values from 0 to 4095, as said below
- sym_map: int32 [8, 2048], P('ka'), may hold values from 0 to 2047, as said below
- weights: int32 [8], replicated, may hold values from 1 to 8
- count: int32 [8], replicated, may hold values from 16 to 64, as said below
Outputs:
- chi_rows: float32 [1, 1024, 2, 2048], P(None, ('ka', 'band'))
Inputs may be any that keep to these rules, and one draw needn't show every extreme that they name: `gidx`: distinct values; 0 and 4095 are among them. `sym_map`: each row is a permutation of 0 to 2047. `count`: some k point has all 64 empty bands, another has 16.
All inputs are finite; a program needn't handle non-finite values.
Results may differ from a plain program's by a relative error of at most 0.0003.
Values sent between devices are 32-bit elements; how exact they have to be, the bound alone decides.
No kernel may reach another device: no remote copies, remote signals or barrier semaphores. Data moves between devices by JAX's collectives and lax.ppermute only.
A program may use at most 128 MiB of HBM per device.

v0:
```python
import math

import jax
import jax.numpy as jnp
from jax import lax
from jax.sharding import PartitionSpec as P

GA = 16
GB = 16
GC = 16
NGC = 1024


def passed_along(shard, axis, by):
    devices = lax.axis_size(axis)
    return lax.ppermute(shard, axis, [(i, (i + by) % devices) for i in range(devices)])


def plane_phase(size_b, size_c):
    line = jnp.arange(size_b * size_c, dtype=jnp.int32)
    outer = line // size_c
    inner = line % size_c
    turns = (outer[:, None] * outer[None, :] % size_b).astype(jnp.float32) / size_b
    turns = turns + (inner[:, None] * inner[None, :] % size_c).astype(jnp.float32) / size_c
    angle = -2.0 * math.pi * turns
    return (jnp.cos(angle), jnp.sin(angle))


def line_phase(size_a):
    line = jnp.arange(size_a, dtype=jnp.int32)
    turns = (line[:, None] * line[None, :] % size_a).astype(jnp.float32) / size_a
    angle = -2.0 * math.pi * turns
    return (jnp.cos(angle), jnp.sin(angle))


def transform(real_pair, imag_pair, plane_cos, plane_sin, line_cos, line_sin):
    highest = lax.Precision.HIGHEST
    first_real = jnp.einsum("pal,lm->pam", real_pair, plane_cos, precision=highest) - jnp.einsum(
        "pal,lm->pam", imag_pair, plane_sin, precision=highest
    )
    first_imag = jnp.einsum("pal,lm->pam", real_pair, plane_sin, precision=highest) + jnp.einsum(
        "pal,lm->pam", imag_pair, plane_cos, precision=highest
    )
    second_real = jnp.einsum("pam,ab->pbm", first_real, line_cos, precision=highest) - jnp.einsum(
        "pam,ab->pbm", first_imag, line_sin, precision=highest
    )
    second_imag = jnp.einsum("pam,ab->pbm", first_real, line_sin, precision=highest) + jnp.einsum(
        "pam,ab->pbm", first_imag, line_cos, precision=highest
    )
    return (second_real, second_imag)


def contract(left, right):
    return lax.dot_general(
        left,
        right,
        (((0,), (0,)), ((), ())),
        precision=lax.Precision.HIGHEST,
        preferred_element_type=jnp.float32,
    )


def row_terms(dens_real, dens_imag, factor, columns):
    left_real = jnp.take(dens_real, columns, axis=1) * factor[:, None]
    left_imag = jnp.take(dens_imag, columns, axis=1) * factor[:, None]
    part_real = contract(left_real, dens_real) + contract(left_imag, dens_imag)
    part_imag = contract(left_real, dens_imag) - contract(left_imag, dens_real)
    return jnp.stack([part_real, part_imag], axis=1)


def local(occ_orb, occ_energy, emp_orb, emp_energy, gidx, sym_map, weights, count):
    k_local = occ_orb.shape[0]
    bands = occ_orb.shape[1]
    emp_local = emp_orb.shape[1]
    points = occ_orb.shape[3]
    plane = GB * GC
    groups = lax.axis_size("ka")
    members = lax.axis_size("band")
    k_total = k_local * groups
    empty_total = emp_local * members
    per_device = NGC // (groups * members)
    next_orb, next_energy = passed_along((emp_orb, emp_energy), "ka", -1)
    orbitals = jnp.concatenate([emp_orb, next_orb], axis=0)
    energies = jnp.concatenate([emp_energy, next_energy], axis=0)
    plane_cos, plane_sin = plane_phase(GB, GC)
    line_cos, line_sin = line_phase(GA)
    wsum = jnp.sum(weights).astype(jnp.float32)
    scale = -4.0 / jnp.sqrt(jnp.float32(bands * empty_total) * wsum)
    first_k = lax.axis_index("ka") * k_local
    band_global = lax.axis_index("band") * emp_local + jnp.arange(emp_local, dtype=jnp.int32)
    real_list = []
    imag_list = []
    factor_list = []
    for slot in range(k_local):
        kpoint = first_k + slot
        raw = kpoint + 1
        wrapped = (raw >= k_total).astype(jnp.int32)
        target = raw - wrapped * k_total
        occ = occ_orb[slot]
        emp = orbitals[slot + 1]
        real_pair = (
            occ[:, None, 0, :] * emp[None, :, 0, :] + occ[:, None, 1, :] * emp[None, :, 1, :]
        )
        imag_pair = (
            occ[:, None, 0, :] * emp[None, :, 1, :] - occ[:, None, 1, :] * emp[None, :, 0, :]
        )
        real_pair = real_pair.reshape(bands * emp_local, GA, plane)
        imag_pair = imag_pair.reshape(bands * emp_local, GA, plane)
        spec_real, spec_imag = transform(
            real_pair, imag_pair, plane_cos, plane_sin, line_cos, line_sin
        )
        norm_root = jnp.sqrt(jnp.float32(points))
        spec_real = spec_real.reshape(bands * emp_local, points) / norm_root
        spec_imag = spec_imag.reshape(bands * emp_local, points) / norm_root
        index = (jnp.take(gidx, sym_map[slot]) + wrapped * plane) % points
        real_list.append(jnp.take(spec_real, index, axis=1))
        imag_list.append(jnp.take(spec_imag, index, axis=1))
        live = (band_global < count[target]).astype(jnp.float32)
        gap = energies[slot + 1][None, :] - occ_energy[slot][:, None]
        factor = scale * weights[kpoint].astype(jnp.float32) * live[None, :] / gap
        factor_list.append(factor.reshape(bands * emp_local))
    dens_real = jnp.concatenate(real_list, axis=0)
    dens_imag = jnp.concatenate(imag_list, axis=0)
    factor_all = jnp.concatenate(factor_list, axis=0)
    columns = jnp.arange(per_device * lax.axis_size(("ka", "band")), dtype=jnp.int32)
    owned = lax.psum_scatter(
        row_terms(dens_real, dens_imag, factor_all, columns),
        ("ka", "band"),
        scatter_dimension=0,
        tiled=True,
    )
    outputs = [owned]
    return jnp.stack(outputs, axis=0)


def solution(mesh):
    return jax.shard_map(
        local,
        mesh=mesh,
        in_specs=(
            P("ka", None, None, None),
            P("ka", None),
            P("ka", "band", None, None),
            P("ka", "band"),
            P(),
            P("ka", None),
            P(),
            P(),
        ),
        out_specs=P(None, ("ka", "band"), None, None),
        check_vma=False,
    )
```

profile of v0, /device:TPU:0, one launch (start us, length us, event | category | flops | bytes accessed | tf_op | source)
XLA Modules:
  0.0 928.0 jit_solution(10359630770667446925)
XLA Ops:
  6.5 2.5 collective-permute-start.1
  9.1 0.7 collective-permute-start
  9.8 0.7 slice_bitcast_fusion.7
  10.5 0.8 slice_bitcast_fusion.3
  11.4 2.5 slice_bitcast_fusion.1
  13.9 4.0 fusion.188
  17.9 0.6 copy.114
  18.6 0.6 copy.113
  19.2 3.8 multiply_add_fusion.1
  23.0 3.3 sub.97
  26.4 5.4 fusion.24
  31.8 5.3 fusion.26
  37.1 3.6 add.208
  40.7 5.7 fusion.43
  46.4 4.2 fusion.16
  50.6 4.2 fusion.18
  54.8 0.6 reduce_sum.9
  56.1 0.7 fusion.194
  58.2 11.8 %gather_fusion.2 = s32[2048]{0:T(1024)S(1)} fusion(s32[2048]{0:T(1024)S(1)} %copy-done, s32[2048]{0:T(1024)S(1)} %fusion.107), kind=kCustom, calls=%fused_computation.3.clone | custom fusion | bytes 24576 | tf_op jit(solution)/shard_map/jit(_take)/gather | solution.py:115
  70.0 12.0 %gather_fusion = s32[2048]{0:T(1024)S(1)} fusion(s32[2048]{0:T(1024)S(1)} %copy-done, s32[2048]{0:T(1024)S(1)} %fusion.106), kind=kCustom, calls=%fused_computation.clone | custom fusion | bytes 24576 | tf_op jit(solution)/shard_map/jit(_take)/gather | solution.py:115
  82.0 0.6 fusion.193
  82.6 0.6 compare_select_fusion.5
  83.4 0.1 div.109
  83.5 3.1 copy.111
  86.6 1.6 copy.112
  88.2 4.1 fusion.40
  92.3 4.3 multiply_bitcast_fusion.3
  96.6 3.0 multiply_bitcast_fusion.1
  99.6 2.3 copy.45
  101.9 2.0 copy.43
  103.9 9.1 gather_fusion.5
  113.0 7.5 gather_fusion.1
  120.6 0.6 compare_select_fusion.4
  121.2 3.0 select_bitcast_fusion.1
  124.6 3.8 multiply_add_fusion
  128.4 3.1 sub.101
  131.5 5.3 fusion.8
  136.8 5.4 fusion.10
  142.2 3.2 add.218
  145.4 5.7 fusion.49
  151.1 2.9 fusion
  154.0 2.9 fusion.2
  156.9 4.3 fusion.46
  161.2 4.3 multiply_bitcast_fusion.2
  165.5 3.0 multiply_bitcast_fusion
  168.5 1.9 copy.46
  170.4 2.0 copy.44
  172.4 9.1 gather_fusion.6
  181.5 7.5 gather_fusion.3
  189.1 1.9 select_bitcast_fusion
  191.0 0.1 pad_maximum_fusion.2
  191.1 0.8 copy-done.5
  191.9 0.4 copy-done.7
  192.3 0.6 copy-done.3
  193.0 1.5 pad_maximum_fusion.1
  194.5 6.2 gather_fusion.4
  200.7 11.3 %fusion.52 = f32[1024,2048]{1,0:T(8,128)} fusion(f32[1024,256]{1,0:T(8,128)} %gather_fusion.4, f32[256]{0:T(256)S(1)} %pad_maximum_fusion.3, pred[1024]{0:T(1024)(128)(4,1)S(1)} %iota_compare_fusion, f32[128,2048]{0,1:T(8,128)} %copy-done.5, f32[128,2048]{0,1:T(8,128)S(1)} %get-tuple-element.28), kind=kOutput, calls=%fused_computation.69 | convolution fusion | flops 6443499520 | bytes 11536384 | tf_op jit(solution)/shard_map/dot_general | solution.py:54
  212.0 9.0 fusion.53
  221.0 4.7 gather_fusion.7
  225.7 10.4 %subtract_bitcast_fusion = f32[1024,1,2048]{2,0,1:T(8,128)S(1)} fusion(f32[1024,2048]{1,0:T(8,128)} %fusion.52, f32[1024,256]{1,0:T(8,128)} %gather_fusion.7, f32[256]{0:T(256)S(1)} %pad_maximum_fusion.3, pred[1024]{0:T(1024)(128)(4,1)S(1)} %iota_compare_fusion, f32[128,2048]{0,1:T(8,128)} %copy-done.7, f32[128,2048]{0,1:T(8,128)} %get-tuple-element.29), kind=kOutput, calls=%fused_computation.9 | convolution fusion | flops 6445596672 | bytes 19924992 | tf_op jit(solution)/shard_map/dot_general | solution.py:54
  236.1 6.8 add_bitcast_fusion
  242.9 6.0 pad_maximum_fusion
  249.0 670.3 %reduce-scatter.2.cloned.1.call-done = f32[8,2,2048]{2,0,1:T(8,128)} async-done(((f32[1024,2,2048]{2,0,1:T(8,128)}), f32[8,2,2048]{2,0,1:T(8,128)}) %reduce-scatter.2.cloned.1.call-update) | async-done | bytes 131088 | tf_op jit(solution)/shard_map/reduce_scatter | solution.py:126
  919.3 1.7 copy.42
  (64 shorter events, 0.7 us)
Async XLA Ops:
  6.5 51.6 %copy-start = (s32[2048]{0:T(1024)S(1)}, s32[2048]{0:T(1024)}, u32[]{:S(2)}) copy-start(s32[2048]{0:T(1024)} %param.18) | copy-start | bytes 24580
  6.5 912.7 %reduce-scatter.2.cloned.1.call-start = ((), (), s32[]{:S(2)}) async-start(), calls=%async_computation.1 | async-start | bytes 16908288 | tf_op jit(solution)/shard_map/reduce_scatter | solution.py:126
  6.5 117.7 %collective-permute-start.1 = (f32[2,2]{1,0:T(2,128)}, f32[2,2]{1,0:T(2,128)S(1)}, u32[]{:S(2)}, u32[]{:S(2)}) collective-permute-start(f32[2,2]{1,0:T(2,128)} %param.17), channel_id=1, source_target_pairs={{0,96},{32,0},{64,32},{96,64},{1,97},{33,1},{65,33},{97,65},{2,98}... | collective-permute-start | bytes 56 | tf_op jit(solution)/shard_map/ppermute | solution.py:16
  9.1 115.4 %collective-permute-start = (f32[2,2,2,4096]{3,2,1,0:T(2,128)}, f32[2,2,2,4096]{3,2,1,0:T(2,128)S(1)}, u32[]{:S(2)}, u32[]{:S(2)}) collective-permute-start(f32[2,2,2,4096]{3,2,1,0:T(2,128)} %param.16), channel_id=1, source_target_pairs={{0,96},{32,0},{64,32},{96,64},{1,97},{33,1},{65,33},{97,65},{2,98}... | collective-permute-start | bytes 393224 | tf_op jit(solution)/shard_map/ppermute | solution.py:16
  50.6 4.3 copy-start.18
  50.6 7.5 copy-start.20
  50.6 7.5 copy-start.17
  70.0 12.0 %copy-start.19 = (s32[8]{0:T(128)S(1)}, s32[8]{0:T(128)}, u32[]{:S(2)}) copy-start(s32[8]{0:T(128)} %param.21) | copy-start | bytes 100
  83.5 4.6 copy-start.13
  88.2 4.1 copy-start.12
  92.3 4.4 copy-start.11
  121.2 3.4 copy-start.15
  121.2 3.4 copy-start.16
  154.0 2.9 copy-start.14
  191.0 1.0 copy-start.5
  191.0 1.3 copy-start.7
  191.0 2.0 copy-start.3
  200.7 11.3 %copy-start.4 = (f32[128,2048]{0,1:T(8,128)S(1)}, f32[128,2048]{0,1:T(8,128)}, u32[]{:S(2)}) copy-start(f32[128,2048]{0,1:T(8,128)} %get-tuple-element.29) | copy-start | bytes 3145732
  200.7 11.3 %copy-start.8 = (f32[128,2048]{0,1:T(8,128)S(1)}, f32[128,2048]{0,1:T(8,128)}, u32[]{:S(2)}) copy-start(f32[128,2048]{0,1:T(8,128)} %copy-done.7) | copy-start | bytes 3145732
  200.7 11.3 %copy-start.9 = (f32[1024,256]{1,0:T(8,128)S(1)}, f32[1024,256]{1,0:T(8,128)}, u32[]{:S(2)}) copy-start(f32[1024,256]{1,0:T(8,128)} %gather_fusion.4) | copy-start | bytes 3145732
  225.7 10.4 %copy-start.2 = (f32[1024,2048]{1,0:T(8,128)S(1)}, f32[1024,2048]{1,0:T(8,128)}, u32[]{:S(2)}) copy-start(f32[1024,2048]{1,0:T(8,128)} %fusion.53) | copy-start | bytes 25165828
  225.7 10.4 %copy-start.6 = (f32[128,2048]{0,1:T(8,128)S(1)}, f32[128,2048]{0,1:T(8,128)}, u32[]{:S(2)}) copy-start(f32[128,2048]{0,1:T(8,128)} %copy-done.5) | copy-start | bytes 3145732
  225.7 10.4 %copy-start.10 = (f32[1024,256]{1,0:T(8,128)S(1)}, f32[1024,256]{1,0:T(8,128)}, u32[]{:S(2)}) copy-start(f32[1024,256]{1,0:T(8,128)} %gather_fusion.7) | copy-start | bytes 3145732
  249.0 672.0 %copy-start.1 = (s32[2048]{0:T(1024)S(1)}, s32[2048]{0:T(1024)}, u32[]{:S(2)}) copy-start(s32[2048]{0:T(1024)} %param.18) | copy-start | bytes 24580
Sparse Core Ops, SparseCore 0:
  249.1 670.1 reduce-scatter.1
where the time goes:
time: 933 us; the launch traced here: 928 us
  waiting for transfers between devices  670 us (72%)
  local copies, waits for them, and re-layouts  109 us (12%)
  matrix products  107 us (11%)
  other arithmetic  22.3 us (2%)
  between operations  16.1 us (2%)
    reduce_scatter x1, waiting for transfers between devices, local(): lax.psum_scatter(row_terms(dens_real, dens_imag, factor_all, columns), ('...  670 us
    dot_general x4, matrix products, contract(): lax.dot_general(left, right, (((0,), (0,)), ((), ())), precision=lax.Prec...  37.5 us
    gather x2, local copies, waits for them, and re-layouts, local(): index = (jnp.take(gidx, sym_map[slot]) + wrapped * plane) % points  23.7 us
  transfers between devices with their start and end apart: 3, of which 1 were waited for; matrix products, arithmetic and copies ran while one was open for 12% of the time, Pallas kernels for 0%

commit v1 on v0

v1 whole, which is shorter than its diff:
```python
import functools

import jax
import jax.numpy as jnp
import numpy as np
from jax import lax
from jax.experimental import pallas as pl
from jax.experimental.pallas import tpu as pltpu
from jax.sharding import PartitionSpec as P

GRID = 16
PLANE = GRID * GRID
POINTS = GRID * PLANE
HALF = PLANE // 2
NG = 2048
VB = 64
KA = 4
BAND = 32
YS = 4
MEMBERS = BAND // YS
CHUNK = 2 * VB
KLOC = 2
DEPTH = KLOC * YS * 2 * CHUNK
ROWS = 256
LINES = POINTS // 128


def plane_matrices():
    point = np.arange(HALF)
    outer, inner = point // GRID, point % GRID
    parts = []
    for parity in range(2):
        turns = np.outer(2 * outer + parity, outer) + np.outer(inner, inner)
        angle = 2.0 * np.pi * (turns % GRID) / GRID
        cos, sin = np.cos(angle), np.sin(angle)
        parts.append(np.block([[cos, sin], [-sin, cos]]))
    whole = np.stack(parts).astype(np.float32)
    high = whole.astype(jnp.bfloat16)
    low = (whole - high.astype(np.float32)).astype(jnp.bfloat16)
    return high, low


def split(value):
    high = value.astype(jnp.bfloat16)
    low = (value - high.astype(jnp.float32)).astype(jnp.bfloat16)
    return high, low


def four(points):
    (ar, ai), (br, bi), (cr, ci), (dr, di) = points
    sr, si = ar + cr, ai + ci
    tr, ti = ar - cr, ai - ci
    ur, ui = br + dr, bi + di
    wr, wi = br - dr, bi - di
    return [(sr + ur, si + ui), (tr + wi, ti - wr), (sr - ur, si - ui), (tr - wi, ti + wr)]


def turned(point, power):
    re, im = point
    power %= GRID
    if power == 0:
        return re, im
    if power == 4:
        return im, -re
    if power == 2:
        root = float(np.sqrt(0.5))
        return (re + im) * root, (im - re) * root
    if power == 6:
        root = float(np.sqrt(0.5))
        return (im - re) * root, (re + im) * -root
    cos = float(np.cos(2 * np.pi * power / GRID))
    sin = float(np.sin(2 * np.pi * power / GRID))
    return re * cos + im * sin, im * cos - re * sin


def dot_t(left, right):
    return lax.dot_general(left, right, (((1,), (1,)), ((), ())), preferred_element_type=jnp.float32)


def kernel(
    place_ref, sym_ref, rows_ref, occ_ref, emp_ref, fac_ref, whi_ref, wlo_ref, near_ref, far_ref,
    mid_ref, xhi_ref, xlo_ref, spec_ref, dens_ref, bhi_ref, blo_ref, ahi_ref, alo_ref,
):
    def one_k(k, carry):
        def one_chunk(chunk, carry):
            def one_block(block, carry):
                band = block // (VB // 16)
                start = pl.multiple_of((block % (VB // 16)) * 16, 16)
                line = k * (2 * YS) + chunk * 2 + band

                def pair(a, half):
                    base = a * PLANE + half * HALF
                    o_re = occ_ref[k, 0, pl.ds(start, 16), pl.ds(base, HALF)]
                    o_im = occ_ref[k, 1, pl.ds(start, 16), pl.ds(base, HALF)]
                    at = a * 2 + half
                    e_re = emp_ref[line, at : at + 1, :]
                    e_im = emp_ref[line, LINES + at : LINES + at + 1, :]
                    return o_re * e_re + o_im * e_im, o_re * e_im - o_im * e_re

                for a0 in range(4):
                    even, odd = [], []
                    for a1 in range(4):
                        fr, fi = pair(4 * a1 + a0, 0)
                        sr, si = pair(4 * a1 + a0, 1)
                        even.append((fr + sr, fi + si))
                        odd.append((fr - sr, fi - si))
                    for parity, points in enumerate((even, odd)):
                        for k0, point in enumerate(four(points)):
                            re, im = turned(point, a0 * k0)
                            mid_ref[parity, k0, a0, 0] = re
                            mid_ref[parity, k0, a0, 1] = im
                row = pl.multiple_of(block * 16, 16)
                for parity in range(2):
                    for k0 in range(4):
                        points = [(mid_ref[parity, k0, a0, 0], mid_ref[parity, k0, a0, 1]) for a0 in range(4)]
                        for k1, point in enumerate(four(points)):
                            at = k0 + 4 * k1
                            for part in range(2):
                                high, low = split(point[part])
                                xhi_ref[parity, pl.ds(at * CHUNK + row, 16), pl.ds(part * HALF, HALF)] = high
                                xlo_ref[parity, pl.ds(at * CHUNK + row, 16), pl.ds(part * HALF, HALF)] = low
                return carry

            lax.fori_loop(0, CHUNK // 16, one_block, 0)

            def one_tile(tile, carry):
                for parity in range(2):
                    at = pl.ds(pl.multiple_of(tile * 2 * CHUNK, 2 * CHUNK), 2 * CHUNK)
                    xhi = xhi_ref[parity, at, :]
                    xlo = xlo_ref[parity, at, :]
                    whi = whi_ref[parity]
                    out = dot_t(whi, xhi) + dot_t(whi, xlo) + dot_t(wlo_ref[parity], xhi)
                    for which in range(2):
                        base = ((tile * 2 + which) * PLANE + parity * HALF) * 8 + chunk * 2
                        for part in range(2):
                            spec_ref[pl.ds(base + part, HALF, stride=8), :] = out[
                                part * HALF : (part + 1) * HALF, which * CHUNK : (which + 1) * CHUNK
                            ]
                return carry

            lax.fori_loop(0, GRID // 2, one_tile, 0)
            return carry

        lax.fori_loop(0, YS, one_chunk, 0)

        shift = rows_ref[ROWS // 8 + k]

        def gathered(count, row_of):
            def sixteen(step, carry):
                for lane in range(16):
                    at = step * 16 + lane
                    source = (place_ref[sym_ref[k, row_of(at)]] + shift) & (POINTS * 8 - 1)
                    source = pl.multiple_of(source, 8)
                    dens_ref[pl.ds(pl.multiple_of(at * 8, 8), 8), :] = spec_ref[pl.ds(source, 8), :]
                return carry

            lax.fori_loop(0, count // 16, sixteen, 0)

        def columns(slot):
            return pl.ds(pl.multiple_of(k * (8 * CHUNK) + slot * CHUNK, CHUNK), CHUNK)

        gathered(ROWS, lambda at: rows_ref[at // 8] + at % 8)

        def left(step, carry):
            row = pl.multiple_of(step * 16, 16)
            for chunk in range(YS):
                factor = fac_ref[pl.ds(k * YS + chunk, 1), :]
                re = dens_ref[pl.ds(row * 8 + 2 * chunk, 16, stride=8), :] * factor
                im = dens_ref[pl.ds(row * 8 + 2 * chunk + 1, 16, stride=8), :] * factor
                rhi, rlo = split(re)
                ihi, ilo = split(im)
                ahi_ref[pl.ds(row, 16), columns(2 * chunk)] = rhi
                alo_ref[pl.ds(row, 16), columns(2 * chunk)] = rlo
                ahi_ref[pl.ds(row, 16), columns(2 * chunk + 1)] = ihi
                alo_ref[pl.ds(row, 16), columns(2 * chunk + 1)] = ilo
                ahi_ref[pl.ds(ROWS + row, 16), columns(2 * chunk)] = -ihi
                alo_ref[pl.ds(ROWS + row, 16), columns(2 * chunk)] = -ilo
                ahi_ref[pl.ds(ROWS + row, 16), columns(2 * chunk + 1)] = rhi
                alo_ref[pl.ds(ROWS + row, 16), columns(2 * chunk + 1)] = rlo
            return carry

        lax.fori_loop(0, ROWS // 16, left, 0)
        gathered(NG, lambda at: at)

        def right(step, carry):
            row = pl.multiple_of(step * 16, 16)
            for slot in range(8):
                high, low = split(dens_ref[pl.ds(row * 8 + slot, 16, stride=8), :])
                bhi_ref[pl.ds(row, 16), columns(slot)] = high
                blo_ref[pl.ds(row, 16), columns(slot)] = low
            return carry

        lax.fori_loop(0, NG // 16, right, 0)
        return carry

    lax.fori_loop(0, KLOC, one_k, 0)

    def one_column(tile, carry):
        at = pl.ds(pl.multiple_of(tile * 256, 256), 256)
        bhi = bhi_ref[at, :]
        blo = blo_ref[at, :]
        ahi = ahi_ref[...]
        out = dot_t(ahi, bhi) + dot_t(ahi, blo) + dot_t(alo_ref[...], bhi)
        for part in range(2):
            near_ref[part, :, at] = out[part * ROWS : part * ROWS + ROWS // 2]
            far_ref[part, :, at] = out[part * ROWS + ROWS // 2 : (part + 1) * ROWS]
        return carry

    lax.fori_loop(0, NG // 256, one_column, 0)


def partial_rows(places, sym_map, rows, occ, emp, factor):
    whi, wlo = plane_matrices()
    vmem = pl.BlockSpec(memory_space=pltpu.VMEM)
    smem = pl.BlockSpec(memory_space=pltpu.SMEM)
    part = jax.ShapeDtypeStruct((2, ROWS // 2, NG), jnp.float32)
    return pl.pallas_call(
        kernel,
        out_shape=(part, part),
        in_specs=[smem, smem, smem, vmem, vmem, vmem, vmem, vmem],
        out_specs=(vmem, vmem),
        scratch_shapes=[
            pltpu.VMEM((2, 4, 4, 2, 16, HALF), jnp.float32),
            pltpu.VMEM((2, GRID * CHUNK, PLANE), jnp.bfloat16),
            pltpu.VMEM((2, GRID * CHUNK, PLANE), jnp.bfloat16),
            pltpu.VMEM((POINTS * 8, CHUNK), jnp.float32),
            pltpu.VMEM((NG * 8, CHUNK), jnp.float32),
            pltpu.VMEM((NG, DEPTH), jnp.bfloat16),
            pltpu.VMEM((NG, DEPTH), jnp.bfloat16),
            pltpu.VMEM((2 * ROWS, DEPTH), jnp.bfloat16),
            pltpu.VMEM((2 * ROWS, DEPTH), jnp.bfloat16),
        ],
        compiler_params=pltpu.CompilerParams(vmem_limit_bytes=62 * 2**20),
        cost_estimate=pl.CostEstimate(flops=40 * 10**9, bytes_accessed=10 * 2**20, transcendentals=0),
    )(places, sym_map, rows, occ, emp, factor, jnp.asarray(whi), jnp.asarray(wlo))


def place(index):
    ka, band = divmod(index, BAND)
    return (ka // 2) * 2 + (band // 4) % 2, ka % 2, band // MEMBERS, band % 4


def index_of(x, core, y, z):
    x, core, y, z = x % 4, core % 2, y % 4, z % 4
    return ((x // 2) * 2 + core) * BAND + y * MEMBERS + (x % 2) * 4 + z


def shifted(value, x=0, core=0, y=0, z=0):
    pairs = []
    for index in range(KA * BAND):
        px, pc, py, pz = place(index)
        pairs.append((index, index_of(px + x, pc + core, py + y, pz + z)))
    return lax.ppermute(value, ("ka", "band"), pairs)


def from_next(value, y):
    pairs = []
    for index in range(KA * BAND):
        ka, band = divmod(index, BAND)
        source = ((ka + 1) % KA) * BAND + (band + y * MEMBERS) % BAND
        pairs.append((source, index))
    return lax.ppermute(value, ("ka", "band"), pairs)


def local(occ_orb, occ_energy, emp_orb, emp_energy, gidx, sym_map, weights, count):
    ka = lax.axis_index("ka")
    band = lax.axis_index("band")
    core = ka % 2
    y = band // MEMBERS
    member = band % MEMBERS
    x = (ka // 2) * 2 + member // 4
    z = member % 4

    energy = jnp.broadcast_to(emp_energy[:, :, None, None], (KLOC, 2, 8, 128))
    lines = jnp.concatenate([emp_orb.reshape(KLOC, 2, 2 * LINES, 128), energy], axis=2)
    here = [lines[1]] + [shifted(lines[1], y=-step) for step in range(1, YS)]
    after = [from_next(lines[0], step) for step in range(YS)]
    emp = jnp.concatenate(here + after, axis=0)
    occ = jnp.transpose(occ_orb, (0, 2, 1, 3))

    kpoint = ka * KLOC + jnp.arange(KLOC, dtype=jnp.int32)
    wrapped = (kpoint + 1 >= KA * KLOC).astype(jnp.int32)
    target = kpoint + 1 - wrapped * (KA * KLOC)
    odd = (gidx // GRID) % 2
    outer = (gidx // (2 * GRID)) % 8
    places = (gidx // PLANE * PLANE + odd * HALF + outer * GRID + gidx % GRID) * 8

    wsum = jnp.sum(weights).astype(jnp.float32)
    scale = -4.0 / jnp.sqrt(jnp.float32(VB * 2 * BAND) * wsum) / POINTS
    owner = (y + jnp.arange(YS, dtype=jnp.int32)) % YS
    bands = owner[:, None] * (2 * MEMBERS) + member * 2 + jnp.arange(2, dtype=jnp.int32)[None, :]
    live = (bands[None] < count[target][:, None, None]).astype(jnp.float32)
    gap = emp[:, 2 * LINES, 0].reshape(KLOC, YS, 2)[..., None] - occ_energy[:, None, None, :]
    strength = (scale * weights[kpoint].astype(jnp.float32))[:, None, None, None]
    factor = (strength * live[..., None] / gap).reshape(KLOC * YS, CHUNK)

    near_core = jnp.arange(2, dtype=jnp.int32)[:, None, None]
    to_x = (x + jnp.arange(4, dtype=jnp.int32)[None, :, None]) % 4
    to_z = (z + jnp.arange(4, dtype=jnp.int32)[None, None, :]) % 4
    to_ka = (to_x // 2) * 2 + (core + near_core) % 2
    rows = (to_ka * 256 + y * 64 + (to_x % 2) * 32 + to_z * 8).reshape(32)
    rows = jnp.concatenate([rows, wrapped * (PLANE * 8)])

    near, far = partial_rows(places, sym_map, rows.astype(jnp.int32), occ, emp, factor)

    both = near + shifted(far, core=1)
    both = both.reshape(2, 4, 4, 8, NG)
    first = both[..., : NG // 2]
    second = both[..., NG // 2 :]
    first_parts = [shifted(first[:, :, step], z=step) for step in range(1, 4)]
    second_parts = [shifted(second[:, step], x=step) for step in range(1, 4)]
    first = first[:, :, 0] + (first_parts[0] + first_parts[1]) + first_parts[2]
    second = second[:, 0] + (second_parts[0] + second_parts[1]) + second_parts[2]
    first_parts = [shifted(first[:, step], x=step) for step in range(1, 4)]
    second_parts = [shifted(second[:, step], z=step) for step in range(1, 4)]
    first = first[:, 0] + (first_parts[0] + first_parts[1]) + first_parts[2]
    second = second[:, 0] + (second_parts[0] + second_parts[1]) + second_parts[2]
    owned = jnp.concatenate([first, second], axis=2)
    return jnp.transpose(owned, (1, 0, 2))[None]


def solution(mesh):
    return jax.shard_map(
        local,
        mesh=mesh,
        in_specs=(
            P("ka", None, None, None),
            P("ka", None),
            P("ka", "band", None, None),
            P("ka", "band"),
            P(),
            P("ka", None),
            P(),
            P(),
        ),
        out_specs=P(None, ("ka", "band"), None, None),
        check_vma=False,
    )
```

time: 933 us -> 171 us (0.18)
  waiting for transfers between devices: 670 us -> 18.8 us
  matrix products: 107 us -> 0 us
  Pallas kernels: 0 us -> 98 us
  local copies, waits for them, and re-layouts: 109 us -> 12.8 us
  starting transfers between devices: 3.22 us -> 33 us
  between operations: 16.1 us -> 1.03 us
  other arithmetic: 22.3 us -> 7.27 us
    reduce_scatter x1 -> x0, waiting for transfers between devices: 670 us -> none  [local(): lax.psum_scatter(row_terms(dens_real, dens_imag, factor_all, columns), ('...]
    dot_general x20 -> x0, matrix products: 107 us -> none  [the longest x4 37.5 us: contract(): lax.dot_general(left, right, (((0,), (0,)), ((), ())), precision=lax.Prec...]
    pallas_call x0 -> x1, Pallas kernels: none -> 98 us  [partial_rows(): pl.pallas_call(kernel, out_shape=(part, part), in_specs=[smem, smem, smem...]
    gather x8 -> x2, local copies, waits for them, and re-layouts: 68 us -> 1.93 us  [the longest x1 1.29 us: local(): weights[kpoint].astype(jnp.float32)]
    ppermute x2 -> x20, starting transfers between devices: 3.22 us -> 33 us  [the longest x16 27.4 us: shifted(): return lax.ppermute(value, ('ka', 'band'), pairs)]
    ppermute x2 -> x20, waiting for transfers between devices: 0.01 us -> 18.8 us  [the longest x16 16.3 us: shifted(): return lax.ppermute(value, ('ka', 'band'), pairs)]
  transfers between devices with their start and end apart: 3 -> 20, of which waited for: 1 -> 9; matrix products, arithmetic and copies ran while one was open for 12% -> 8% of each run, Pallas kernels for 0% -> 0%
where the time goes in v1:
time: 171 us
  Pallas kernels  98 us (57%)
  starting transfers between devices  33 us (19%)
  waiting for transfers between devices  18.8 us (11%)
  local copies, waits for them, and re-layouts  12.8 us (7%)
  other arithmetic  7.27 us (4%)
    pallas_call x1, Pallas kernels, partial_rows(): pl.pallas_call(kernel, out_shape=(part, part), in_specs=[smem, smem, smem...  98 us
    ppermute x16, starting transfers between devices, shifted(): return lax.ppermute(value, ('ka', 'band'), pairs)  27.4 us
    ppermute x16, waiting for transfers between devices, shifted(): return lax.ppermute(value, ('ka', 'band'), pairs)  16.3 us
    unnamed x19, local copies, waits for them, and re-layouts  7.87 us
    ppermute x4, starting transfers between devices, from_next(): return lax.ppermute(value, ('ka', 'band'), pairs)  5.61 us
  transfers between devices with their start and end apart: 20, of which 9 were waited for; matrix products, arithmetic and copies ran while one was open for 8% of the time, Pallas kernels for 0%

profile of v1, /device:TPU:0, one launch (start us, length us, event | category | flops | bytes accessed | tf_op | source)
XLA Modules:
  0.0 170.9 jit_solution(2531371160328275935)
XLA Ops:
  0.0 1.0 reshape.280
  1.0 0.8 broadcast_in_dim.4
  1.8 1.7 %collective-permute-start.2 = (f32[2,72,128]{2,1,0:T(8,128)S(1)}, f32[2,72,128]{2,1,0:T(8,128)S(1)}, u32[]{:S(2)}, u32[]{:S(2)}) collective-permute-start(f32[2,72,128]{2,1,0:T(8,128)S(1)} %get-tuple-element.24), channel_id=1, source_target_pairs={{0,8},{1,9},{2,10},{3,11},{4,12},{5,13},{6,14},{7,15},{8,16},{9,17... | collective-permute-start | bytes 221192 | tf_op jit(solution)/shard_map/ppermute | solution.py:253
  3.5 2.9 %collective-permute-start.1 = (f32[2,72,128]{2,1,0:T(8,128)S(1)}, f32[2,72,128]{2,1,0:T(8,128)S(1)}, u32[]{:S(2)}, u32[]{:S(2)}) collective-permute-start(f32[2,72,128]{2,1,0:T(8,128)S(1)} %get-tuple-element.24), channel_id=1, source_target_pairs={{0,16},{1,17},{2,18},{3,19},{4,20},{5,21},{6,22},{7,23},{8,24},{9,... | collective-permute-start | bytes 221192 | tf_op jit(solution)/shard_map/ppermute | solution.py:253
  6.4 1.3 collective-permute-start
  7.8 1.7 %collective-permute-start.6 = (f32[2,72,128]{2,1,0:T(8,128)S(1)}, f32[2,72,128]{2,1,0:T(8,128)S(1)}, u32[]{:S(2)}, u32[]{:S(2)}) collective-permute-start(f32[2,72,128]{2,1,0:T(8,128)S(1)} %get-tuple-element.23), channel_id=1, source_target_pairs={{56,0},{57,1},{58,2},{59,3},{60,4},{61,5},{62,6},{63,7},{32,8},{33... | collective-permute-start | bytes 221192 | tf_op jit(solution)/shard_map/ppermute | solution.py:262
  9.5 1.9 %collective-permute-start.5 = (f32[2,72,128]{2,1,0:T(8,128)S(1)}, f32[2,72,128]{2,1,0:T(8,128)S(1)}, u32[]{:S(2)}, u32[]{:S(2)}) collective-permute-start(f32[2,72,128]{2,1,0:T(8,128)S(1)} %get-tuple-element.23), channel_id=1, source_target_pairs={{48,0},{49,1},{50,2},{51,3},{52,4},{53,5},{54,6},{55,7},{56,8},{57... | collective-permute-start | bytes 221192 | tf_op jit(solution)/shard_map/ppermute | solution.py:262
  11.5 1.3 reduce_sum.9
  13.6 0.1 iota_add_fusion
  13.7 0.1 add_add_fusion
  13.7 0.1 broadcast_add_fusion
  13.8 0.1 add.359
  13.9 1.3 gather_fusion.1
  15.2 1.3 fusion.16.place_ref
  16.6 6.6 %copy.54 = f32[2,64,2,4096]{3,1,2,0:T(8,128)} copy(f32[2,64,2,4096]{3,2,1,0:T(2,128)} %param.10) | data formatting | bytes 8388608 | tf_op args[0]
  23.1 0.6 gather_fusion
  23.8 0.1 compare_select_fusion
  23.9 0.6 pad_add_fusion.rows_ref
  24.5 0.0 collective-permute-done
  24.5 1.9 %collective-permute-start.4 = (f32[2,72,128]{2,1,0:T(8,128)S(1)}, f32[2,72,128]{2,1,0:T(8,128)S(1)}, u32[]{:S(2)}, u32[]{:S(2)}) collective-permute-start(f32[2,72,128]{2,1,0:T(8,128)S(1)} %get-tuple-element.23), channel_id=1, source_target_pairs={{40,0},{41,1},{42,2},{43,3},{44,4},{45,5},{46,6},{47,7},{48,8},{49... | collective-permute-start | bytes 221192 | tf_op jit(solution)/shard_map/ppermute | solution.py:262
  26.4 0.0 collective-permute-done.1
  26.4 0.1 collective-permute-start.3
  26.5 2.5 %collective-permute-done.3 = f32[2,72,128]{2,1,0:T(8,128)S(1)} collective-permute-done((f32[2,72,128]{2,1,0:T(8,128)S(1)}, f32[2,72,128]{2,1,0:T(8,128)S(1)}, u32[]{:S(2)}, u32[]{:S(2)}) %collective-permute-start.3) | collective-permute-done | bytes 73760 | tf_op jit(solution)/shard_map/ppermute | solution.py:262
  29.2 0.2 slice_reduce_fusion
  29.4 0.1 sub.63
  29.4 0.1 subtract_divide_fusion
  29.5 0.7 div.107.fac_ref
  30.2 98.0 %shard_map.100 = (f32[2,128,2048]{2,1,0:T(8,128)}, f32[2,128,2048]{2,1,0:T(8,128)}) custom-call(s32[2048]{0:T(1024)} %fusion.16.place_ref, s32[2,2048]{1,0:T(2,128)} %sym_ref.1, s32[34]{0:T(128)} %pad_add_fusion.rows_ref, f32[2,2,64,4096]{3,2,1,0:T(8,128)} %bitcast.74, f32[16,72,128]{2,1,0:T(8,128)} %copy-done.1, f32[8,128]{1,0:T(8,128)} %div.107.fac_ref, ...), custom_call_target="tpu_custom_call" | custom-call | flops 40000000000 | bytes 10485760 | tf_op jit(solution)/shard_map/pallas_call | solution.py:217
  128.2 2.4 %collective-permute-start.7 = (f32[2,128,2048]{2,1,0:T(8,128)}, f32[2,128,2048]{2,1,0:T(8,128)S(1)}, u32[]{:S(2)}, u32[]{:S(2)}) collective-permute-start(f32[2,128,2048]{2,1,0:T(8,128)} %get-tuple-element.8), channel_id=1, source_target_pairs={{0,32},{1,33},{2,34},{3,35},{4,36},{5,37},{6,38},{7,39},{8,40},{9,... | collective-permute-start | bytes 6291464 | tf_op jit(solution)/shard_map/ppermute | solution.py:253
  130.6 4.0 %collective-permute-done.7 = f32[2,128,2048]{2,1,0:T(8,128)S(1)} collective-permute-done((f32[2,128,2048]{2,1,0:T(8,128)}, f32[2,128,2048]{2,1,0:T(8,128)S(1)}, u32[]{:S(2)}, u32[]{:S(2)}) %collective-permute-start.7) | collective-permute-done | bytes 2097184 | tf_op jit(solution)/shard_map/ppermute | solution.py:253
  134.6 1.9 %add.376 = f32[2,128,2048]{2,1,0:T(8,128)S(1)} add(f32[2,128,2048]{2,1,0:T(8,128)} %get-tuple-element.7, f32[2,128,2048]{2,1,0:T(8,128)S(1)} %collective-permute-done.7) | non-fusion elementwise | flops 524288 | bytes 6291456 | tf_op jit(solution)/shard_map/add | solution.py:306
  136.6 0.1 fusion.37
  136.6 0.2 copy.59
  136.8 0.2 copy.58
  137.1 0.2 copy.60
  137.3 2.0 %collective-permute-start.8 = (f32[2,4,8,1024]{3,0,2,1:T(2,128)S(1)}, f32[2,4,8,1024]{3,0,2,1:T(2,128)S(1)}, u32[]{:S(2)}, u32[]{:S(2)}) collective-permute-start(f32[2,4,8,1024]{3,0,2,1:T(2,128)S(1)} %bitcast.80), channel_id=1, source_target_pairs={{0,1},{1,2},{2,3},{3,0},{4,5},{5,6},{6,7},{7,4},{8,9},{9,10},{10,1... | collective-permute-start | bytes 786440 | tf_op jit(solution)/shard_map/ppermute | solution.py:253
  139.2 2.2 %collective-permute-start.10 = (f32[2,4,8,1024]{3,0,2,1:T(2,128)S(1)}, f32[2,4,8,1024]{3,0,2,1:T(2,128)S(1)}, u32[]{:S(2)}, u32[]{:S(2)}) collective-permute-start(f32[2,4,8,1024]{3,0,2,1:T(2,128)S(1)} %bitcast.78), channel_id=1, source_target_pairs={{0,3},{1,0},{2,1},{3,2},{4,7},{5,4},{6,5},{7,6},{8,11},{9,8},{10,9... | collective-permute-start | bytes 786440 | tf_op jit(solution)/shard_map/ppermute | solution.py:253
  141.5 1.8 %collective-permute-start.9 = (f32[2,4,8,1024]{3,0,2,1:T(2,128)S(1)}, f32[2,4,8,1024]{3,0,2,1:T(2,128)S(1)}, u32[]{:S(2)}, u32[]{:S(2)}) collective-permute-start(f32[2,4,8,1024]{3,0,2,1:T(2,128)S(1)} %bitcast.77), channel_id=1, source_target_pairs={{0,2},{1,3},{2,0},{3,1},{4,6},{5,7},{6,4},{7,5},{8,10},{9,11},{10,... | collective-permute-start | bytes 786440 | tf_op jit(solution)/shard_map/ppermute | solution.py:253
  143.2 0.1 fusion.38
  143.3 0.2 copy.56
  143.5 0.2 copy.57
  143.7 0.2 copy.55
  144.0 1.2 collective-permute-start.16
  145.2 0.9 collective-permute-start.14
  146.1 2.1 %collective-permute-done.8 = f32[2,4,8,1024]{3,0,2,1:T(2,128)S(1)} collective-permute-done((f32[2,4,8,1024]{3,0,2,1:T(2,128)S(1)}, f32[2,4,8,1024]{3,0,2,1:T(2,128)S(1)}, u32[]{:S(2)}, u32[]{:S(2)}) %collective-permute-start.8) | collective-permute-done | bytes 262176 | tf_op jit(solution)/shard_map/ppermute | solution.py:253
  148.2 1.4 collective-permute-start.15
  149.6 3.6 %collective-permute-done.10 = f32[2,4,8,1024]{3,0,2,1:T(2,128)S(1)} collective-permute-done((f32[2,4,8,1024]{3,0,2,1:T(2,128)S(1)}, f32[2,4,8,1024]{3,0,2,1:T(2,128)S(1)}, u32[]{:S(2)}, u32[]{:S(2)}) %collective-permute-start.10) | collective-permute-done | bytes 262176 | tf_op jit(solution)/shard_map/ppermute | solution.py:253
  153.2 1.8 %collective-permute-done.9 = f32[2,4,8,1024]{3,0,2,1:T(2,128)S(1)} collective-permute-done((f32[2,4,8,1024]{3,0,2,1:T(2,128)S(1)}, f32[2,4,8,1024]{3,0,2,1:T(2,128)S(1)}, u32[]{:S(2)}, u32[]{:S(2)}) %collective-permute-start.9) | collective-permute-done | bytes 262176 | tf_op jit(solution)/shard_map/ppermute | solution.py:253
  155.0 0.4 fusion.3
  155.4 1.5 collective-permute-start.12
  156.9 1.9 %collective-permute-start.13 = (f32[2,8,1024]{2,0,1:T(2,128)S(1)}, f32[2,8,1024]{2,0,1:T(2,128)S(1)}, u32[]{:S(2)}, u32[]{:S(2)}) collective-permute-start(f32[2,8,1024]{2,0,1:T(2,128)S(1)} %get-tuple-element.18), channel_id=1, source_target_pairs={{0,68},{1,69},{2,70},{3,71},{4,0},{5,1},{6,2},{7,3},{8,76},{9,77},... | collective-permute-start | bytes 196616 | tf_op jit(solution)/shard_map/ppermute | solution.py:253
  158.8 0.0 collective-permute-done.16
  158.8 0.1 collective-permute-start.11
  158.9 1.2 collective-permute-done.14
  160.2 0.4 fusion.1
  160.6 4.0 %collective-permute-start.18 = (f32[2,8,1024]{2,0,1:T(2,128)S(1)}, f32[2,8,1024]{2,0,1:T(2,128)S(1)}, u32[]{:S(2)}, u32[]{:S(2)}) collective-permute-start(f32[2,8,1024]{2,0,1:T(2,128)S(1)} %get-tuple-element.20), channel_id=1, source_target_pairs={{0,2},{1,3},{2,0},{3,1},{4,6},{5,7},{6,4},{7,5},{8,10},{9,11},{10,... | collective-permute-start | bytes 196616 | tf_op jit(solution)/shard_map/ppermute | solution.py:253
  164.6 0.1 collective-permute-start.19
  164.7 1.9 %collective-permute-start.17 = (f32[2,8,1024]{2,0,1:T(2,128)S(1)}, f32[2,8,1024]{2,0,1:T(2,128)S(1)}, u32[]{:S(2)}, u32[]{:S(2)}) collective-permute-start(f32[2,8,1024]{2,0,1:T(2,128)S(1)} %get-tuple-element.22), channel_id=1, source_target_pairs={{0,1},{1,2},{2,3},{3,0},{4,5},{5,6},{6,7},{7,4},{8,9},{9,10},{10,1... | collective-permute-start | bytes 196616 | tf_op jit(solution)/shard_map/ppermute | solution.py:253
  166.6 0.1 fusion.10
  166.7 0.1 collective-permute-done.18
  166.8 2.0 %collective-permute-done.19 = f32[2,8,1024]{2,0,1:T(2,128)S(1)} collective-permute-done((f32[2,8,1024]{2,0,1:T(2,128)S(1)}, f32[2,8,1024]{2,0,1:T(2,128)S(1)}, u32[]{:S(2)}, u32[]{:S(2)}) %collective-permute-start.19) | collective-permute-done | bytes 65568 | tf_op jit(solution)/shard_map/ppermute | solution.py:253
  168.8 1.3 collective-permute-done.17
  170.1 0.1 fusion.8
  170.2 0.7 maximum_bitcast_fusion
  (34 shorter events, 0.2 us)
Async XLA Ops:
  0.0 23.1 %copy-start = (s32[8]{0:T(128)S(1)}, s32[8]{0:T(128)}, u32[]{:S(2)}) copy-start(s32[8]{0:T(128)} %param.17) | copy-start | bytes 100
  1.8 24.7 %collective-permute-start.2 = (f32[2,72,128]{2,1,0:T(8,128)S(1)}, f32[2,72,128]{2,1,0:T(8,128)S(1)}, u32[]{:S(2)}, u32[]{:S(2)}) collective-permute-start(f32[2,72,128]{2,1,0:T(8,128)S(1)} %get-tuple-element.24), channel_id=1, source_target_pairs={{0,8},{1,9},{2,10},{3,11},{4,12},{5,13},{6,14},{7,15},{8,16},{9,17... | collective-permute-start | bytes 221192 | tf_op jit(solution)/shard_map/ppermute | solution.py:253
  3.5 22.9 %collective-permute-start.1 = (f32[2,72,128]{2,1,0:T(8,128)S(1)}, f32[2,72,128]{2,1,0:T(8,128)S(1)}, u32[]{:S(2)}, u32[]{:S(2)}) collective-permute-start(f32[2,72,128]{2,1,0:T(8,128)S(1)} %get-tuple-element.24), channel_id=1, source_target_pairs={{0,16},{1,17},{2,18},{3,19},{4,20},{5,21},{6,22},{7,23},{8,24},{9,... | collective-permute-start | bytes 221192 | tf_op jit(solution)/shard_map/ppermute | solution.py:253
  6.4 18.1 %collective-permute-start = (f32[2,72,128]{2,1,0:T(8,128)S(1)}, f32[2,72,128]{2,1,0:T(8,128)S(1)}, u32[]{:S(2)}, u32[]{:S(2)}) collective-permute-start(f32[2,72,128]{2,1,0:T(8,128)S(1)} %get-tuple-element.24), channel_id=1, source_target_pairs={{0,24},{1,25},{2,26},{3,27},{4,28},{5,29},{6,30},{7,31},{8,0},{9,1... | collective-permute-start | bytes 221192 | tf_op jit(solution)/shard_map/ppermute | solution.py:253
  7.8 21.3 %collective-permute-start.6 = (f32[2,72,128]{2,1,0:T(8,128)S(1)}, f32[2,72,128]{2,1,0:T(8,128)S(1)}, u32[]{:S(2)}, u32[]{:S(2)}) collective-permute-start(f32[2,72,128]{2,1,0:T(8,128)S(1)} %get-tuple-element.23), channel_id=1, source_target_pairs={{56,0},{57,1},{58,2},{59,3},{60,4},{61,5},{62,6},{63,7},{32,8},{33... | collective-permute-start | bytes 221192 | tf_op jit(solution)/shard_map/ppermute | solution.py:262
  9.5 19.6 %collective-permute-start.5 = (f32[2,72,128]{2,1,0:T(8,128)S(1)}, f32[2,72,128]{2,1,0:T(8,128)S(1)}, u32[]{:S(2)}, u32[]{:S(2)}) collective-permute-start(f32[2,72,128]{2,1,0:T(8,128)S(1)} %get-tuple-element.23), channel_id=1, source_target_pairs={{48,0},{49,1},{50,2},{51,3},{52,4},{53,5},{54,6},{55,7},{56,8},{57... | collective-permute-start | bytes 221192 | tf_op jit(solution)/shard_map/ppermute | solution.py:262
  16.6 12.9 %copy-start.2 = (f32[2,64]{1,0:T(2,128)S(1)}, f32[2,64]{1,0:T(2,128)}, u32[]{:S(2)}) copy-start(f32[2,64]{1,0:T(2,128)} %param.11) | copy-start | bytes 1540
  24.5 4.6 %collective-permute-start.4 = (f32[2,72,128]{2,1,0:T(8,128)S(1)}, f32[2,72,128]{2,1,0:T(8,128)S(1)}, u32[]{:S(2)}, u32[]{:S(2)}) collective-permute-start(f32[2,72,128]{2,1,0:T(8,128)S(1)} %get-tuple-element.23), channel_id=1, source_target_pairs={{40,0},{41,1},{42,2},{43,3},{44,4},{45,5},{46,6},{47,7},{48,8},{49... | collective-permute-start | bytes 221192 | tf_op jit(solution)/shard_map/ppermute | solution.py:262
  26.4 2.7 %collective-permute-start.3 = (f32[2,72,128]{2,1,0:T(8,128)S(1)}, f32[2,72,128]{2,1,0:T(8,128)S(1)}, u32[]{:S(2)}, u32[]{:S(2)}) collective-permute-start(f32[2,72,128]{2,1,0:T(8,128)S(1)} %get-tuple-element.23), channel_id=1, source_target_pairs={{32,0},{33,1},{34,2},{35,3},{36,4},{37,5},{38,6},{39,7},{40,8},{41... | collective-permute-start | bytes 221192 | tf_op jit(solution)/shard_map/ppermute | solution.py:262
  29.1 1.1 copy-start.1
  128.2 6.4 %collective-permute-start.7 = (f32[2,128,2048]{2,1,0:T(8,128)}, f32[2,128,2048]{2,1,0:T(8,128)S(1)}, u32[]{:S(2)}, u32[]{:S(2)}) collective-permute-start(f32[2,128,2048]{2,1,0:T(8,128)} %get-tuple-element.8), channel_id=1, source_target_pairs={{0,32},{1,33},{2,34},{3,35},{4,36},{5,37},{6,38},{7,39},{8,40},{9,... | collective-permute-start | bytes 6291464 | tf_op jit(solution)/shard_map/ppermute | solution.py:253
  137.3 10.9 %collective-permute-start.8 = (f32[2,4,8,1024]{3,0,2,1:T(2,128)S(1)}, f32[2,4,8,1024]{3,0,2,1:T(2,128)S(1)}, u32[]{:S(2)}, u32[]{:S(2)}) collective-permute-start(f32[2,4,8,1024]{3,0,2,1:T(2,128)S(1)} %bitcast.80), channel_id=1, source_target_pairs={{0,1},{1,2},{2,3},{3,0},{4,5},{5,6},{6,7},{7,4},{8,9},{9,10},{10,1... | collective-permute-start | bytes 786440 | tf_op jit(solution)/shard_map/ppermute | solution.py:253
  139.2 13.9 %collective-permute-start.10 = (f32[2,4,8,1024]{3,0,2,1:T(2,128)S(1)}, f32[2,4,8,1024]{3,0,2,1:T(2,128)S(1)}, u32[]{:S(2)}, u32[]{:S(2)}) collective-permute-start(f32[2,4,8,1024]{3,0,2,1:T(2,128)S(1)} %bitcast.78), channel_id=1, source_target_pairs={{0,3},{1,0},{2,1},{3,2},{4,7},{5,4},{6,5},{7,6},{8,11},{9,8},{10,9... | collective-permute-start | bytes 786440 | tf_op jit(solution)/shard_map/ppermute | solution.py:253
  141.5 13.5 %collective-permute-start.9 = (f32[2,4,8,1024]{3,0,2,1:T(2,128)S(1)}, f32[2,4,8,1024]{3,0,2,1:T(2,128)S(1)}, u32[]{:S(2)}, u32[]{:S(2)}) collective-permute-start(f32[2,4,8,1024]{3,0,2,1:T(2,128)S(1)} %bitcast.77), channel_id=1, source_target_pairs={{0,2},{1,3},{2,0},{3,1},{4,6},{5,7},{6,4},{7,5},{8,10},{9,11},{10,... | collective-permute-start | bytes 786440 | tf_op jit(solution)/shard_map/ppermute | solution.py:253
  144.0 14.8 %collective-permute-start.16 = (f32[2,4,8,1024]{3,0,2,1:T(2,128)S(1)}, f32[2,4,8,1024]{3,0,2,1:T(2,128)S(1)}, u32[]{:S(2)}, u32[]{:S(2)}) collective-permute-start(f32[2,4,8,1024]{3,0,2,1:T(2,128)S(1)} %bitcast.79), channel_id=1, source_target_pairs={{0,68},{1,69},{2,70},{3,71},{4,0},{5,1},{6,2},{7,3},{8,76},{9,77},... | collective-permute-start | bytes 786440 | tf_op jit(solution)/shard_map/ppermute | solution.py:253
  145.2 15.0 %collective-permute-start.14 = (f32[2,4,8,1024]{3,0,2,1:T(2,128)S(1)}, f32[2,4,8,1024]{3,0,2,1:T(2,128)S(1)}, u32[]{:S(2)}, u32[]{:S(2)}) collective-permute-start(f32[2,4,8,1024]{3,0,2,1:T(2,128)S(1)} %bitcast.76), channel_id=1, source_target_pairs={{0,4},{1,5},{2,6},{3,7},{4,64},{5,65},{6,66},{7,67},{8,12},{9,13},... | collective-permute-start | bytes 786440 | tf_op jit(solution)/shard_map/ppermute | solution.py:253
  148.2 12.0 %collective-permute-start.15 = (f32[2,4,8,1024]{3,0,2,1:T(2,128)S(1)}, f32[2,4,8,1024]{3,0,2,1:T(2,128)S(1)}, u32[]{:S(2)}, u32[]{:S(2)}) collective-permute-start(f32[2,4,8,1024]{3,0,2,1:T(2,128)S(1)} %bitcast.75), channel_id=1, source_target_pairs={{0,64},{1,65},{2,66},{3,67},{4,68},{5,69},{6,70},{7,71},{8,72},{9,... | collective-permute-start | bytes 786440 | tf_op jit(solution)/shard_map/ppermute | solution.py:253
  155.4 9.3 %collective-permute-start.12 = (f32[2,8,1024]{2,0,1:T(2,128)S(1)}, f32[2,8,1024]{2,0,1:T(2,128)S(1)}, u32[]{:S(2)}, u32[]{:S(2)}) collective-permute-start(f32[2,8,1024]{2,0,1:T(2,128)S(1)} %get-tuple-element.17), channel_id=1, source_target_pairs={{0,64},{1,65},{2,66},{3,67},{4,68},{5,69},{6,70},{7,71},{8,72},{9,... | collective-permute-start | bytes 196616 | tf_op jit(solution)/shard_map/ppermute | solution.py:253
  156.9 9.7 %collective-permute-start.13 = (f32[2,8,1024]{2,0,1:T(2,128)S(1)}, f32[2,8,1024]{2,0,1:T(2,128)S(1)}, u32[]{:S(2)}, u32[]{:S(2)}) collective-permute-start(f32[2,8,1024]{2,0,1:T(2,128)S(1)} %get-tuple-element.18), channel_id=1, source_target_pairs={{0,68},{1,69},{2,70},{3,71},{4,0},{5,1},{6,2},{7,3},{8,76},{9,77},... | collective-permute-start | bytes 196616 | tf_op jit(solution)/shard_map/ppermute | solution.py:253
  158.8 7.8 %collective-permute-start.11 = (f32[2,8,1024]{2,0,1:T(2,128)S(1)}, f32[2,8,1024]{2,0,1:T(2,128)S(1)}, u32[]{:S(2)}, u32[]{:S(2)}) collective-permute-start(f32[2,8,1024]{2,0,1:T(2,128)S(1)} %get-tuple-element.19), channel_id=1, source_target_pairs={{0,4},{1,5},{2,6},{3,7},{4,64},{5,65},{6,66},{7,67},{8,12},{9,13},... | collective-permute-start | bytes 196616 | tf_op jit(solution)/shard_map/ppermute | solution.py:253
  160.6 6.3 %collective-permute-start.18 = (f32[2,8,1024]{2,0,1:T(2,128)S(1)}, f32[2,8,1024]{2,0,1:T(2,128)S(1)}, u32[]{:S(2)}, u32[]{:S(2)}) collective-permute-start(f32[2,8,1024]{2,0,1:T(2,128)S(1)} %get-tuple-element.20), channel_id=1, source_target_pairs={{0,2},{1,3},{2,0},{3,1},{4,6},{5,7},{6,4},{7,5},{8,10},{9,11},{10,... | collective-permute-start | bytes 196616 | tf_op jit(solution)/shard_map/ppermute | solution.py:253
  164.6 4.3 %collective-permute-start.19 = (f32[2,8,1024]{2,0,1:T(2,128)S(1)}, f32[2,8,1024]{2,0,1:T(2,128)S(1)}, u32[]{:S(2)}, u32[]{:S(2)}) collective-permute-start(f32[2,8,1024]{2,0,1:T(2,128)S(1)} %get-tuple-element.21), channel_id=1, source_target_pairs={{0,3},{1,0},{2,1},{3,2},{4,7},{5,4},{6,5},{7,6},{8,11},{9,8},{10,9... | collective-permute-start | bytes 196616 | tf_op jit(solution)/shard_map/ppermute | solution.py:253
  164.7 5.5 %collective-permute-start.17 = (f32[2,8,1024]{2,0,1:T(2,128)S(1)}, f32[2,8,1024]{2,0,1:T(2,128)S(1)}, u32[]{:S(2)}, u32[]{:S(2)}) collective-permute-start(f32[2,8,1024]{2,0,1:T(2,128)S(1)} %get-tuple-element.22), channel_id=1, source_target_pairs={{0,1},{1,2},{2,3},{3,0},{4,5},{5,6},{6,7},{7,4},{8,9},{9,10},{10,1... | collective-permute-start | bytes 196616 | tf_op jit(solution)/shard_map/ppermute | solution.py:253

commit v2 on v1

v2 whole, which is shorter than its diff:
```python
import functools

import jax
import jax.numpy as jnp
import numpy as np
from jax import lax
from jax.experimental import pallas as pl
from jax.experimental.pallas import tpu as pltpu
from jax.sharding import Mesh, PartitionSpec as P

GRID = 16
PLANE = GRID * GRID
POINTS = GRID * PLANE
HALF = PLANE // 2
NG = 2048
VB = 64
KA_AXES = ("x_hi", "core")
BAND_AXES = ("y", "x_lo", "z")
KA = 4
BAND = 32
YS = 4
MEMBERS = BAND // YS
CHUNK = 2 * VB
KLOC = 2
DEPTH = KLOC * YS * 2 * CHUNK
ROWS = 256
OWNERS = ROWS // 16
LINES = POINTS // 128


def plane_matrices():
    point = np.arange(HALF)
    outer, inner = point // GRID, point % GRID
    parts = []
    for parity in range(2):
        turns = np.outer(2 * outer + parity, outer) + np.outer(inner, inner)
        angle = 2.0 * np.pi * (turns % GRID) / GRID
        cos, sin = np.cos(angle), np.sin(angle)
        parts.append(np.block([[cos, sin], [-sin, cos]]))
    whole = np.stack(parts).astype(np.float32)
    high = whole.astype(jnp.bfloat16)
    low = (whole - high.astype(np.float32)).astype(jnp.bfloat16)
    return high, low


def split(value):
    high = value.astype(jnp.bfloat16)
    low = (value - high.astype(jnp.float32)).astype(jnp.bfloat16)
    return high, low


def four(points):
    (ar, ai), (br, bi), (cr, ci), (dr, di) = points
    sr, si = ar + cr, ai + ci
    tr, ti = ar - cr, ai - ci
    ur, ui = br + dr, bi + di
    wr, wi = br - dr, bi - di
    return [(sr + ur, si + ui), (tr + wi, ti - wr), (sr - ur, si - ui), (tr - wi, ti + wr)]


def turned(point, power):
    re, im = point
    power %= GRID
    if power == 0:
        return re, im
    if power == 4:
        return im, -re
    if power == 2:
        root = float(np.sqrt(0.5))
        return (re + im) * root, (im - re) * root
    if power == 6:
        root = float(np.sqrt(0.5))
        return (im - re) * root, (re + im) * -root
    cos = float(np.cos(2 * np.pi * power / GRID))
    sin = float(np.sin(2 * np.pi * power / GRID))
    return re * cos + im * sin, im * cos - re * sin


def dot_t(left, right):
    return lax.dot_general(left, right, (((1,), (1,)), ((), ())), preferred_element_type=jnp.float32)


def kernel(
    place_ref, sym_ref, rows_ref, occ_hbm, emp_ref, fac_ref, whi_ref, wlo_ref, near_ref, far_ref,
    occ_ref, mid_ref, xhi0_ref, xlo0_ref, xhi1_ref, xlo1_ref, spec_ref, left_ref,
    pick0_ref, pick1_ref, pick2_ref, pick3_ref, bhi_ref, blo_ref, ahi_ref, alo_ref, idx_ref, sems,
):
    slots = ((xhi0_ref, xlo0_ref), (xhi1_ref, xlo1_ref))
    picks = (pick0_ref, pick1_ref, pick2_ref, pick3_ref)
    copies = [
        [pltpu.make_async_copy(occ_hbm.at[k, :, part], occ_ref.at[k, part], sems.at[k, part]) for part in range(2)]
        for k in range(KLOC)
    ]
    for copy in copies[0] + copies[1]:
        copy.start()

    def pairs(step, block, slot):
        xhi_ref, xlo_ref = slots[slot]
        k = step // YS
        band = block // (VB // 16)
        start = pl.multiple_of((block % (VB // 16)) * 16, 16)
        line = step * 2 + band

        def pair(a, half):
            base = a * PLANE + half * HALF
            o_re = occ_ref[k, 0, pl.ds(start, 16), pl.ds(base, HALF)]
            o_im = occ_ref[k, 1, pl.ds(start, 16), pl.ds(base, HALF)]
            at = a * 2 + half
            e_re = emp_ref[line, at : at + 1, :]
            e_im = emp_ref[line, LINES + at : LINES + at + 1, :]
            return o_re * e_re + o_im * e_im, o_re * e_im - o_im * e_re

        for a0 in range(4):
            even, odd = [], []
            for a1 in range(4):
                fr, fi = pair(4 * a1 + a0, 0)
                sr, si = pair(4 * a1 + a0, 1)
                even.append((fr + sr, fi + si))
                odd.append((fr - sr, fi - si))
            for parity, points in enumerate((even, odd)):
                for k0, point in enumerate(four(points)):
                    re, im = turned(point, a0 * k0)
                    mid_ref[parity, k0, a0, 0] = re
                    mid_ref[parity, k0, a0, 1] = im
        row = pl.multiple_of(block * 16, 16)
        for parity in range(2):
            for k0 in range(4):
                points = [(mid_ref[parity, k0, a0, 0], mid_ref[parity, k0, a0, 1]) for a0 in range(4)]
                for k1, point in enumerate(four(points)):
                    at = k0 + 4 * k1
                    for part in range(2):
                        high, low = split(point[part])
                        xhi_ref[parity, pl.ds(at * CHUNK + row, 16), pl.ds(part * HALF, HALF)] = high
                        xlo_ref[parity, pl.ds(at * CHUNK + row, 16), pl.ds(part * HALF, HALF)] = low

    def places(step, block):
        base = (step * 8 + block) * 64
        shift = rows_ref[ROWS // 8 + step // YS]
        for lane in range(64):
            idx_ref[base + lane] = (place_ref[sym_ref[base + lane]] + shift) & (POINTS * 8 - 1)

    def planes(step, tile, slot):
        xhi_ref, xlo_ref = slots[slot]
        chunk = step % YS
        for parity in range(2):
            at = pl.ds(pl.multiple_of(tile * 2 * CHUNK, 2 * CHUNK), 2 * CHUNK)
            xhi = xhi_ref[parity, at, :]
            xlo = xlo_ref[parity, at, :]
            whi = whi_ref[parity]
            wide = dot_t(jnp.concatenate([whi, wlo_ref[parity]], axis=0), xhi)
            out = dot_t(whi, xlo) + wide[:PLANE] + wide[PLANE:]
            for which in range(2):
                base = ((tile * 2 + which) * PLANE + parity * HALF) * 8 + chunk * 2
                for part in range(2):
                    spec_ref[pl.ds(base + part, HALF, stride=8), :] = out[
                        part * HALF : (part + 1) * HALF, which * CHUNK : (which + 1) * CHUNK
                    ]

    def columns(k, slot):
        return pl.ds(pl.multiple_of(k * (8 * CHUNK) + slot * CHUNK, CHUNK), CHUNK)

    def gather(k):
        def pick(at, to_ref, to):
            source = pl.multiple_of(idx_ref[k * NG + at], 8)
            to_ref[pl.ds(to, 8), :] = spec_ref[pl.ds(source, 8), :]

        def left(step, carry):
            row = pl.multiple_of(step * 16, 16)
            for lane in range(16):
                pick(rows_ref[step * 2 + lane // 8] + lane % 8, left_ref, lane * 8)
            for chunk in range(YS):
                factor = fac_ref[pl.ds(k * YS + chunk, 1), :]
                re = left_ref[pl.ds(2 * chunk, 16, stride=8), :] * factor
                im = left_ref[pl.ds(2 * chunk + 1, 16, stride=8), :] * factor
                rhi, rlo = split(re)
                ihi, ilo = split(im)
                first, second = columns(k, 2 * chunk), columns(k, 2 * chunk + 1)
                ahi_ref[pl.ds(row, 16), first] = rhi
                alo_ref[pl.ds(row, 16), first] = rlo
                ahi_ref[pl.ds(row, 16), second] = ihi
                alo_ref[pl.ds(row, 16), second] = ilo
                ahi_ref[pl.ds(ROWS + row, 16), first] = -ihi
                alo_ref[pl.ds(ROWS + row, 16), first] = -ilo
                ahi_ref[pl.ds(ROWS + row, 16), second] = rhi
                alo_ref[pl.ds(ROWS + row, 16), second] = rlo
            return carry

        lax.fori_loop(0, ROWS // 16, left, 0)

        def right(step, carry):
            for which, pick_ref in enumerate(picks):
                row = pl.multiple_of(step * (16 * len(picks)) + which * 16, 16)
                for lane in range(16):
                    pick(row + lane, pick_ref, lane * 8)
                for slot in range(8):
                    high, low = split(pick_ref[pl.ds(slot, 16, stride=8), :])
                    bhi_ref[pl.ds(row, 16), columns(k, slot)] = high
                    blo_ref[pl.ds(row, 16), columns(k, slot)] = low
            return carry

        lax.fori_loop(0, NG // (16 * len(picks)), right, 0)

    def first(block, carry):
        pairs(0, block, 0)
        places(0, block)
        return carry

    def both(step, slot):
        def body(turn, carry):
            for part in range(2):
                planes(step - 1, turn * 2 + part, 1 - slot)
                pairs(step, turn * 2 + part, slot)
                places(step, turn * 2 + part)
            return carry

        lax.fori_loop(0, 4, body, 0)

    def last(block, carry):
        for part in range(4):
            planes(KLOC * YS - 1, block * 4 + part, 1)
        return carry

    for copy in copies[0]:
        copy.wait()
    lax.fori_loop(0, 8, first, 0)

    def two(turn, carry):
        both(2 * turn + 1, 1)

        @pl.when(turn == 1)
        def _():
            for copy in copies[1]:
                copy.wait()

        both(2 * turn + 2, 0)

        @pl.when(turn == 1)
        def _():
            gather(0)

        return carry

    lax.fori_loop(0, 3, two, 0)
    both(KLOC * YS - 1, 1)
    lax.fori_loop(0, 2, last, 0)
    gather(1)

    def one_column(tile, carry):
        at = pl.ds(pl.multiple_of(tile * 256, 256), 256)
        bhi = bhi_ref[at, :]
        blo = blo_ref[at, :]
        ahi = ahi_ref[...]
        out = dot_t(ahi, bhi) + dot_t(ahi, blo) + dot_t(alo_ref[...], bhi)
        for part in range(2):
            for to in range(OWNERS):
                row = part * ROWS + to * 8
                near_ref[to, part, :, at] = out[row : row + 8]
                far_ref[to, part, :, at] = out[row + ROWS // 2 : row + ROWS // 2 + 8]
        return carry

    lax.fori_loop(0, NG // 256, one_column, 0)


def partial_rows(places, sym_map, rows, occ, emp, factor):
    whi, wlo = plane_matrices()
    vmem = pl.BlockSpec(memory_space=pltpu.VMEM)
    smem = pl.BlockSpec(memory_space=pltpu.SMEM)
    part = jax.ShapeDtypeStruct((OWNERS, 2, 8, NG), jnp.float32)
    return pl.pallas_call(
        kernel,
        out_shape=(part, part),
        in_specs=[smem, smem, smem, pl.BlockSpec(memory_space=pl.ANY), vmem, vmem, vmem, vmem],
        out_specs=(vmem, vmem),
        scratch_shapes=[
            pltpu.VMEM((KLOC, 2, VB, POINTS), jnp.float32),
            pltpu.VMEM((2, 4, 4, 2, 16, HALF), jnp.float32),
            pltpu.VMEM((2, GRID * CHUNK, PLANE), jnp.bfloat16),
            pltpu.VMEM((2, GRID * CHUNK, PLANE), jnp.bfloat16),
            pltpu.VMEM((2, GRID * CHUNK, PLANE), jnp.bfloat16),
            pltpu.VMEM((2, GRID * CHUNK, PLANE), jnp.bfloat16),
            pltpu.VMEM((POINTS * 8, CHUNK), jnp.float32),
            pltpu.VMEM((16 * 8, CHUNK), jnp.float32),
            pltpu.VMEM((16 * 8, CHUNK), jnp.float32),
            pltpu.VMEM((16 * 8, CHUNK), jnp.float32),
            pltpu.VMEM((16 * 8, CHUNK), jnp.float32),
            pltpu.VMEM((16 * 8, CHUNK), jnp.float32),
            pltpu.VMEM((NG, DEPTH), jnp.bfloat16),
            pltpu.VMEM((NG, DEPTH), jnp.bfloat16),
            pltpu.VMEM((2 * ROWS, DEPTH), jnp.bfloat16),
            pltpu.VMEM((2 * ROWS, DEPTH), jnp.bfloat16),
            pltpu.SMEM((KLOC * NG,), jnp.int32),
            pltpu.SemaphoreType.DMA((KLOC, 2)),
        ],
        compiler_params=pltpu.CompilerParams(vmem_limit_bytes=62 * 2**20),
        cost_estimate=pl.CostEstimate(flops=40 * 10**9, bytes_accessed=10 * 2**20, transcendentals=0),
    )(places, sym_map, rows, occ, emp, factor, jnp.asarray(whi), jnp.asarray(wlo))


def shifted(value, axis, by):
    size = lax.axis_size(axis)
    return lax.ppermute(value, axis, [(index, (index + by) % size) for index in range(size)])


def local(occ_orb, occ_energy, emp_orb, emp_energy, gidx, sym_map, weights, count):
    ka = lax.axis_index(KA_AXES)
    core = lax.axis_index("core")
    y = lax.axis_index("y")
    member = lax.axis_index(("x_lo", "z"))

    energy = jnp.broadcast_to(emp_energy[:, :, None, None], (KLOC, 2, 8, 128))
    lines = jnp.concatenate([emp_orb.reshape(KLOC, 2, 2 * LINES, 128), energy], axis=2)
    own = jnp.stack([lines[1], shifted(lines[0], KA_AXES, -1)])
    emp = jnp.concatenate([own] + [shifted(own, "y", -step) for step in range(1, YS)], axis=1)
    emp = emp.reshape(KLOC * YS * 2, 2 * LINES + 8, 128)

    kpoint = ka * KLOC + jnp.arange(KLOC, dtype=jnp.int32)
    wrapped = (kpoint + 1 >= KA * KLOC).astype(jnp.int32)
    target = kpoint + 1 - wrapped * (KA * KLOC)
    odd = (gidx // GRID) % 2
    outer = (gidx // (2 * GRID)) % 8
    places = (gidx // PLANE * PLANE + odd * HALF + outer * GRID + gidx % GRID) * 8

    wsum = jnp.sum(weights).astype(jnp.float32)
    scale = -4.0 / jnp.sqrt(jnp.float32(VB * 2 * BAND) * wsum) / POINTS
    owner = (y + jnp.arange(YS, dtype=jnp.int32)) % YS
    bands = owner[:, None] * (2 * MEMBERS) + member * 2 + jnp.arange(2, dtype=jnp.int32)[None, :]
    live = (bands[None] < count[target][:, None, None]).astype(jnp.float32)
    gap = emp[:, 2 * LINES, 0].reshape(KLOC, YS, 2)[..., None] - occ_energy[:, None, None, :]
    strength = (scale * weights[kpoint].astype(jnp.float32))[:, None, None, None]
    factor = (strength * live[..., None] / gap).reshape(KLOC * YS, CHUNK)

    near_core = jnp.arange(2, dtype=jnp.int32)[:, None, None]
    x = lax.axis_index(("x_hi", "x_lo"))
    z = lax.axis_index("z")
    to_x = (x + jnp.arange(4, dtype=jnp.int32)[None, :, None]) % 4
    to_z = (z + jnp.arange(4, dtype=jnp.int32)[None, None, :]) % 4
    to_ka = (to_x // 2) * 2 + (core + near_core) % 2
    rows = (to_ka * 256 + y * 64 + (to_x % 2) * 32 + to_z * 8).reshape(32)
    rows = jnp.concatenate([rows, wrapped * (PLANE * 8)])

    near, far = partial_rows(places, sym_map.reshape(KLOC * NG), rows.astype(jnp.int32), occ_orb, emp, factor)

    both = near + shifted(far, "core", 1)
    both = both.reshape(4, 4, 2, 8, NG)
    x_axes = ("x_hi", "x_lo")

    def added(own, parts):
        return own + (parts[0] + parts[1]) + parts[2]

    first, second = both[:, :, 0], both[:, :, 1]
    first_parts = [shifted(first[:, step], "z", step) for step in range(1, 4)]
    second_parts = [shifted(second[step], x_axes, step) for step in range(1, 4)]
    first = added(first[:, 0], first_parts)
    second = added(second[0], second_parts)
    first_parts = [shifted(first[step], x_axes, step) for step in range(1, 4)]
    second_parts = [shifted(second[step], "z", step) for step in range(1, 4)]
    owned = jnp.stack([added(first[0], first_parts), added(second[0], second_parts)], axis=1)
    return owned[None]


def solution(mesh):
    fine = Mesh(mesh.devices.reshape(2, 2, YS, 2, 4), KA_AXES + BAND_AXES)
    return jax.shard_map(
        local,
        mesh=fine,
        in_specs=(
            P(KA_AXES, None, None, None),
            P(KA_AXES, None),
            P(KA_AXES, BAND_AXES, None, None),
            P(KA_AXES, BAND_AXES),
            P(),
            P(KA_AXES, None),
            P(),
            P(),
        ),
        out_specs=P(None, KA_AXES + BAND_AXES, None, None),
        check_vma=False,
    )
```

time: 171 us -> 118 us (0.69)
  Pallas kernels: 98 us -> 58.1 us
  local copies, waits for them, and re-layouts: 12.8 us -> 6.4 us
  starting transfers between devices: 33 us -> 29.6 us
  waiting for transfers between devices: 18.8 us -> 16 us
    pallas_call x1, Pallas kernels: 98 us -> 58.1 us  [partial_rows(): pl.pallas_call(kernel, out_shape=(part, part), in_specs=[smem, smem, smem...]
    unnamed x19 -> x7, local copies, waits for them, and re-layouts: 7.87 us -> 1.34 us
    ppermute x20 -> x17, starting transfers between devices: 33 us -> 29.6 us  [shifted(): lax.ppermute(value, axis, [(index, (index + by) % size) for index in rang...]
    ppermute x20 -> x17, waiting for transfers between devices: 18.8 us -> 16 us  [shifted(): lax.ppermute(value, axis, [(index, (index + by) % size) for index in rang...]
  transfers between devices with their start and end apart: 20 -> 17, of which waited for: 9 -> 7; matrix products, arithmetic and copies ran while one was open for 8% -> 6% of each run, Pallas kernels for 0% -> 0%
where the time goes in v2:
time: 118 us
  Pallas kernels  58.1 us (49%)
  starting transfers between devices  29.6 us (25%)
  waiting for transfers between devices  16 us (14%)
  other arithmetic  6.7 us (6%)
  local copies, waits for them, and re-layouts  6.4 us (5%)
    pallas_call x1, Pallas kernels, partial_rows(): pl.pallas_call(kernel, out_shape=(part, part), in_specs=[smem, smem, smem...  58.1 us
    ppermute x17, starting transfers between devices, shifted(): lax.ppermute(value, axis, [(index, (index + by) % size) for index in rang...  29.6 us
    ppermute x17, waiting for transfers between devices, shifted(): lax.ppermute(value, axis, [(index, (index + by) % size) for index in rang...  16 us
  transfers between devices with their start and end apart: 17, of which 7 were waited for; matrix products, arithmetic and copies ran while one was open for 6% of the time, Pallas kernels for 0%

profile of v2, /device:TPU:0, one launch (start us, length us, event | category | flops | bytes accessed | tf_op | source)
XLA Modules:
  0.0 117.7 jit_solution(6626439593134521103)
XLA Ops:
  0.0 0.0 copy-start
  0.0 1.0 reshape.295
  1.1 0.8 broadcast_in_dim.4
  1.8 2.6 %collective-permute-start = (f32[2,72,128]{2,1,0:T(8,128)S(1)}, f32[2,72,128]{2,1,0:T(8,128)S(1)}, u32[]{:S(2)}, u32[]{:S(2)}) collective-permute-start(f32[2,72,128]{2,1,0:T(8,128)S(1)} %get-tuple-element.22), channel_id=1, source_target_pairs={{0,96},{32,0},{64,32},{96,64},{1,97},{33,1},{65,33},{97,65},{2,98}... | collective-permute-start | bytes 221192 | tf_op jit(solution)/shard_map/ppermute | solution.py:301
  4.5 1.3 %reduce_sum.9 = s32[]{:T(128)} reduce(s32[8]{0:T(128)} %param.16, s32[]{:T(128)} %constant.151.clone.1), dimensions={0}, to_apply=%region_0.1 | reduce | flops 7 | bytes 40 | tf_op jit(solution)/shard_map/reduce_sum | solution.py:323
  6.5 0.1 iota_add_fusion
  6.6 1.3 %gather_fusion.1 = s32[2]{0:T(128)S(1)} fusion(s32[8]{0:T(128)} %param.16, s32[1024]{0:T(1024)S(1)} %pad_clamp_fusion), kind=kCustom, calls=%fused_computation.1 | custom fusion | bytes 24 | tf_op jit(solution)/shard_map/gather | solution.py:329
  7.9 1.3 %fusion.15.place_ref = s32[2048]{0:T(1024)} fusion(s32[2048]{0:T(1024)} %param.14), kind=kLoop, calls=%fused_computation.57 | loop fusion | flops 139264 | bytes 16384 | tf_op jit(solution)/shard_map/mul | solution.py:321
  9.2 0.0 copy-done
  9.2 0.6 gather_fusion
  9.9 0.1 compare_select_fusion
  9.9 0.1 add_add_fusion
  10.0 0.1 broadcast_add_fusion
  10.1 0.0 collective-permute-done
  10.1 1.6 %collective-permute-start.3 = (f32[2,2,72,128]{3,2,1,0:T(8,128)S(1)}, f32[2,2,72,128]{3,2,1,0:T(8,128)S(1)}, u32[]{:S(2)}, u32[]{:S(2)}) collective-permute-start(f32[2,2,72,128]{3,2,1,0:T(8,128)S(1)} %pad_maximum_fusion.1), channel_id=1, source_target_pairs={{0,8},{8,16},{16,24},{24,0},{1,9},{9,17},{17,25},{25,1},{2,10},{10... | collective-permute-start | bytes 442376 | tf_op jit(solution)/shard_map/ppermute | solution.py:301
  11.8 2.9 %collective-permute-start.2 = (f32[2,2,72,128]{3,2,1,0:T(8,128)S(1)}, f32[2,2,72,128]{3,2,1,0:T(8,128)S(1)}, u32[]{:S(2)}, u32[]{:S(2)}) collective-permute-start(f32[2,2,72,128]{3,2,1,0:T(8,128)S(1)} %pad_maximum_fusion.1), channel_id=1, source_target_pairs={{0,16},{8,24},{16,0},{24,8},{1,17},{9,25},{17,1},{25,9},{2,18},{10... | collective-permute-start | bytes 442376 | tf_op jit(solution)/shard_map/ppermute | solution.py:301
  14.7 1.3 %collective-permute-start.1 = (f32[2,2,72,128]{3,2,1,0:T(8,128)S(1)}, f32[2,2,72,128]{3,2,1,0:T(8,128)S(1)}, u32[]{:S(2)}, u32[]{:S(2)}) collective-permute-start(f32[2,2,72,128]{3,2,1,0:T(8,128)S(1)} %pad_maximum_fusion.1), channel_id=1, source_target_pairs={{0,24},{8,0},{16,8},{24,16},{1,25},{9,1},{17,9},{25,17},{2,26},{10... | collective-permute-start | bytes 442376 | tf_op jit(solution)/shard_map/ppermute | solution.py:301
  16.0 0.1 add.349
  16.1 1.3 %copy.26 = s32[1,16,2,128]{3,1,2,0:T(8,128)} copy(s32[1,16,2,128]{3,2,1,0:T(2,128)} %bitcast.78) | data formatting | bytes 32768
  17.4 0.7 pad_add_fusion.rows_ref
  18.1 0.0 collective-permute-done.3
  18.1 1.5 %collective-permute-done.2 = f32[2,2,72,128]{3,2,1,0:T(8,128)S(1)} collective-permute-done((f32[2,2,72,128]{3,2,1,0:T(8,128)S(1)}, f32[2,2,72,128]{3,2,1,0:T(8,128)S(1)}, u32[]{:S(2)}, u32[]{:S(2)}) %collective-permute-start.2) | collective-permute-done | bytes 147488 | tf_op jit(solution)/shard_map/ppermute | solution.py:301
  19.6 0.2 collective-permute-done.1
  19.8 0.0 copy-start.1
  19.8 0.2 slice_reduce_fusion
  20.1 0.1 sub.50
  20.1 0.0 copy-done.2
  20.1 0.1 subtract_divide_fusion
  20.2 0.7 div.76.fac_ref
  20.9 0.0 copy-done.1
  20.9 58.1 %shard_map.100 = (f32[16,2,8,2048]{3,2,1,0:T(8,128)}, f32[16,2,8,2048]{3,2,1,0:T(8,128)}) custom-call(s32[2048]{0:T(1024)} %fusion.15.place_ref, s32[4096]{0:T(1024)} %bitcast.79, s32[34]{0:T(128)} %pad_add_fusion.rows_ref, f32[2,64,2,4096]{3,2,1,0:T(2,128)} %occ_hbm.1, f32[16,72,128]{2,1,0:T(8,128)} %bitcast.75, f32[8,128]{1,0:T(8,128)} %div.76.fac_ref, ...), custom_call_target="tpu_custom_call" | custom-call | flops 40000000000 | bytes 10485760 | tf_op jit(solution)/shard_map/pallas_call | solution.py:269
  79.0 0.1 collective-permute-start.4
  79.1 4.4 %collective-permute-done.4 = f32[16,2,8,2048]{3,2,1,0:T(8,128)S(1)} collective-permute-done((f32[16,2,8,2048]{3,2,1,0:T(8,128)}, f32[16,2,8,2048]{3,2,1,0:T(8,128)S(1)}, u32[]{:S(2)}, u32[]{:S(2)}) %collective-permute-start.4) | collective-permute-done | bytes 2097184 | tf_op jit(solution)/shard_map/ppermute | solution.py:301
  83.5 1.9 %add.368 = f32[16,2,8,2048]{3,2,1,0:T(8,128)S(1)} add(f32[16,2,8,2048]{3,2,1,0:T(8,128)} %get-tuple-element.7, f32[16,2,8,2048]{3,2,1,0:T(8,128)S(1)} %collective-permute-done.4) | non-fusion elementwise | flops 524288 | bytes 6291456 | tf_op jit(solution)/shard_map/add | solution.py:343
  85.4 0.1 slice_bitcast_fusion.1
  85.5 0.1 copy_bitcast_fusion
  85.5 2.9 %collective-permute-start.12 = (f32[4,8,2048]{2,1,0:T(8,128)S(1)}, f32[4,8,2048]{2,1,0:T(8,128)S(1)}, u32[]{:S(2)}, u32[]{:S(2)}) collective-permute-start(f32[4,8,2048]{2,1,0:T(8,128)S(1)} %get-tuple-element.9), channel_id=1, source_target_pairs={{0,64},{4,68},{64,0},{68,4},{1,65},{5,69},{65,1},{69,5},{2,66},{6,... | collective-permute-start | bytes 786440 | tf_op jit(solution)/shard_map/ppermute | solution.py:301
  88.4 0.6 collective-permute-start.11
  89.0 2.6 %collective-permute-start.13 = (f32[4,8,2048]{2,1,0:T(8,128)S(1)}, f32[4,8,2048]{2,1,0:T(8,128)S(1)}, u32[]{:S(2)}, u32[]{:S(2)}) collective-permute-start(f32[4,8,2048]{2,1,0:T(8,128)S(1)} %get-tuple-element.11), channel_id=1, source_target_pairs={{0,68},{4,0},{64,4},{68,64},{1,69},{5,1},{65,5},{69,65},{2,70},{6,... | collective-permute-start | bytes 786440 | tf_op jit(solution)/shard_map/ppermute | solution.py:301
  91.7 0.1 slice_bitcast_fusion.5
  91.7 4.0 %collective-permute-start.6 = (f32[4,8,2048]{2,1,0:T(8,128)S(1)}, f32[4,8,2048]{2,1,0:T(8,128)S(1)}, u32[]{:S(2)}, u32[]{:S(2)}) collective-permute-start(f32[4,8,2048]{2,1,0:T(8,128)S(1)} %get-tuple-element.12), channel_id=1, source_target_pairs={{0,2},{1,3},{2,0},{3,1},{4,6},{5,7},{6,4},{7,5},{8,10},{9,11},{10,... | collective-permute-start | bytes 786440 | tf_op jit(solution)/shard_map/ppermute | solution.py:301
  95.7 0.7 collective-permute-start.7
  96.4 0.0 collective-permute-done.12
  96.4 1.8 %collective-permute-start.5 = (f32[4,8,2048]{2,1,0:T(8,128)S(1)}, f32[4,8,2048]{2,1,0:T(8,128)S(1)}, u32[]{:S(2)}, u32[]{:S(2)}) collective-permute-start(f32[4,8,2048]{2,1,0:T(8,128)S(1)} %get-tuple-element.14), channel_id=1, source_target_pairs={{0,1},{1,2},{2,3},{3,0},{4,5},{5,6},{6,7},{7,4},{8,9},{9,10},{10,1... | collective-permute-start | bytes 786440 | tf_op jit(solution)/shard_map/ppermute | solution.py:301
  98.2 2.9 %collective-permute-done.11 = f32[4,8,2048]{2,1,0:T(8,128)S(1)} collective-permute-done((f32[4,8,2048]{2,1,0:T(8,128)S(1)}, f32[4,8,2048]{2,1,0:T(8,128)S(1)}, u32[]{:S(2)}, u32[]{:S(2)}) %collective-permute-start.11) | collective-permute-done | bytes 262176 | tf_op jit(solution)/shard_map/ppermute | solution.py:301
  101.1 0.0 collective-permute-done.13
  101.1 0.1 fusion.1
  101.2 4.0 %collective-permute-start.15 = (f32[8,2048]{1,0:T(8,128)S(1)}, f32[8,2048]{1,0:T(8,128)S(1)}, u32[]{:S(2)}, u32[]{:S(2)}) collective-permute-start(f32[8,2048]{1,0:T(8,128)S(1)} %get-tuple-element.18), channel_id=1, source_target_pairs={{0,2},{1,3},{2,0},{3,1},{4,6},{5,7},{6,4},{7,5},{8,10},{9,11},{10,... | collective-permute-start | bytes 196616 | tf_op jit(solution)/shard_map/ppermute | solution.py:301
  105.2 0.7 collective-permute-start.16
  105.9 0.0 collective-permute-done.6
  105.9 1.3 %collective-permute-start.14 = (f32[8,2048]{1,0:T(8,128)S(1)}, f32[8,2048]{1,0:T(8,128)S(1)}, u32[]{:S(2)}, u32[]{:S(2)}) collective-permute-start(f32[8,2048]{1,0:T(8,128)S(1)} %get-tuple-element.20), channel_id=1, source_target_pairs={{0,1},{1,2},{2,3},{3,0},{4,5},{5,6},{6,7},{7,4},{8,9},{9,10},{10,1... | collective-permute-start | bytes 196616 | tf_op jit(solution)/shard_map/ppermute | solution.py:301
  107.2 1.7 %collective-permute-done.7 = f32[4,8,2048]{2,1,0:T(8,128)S(1)} collective-permute-done((f32[4,8,2048]{2,1,0:T(8,128)S(1)}, f32[4,8,2048]{2,1,0:T(8,128)S(1)}, u32[]{:S(2)}, u32[]{:S(2)}) %collective-permute-start.7) | collective-permute-done | bytes 262176 | tf_op jit(solution)/shard_map/ppermute | solution.py:301
  108.9 0.0 collective-permute-done.5
  108.9 0.1 fusion.3
  109.0 0.3 collective-permute-start.9
  109.3 2.1 %collective-permute-start.10 = (f32[8,2048]{1,0:T(8,128)S(1)}, f32[8,2048]{1,0:T(8,128)S(1)}, u32[]{:S(2)}, u32[]{:S(2)}) collective-permute-start(f32[8,2048]{1,0:T(8,128)S(1)} %get-tuple-element.16), channel_id=1, source_target_pairs={{0,68},{4,0},{64,4},{68,64},{1,69},{5,1},{65,5},{69,65},{2,70},{6,... | collective-permute-start | bytes 196616 | tf_op jit(solution)/shard_map/ppermute | solution.py:301
  111.4 0.0 collective-permute-done.15
  111.4 0.0 collective-permute-start.8
  111.4 0.0 collective-permute-done.16
  111.4 0.0 collective-permute-done.14
  111.5 3.4 %collective-permute-done.9 = f32[8,2048]{1,0:T(8,128)S(1)} collective-permute-done((f32[8,2048]{1,0:T(8,128)S(1)}, f32[8,2048]{1,0:T(8,128)S(1)}, u32[]{:S(2)}, u32[]{:S(2)}) %collective-permute-start.9) | collective-permute-done | bytes 65568 | tf_op jit(solution)/shard_map/ppermute | solution.py:301
  114.9 0.0 collective-permute-done.10
  114.9 1.9 %collective-permute-done.8 = f32[8,2048]{1,0:T(8,128)S(1)} collective-permute-done((f32[8,2048]{1,0:T(8,128)S(1)}, f32[8,2048]{1,0:T(8,128)S(1)}, u32[]{:S(2)}, u32[]{:S(2)}) %collective-permute-start.8) | collective-permute-done | bytes 65568 | tf_op jit(solution)/shard_map/ppermute | solution.py:301
  117.0 0.8 maximum_bitcast_fusion
  (19 shorter events, 0.3 us)
Async XLA Ops:
  0.0 9.2 %copy-start = (s32[8]{0:T(128)S(1)}, s32[8]{0:T(128)}, u32[]{:S(2)}) copy-start(s32[8]{0:T(128)} %param.17) | copy-start | bytes 100
  0.0 20.1 %copy-start.2 = (f32[2,64]{1,0:T(2,128)S(1)}, f32[2,64]{1,0:T(2,128)}, u32[]{:S(2)}) copy-start(f32[2,64]{1,0:T(2,128)} %param.11) | copy-start | bytes 1540
  1.8 8.3 %collective-permute-start = (f32[2,72,128]{2,1,0:T(8,128)S(1)}, f32[2,72,128]{2,1,0:T(8,128)S(1)}, u32[]{:S(2)}, u32[]{:S(2)}) collective-permute-start(f32[2,72,128]{2,1,0:T(8,128)S(1)} %get-tuple-element.22), channel_id=1, source_target_pairs={{0,96},{32,0},{64,32},{96,64},{1,97},{33,1},{65,33},{97,65},{2,98}... | collective-permute-start | bytes 221192 | tf_op jit(solution)/shard_map/ppermute | solution.py:301
  10.1 8.0 %collective-permute-start.3 = (f32[2,2,72,128]{3,2,1,0:T(8,128)S(1)}, f32[2,2,72,128]{3,2,1,0:T(8,128)S(1)}, u32[]{:S(2)}, u32[]{:S(2)}) collective-permute-start(f32[2,2,72,128]{3,2,1,0:T(8,128)S(1)} %pad_maximum_fusion.1), channel_id=1, source_target_pairs={{0,8},{8,16},{16,24},{24,0},{1,9},{9,17},{17,25},{25,1},{2,10},{10... | collective-permute-start | bytes 442376 | tf_op jit(solution)/shard_map/ppermute | solution.py:301
  11.8 7.8 %collective-permute-start.2 = (f32[2,2,72,128]{3,2,1,0:T(8,128)S(1)}, f32[2,2,72,128]{3,2,1,0:T(8,128)S(1)}, u32[]{:S(2)}, u32[]{:S(2)}) collective-permute-start(f32[2,2,72,128]{3,2,1,0:T(8,128)S(1)} %pad_maximum_fusion.1), channel_id=1, source_target_pairs={{0,16},{8,24},{16,0},{24,8},{1,17},{9,25},{17,1},{25,9},{2,18},{10... | collective-permute-start | bytes 442376 | tf_op jit(solution)/shard_map/ppermute | solution.py:301
  14.7 5.1 %collective-permute-start.1 = (f32[2,2,72,128]{3,2,1,0:T(8,128)S(1)}, f32[2,2,72,128]{3,2,1,0:T(8,128)S(1)}, u32[]{:S(2)}, u32[]{:S(2)}) collective-permute-start(f32[2,2,72,128]{3,2,1,0:T(8,128)S(1)} %pad_maximum_fusion.1), channel_id=1, source_target_pairs={{0,24},{8,0},{16,8},{24,16},{1,25},{9,1},{17,9},{25,17},{2,26},{10... | collective-permute-start | bytes 442376 | tf_op jit(solution)/shard_map/ppermute | solution.py:301
  19.8 1.1 copy-start.1
  79.0 4.5 %collective-permute-start.4 = (f32[16,2,8,2048]{3,2,1,0:T(8,128)}, f32[16,2,8,2048]{3,2,1,0:T(8,128)S(1)}, u32[]{:S(2)}, u32[]{:S(2)}) collective-permute-start(f32[16,2,8,2048]{3,2,1,0:T(8,128)} %get-tuple-element.8), channel_id=1, source_target_pairs={{0,32},{32,0},{1,33},{33,1},{2,34},{34,2},{3,35},{35,3},{4,36},{36... | collective-permute-start | bytes 6291464 | tf_op jit(solution)/shard_map/ppermute | solution.py:301
  85.5 10.8 %collective-permute-start.12 = (f32[4,8,2048]{2,1,0:T(8,128)S(1)}, f32[4,8,2048]{2,1,0:T(8,128)S(1)}, u32[]{:S(2)}, u32[]{:S(2)}) collective-permute-start(f32[4,8,2048]{2,1,0:T(8,128)S(1)} %get-tuple-element.9), channel_id=1, source_target_pairs={{0,64},{4,68},{64,0},{68,4},{1,65},{5,69},{65,1},{69,5},{2,66},{6,... | collective-permute-start | bytes 786440 | tf_op jit(solution)/shard_map/ppermute | solution.py:301
  88.4 12.7 %collective-permute-start.11 = (f32[4,8,2048]{2,1,0:T(8,128)S(1)}, f32[4,8,2048]{2,1,0:T(8,128)S(1)}, u32[]{:S(2)}, u32[]{:S(2)}) collective-permute-start(f32[4,8,2048]{2,1,0:T(8,128)S(1)} %get-tuple-element.10), channel_id=1, source_target_pairs={{0,4},{4,64},{64,68},{68,0},{1,5},{5,65},{65,69},{69,1},{2,6},{6,6... | collective-permute-start | bytes 786440 | tf_op jit(solution)/shard_map/ppermute | solution.py:301
  89.0 12.1 %collective-permute-start.13 = (f32[4,8,2048]{2,1,0:T(8,128)S(1)}, f32[4,8,2048]{2,1,0:T(8,128)S(1)}, u32[]{:S(2)}, u32[]{:S(2)}) collective-permute-start(f32[4,8,2048]{2,1,0:T(8,128)S(1)} %get-tuple-element.11), channel_id=1, source_target_pairs={{0,68},{4,0},{64,4},{68,64},{1,69},{5,1},{65,5},{69,65},{2,70},{6,... | collective-permute-start | bytes 786440 | tf_op jit(solution)/shard_map/ppermute | solution.py:301
  91.7 14.1 %collective-permute-start.6 = (f32[4,8,2048]{2,1,0:T(8,128)S(1)}, f32[4,8,2048]{2,1,0:T(8,128)S(1)}, u32[]{:S(2)}, u32[]{:S(2)}) collective-permute-start(f32[4,8,2048]{2,1,0:T(8,128)S(1)} %get-tuple-element.12), channel_id=1, source_target_pairs={{0,2},{1,3},{2,0},{3,1},{4,6},{5,7},{6,4},{7,5},{8,10},{9,11},{10,... | collective-permute-start | bytes 786440 | tf_op jit(solution)/shard_map/ppermute | solution.py:301
  95.7 13.2 %collective-permute-start.7 = (f32[4,8,2048]{2,1,0:T(8,128)S(1)}, f32[4,8,2048]{2,1,0:T(8,128)S(1)}, u32[]{:S(2)}, u32[]{:S(2)}) collective-permute-start(f32[4,8,2048]{2,1,0:T(8,128)S(1)} %get-tuple-element.13), channel_id=1, source_target_pairs={{0,3},{1,0},{2,1},{3,2},{4,7},{5,4},{6,5},{7,6},{8,11},{9,8},{10,9... | collective-permute-start | bytes 786440 | tf_op jit(solution)/shard_map/ppermute | solution.py:301
  96.4 12.5 %collective-permute-start.5 = (f32[4,8,2048]{2,1,0:T(8,128)S(1)}, f32[4,8,2048]{2,1,0:T(8,128)S(1)}, u32[]{:S(2)}, u32[]{:S(2)}) collective-permute-start(f32[4,8,2048]{2,1,0:T(8,128)S(1)} %get-tuple-element.14), channel_id=1, source_target_pairs={{0,1},{1,2},{2,3},{3,0},{4,5},{5,6},{6,7},{7,4},{8,9},{9,10},{10,1... | collective-permute-start | bytes 786440 | tf_op jit(solution)/shard_map/ppermute | solution.py:301
  101.2 10.2 %collective-permute-start.15 = (f32[8,2048]{1,0:T(8,128)S(1)}, f32[8,2048]{1,0:T(8,128)S(1)}, u32[]{:S(2)}, u32[]{:S(2)}) collective-permute-start(f32[8,2048]{1,0:T(8,128)S(1)} %get-tuple-element.18), channel_id=1, source_target_pairs={{0,2},{1,3},{2,0},{3,1},{4,6},{5,7},{6,4},{7,5},{8,10},{9,11},{10,... | collective-permute-start | bytes 196616 | tf_op jit(solution)/shard_map/ppermute | solution.py:301
  105.2 6.3 %collective-permute-start.16 = (f32[8,2048]{1,0:T(8,128)S(1)}, f32[8,2048]{1,0:T(8,128)S(1)}, u32[]{:S(2)}, u32[]{:S(2)}) collective-permute-start(f32[8,2048]{1,0:T(8,128)S(1)} %get-tuple-element.19), channel_id=1, source_target_pairs={{0,3},{1,0},{2,1},{3,2},{4,7},{5,4},{6,5},{7,6},{8,11},{9,8},{10,9... | collective-permute-start | bytes 196616 | tf_op jit(solution)/shard_map/ppermute | solution.py:301
  105.9 5.5 %collective-permute-start.14 = (f32[8,2048]{1,0:T(8,128)S(1)}, f32[8,2048]{1,0:T(8,128)S(1)}, u32[]{:S(2)}, u32[]{:S(2)}) collective-permute-start(f32[8,2048]{1,0:T(8,128)S(1)} %get-tuple-element.20), channel_id=1, source_target_pairs={{0,1},{1,2},{2,3},{3,0},{4,5},{5,6},{6,7},{7,4},{8,9},{9,10},{10,1... | collective-permute-start | bytes 196616 | tf_op jit(solution)/shard_map/ppermute | solution.py:301
  109.0 6.0 %collective-permute-start.9 = (f32[8,2048]{1,0:T(8,128)S(1)}, f32[8,2048]{1,0:T(8,128)S(1)}, u32[]{:S(2)}, u32[]{:S(2)}) collective-permute-start(f32[8,2048]{1,0:T(8,128)S(1)} %get-tuple-element.15), channel_id=1, source_target_pairs={{0,64},{4,68},{64,0},{68,4},{1,65},{5,69},{65,1},{69,5},{2,66},{6,... | collective-permute-start | bytes 196616 | tf_op jit(solution)/shard_map/ppermute | solution.py:301
  109.3 5.6 %collective-permute-start.10 = (f32[8,2048]{1,0:T(8,128)S(1)}, f32[8,2048]{1,0:T(8,128)S(1)}, u32[]{:S(2)}, u32[]{:S(2)}) collective-permute-start(f32[8,2048]{1,0:T(8,128)S(1)} %get-tuple-element.16), channel_id=1, source_target_pairs={{0,68},{4,0},{64,4},{68,64},{1,69},{5,1},{65,5},{69,65},{2,70},{6,... | collective-permute-start | bytes 196616 | tf_op jit(solution)/shard_map/ppermute | solution.py:301
  111.4 5.5 %collective-permute-start.8 = (f32[8,2048]{1,0:T(8,128)S(1)}, f32[8,2048]{1,0:T(8,128)S(1)}, u32[]{:S(2)}, u32[]{:S(2)}) collective-permute-start(f32[8,2048]{1,0:T(8,128)S(1)} %get-tuple-element.17), channel_id=1, source_target_pairs={{0,4},{4,64},{64,68},{68,0},{1,5},{5,65},{65,69},{69,1},{2,6},{6,6... | collective-permute-start | bytes 196616 | tf_op jit(solution)/shard_map/ppermute | solution.py:301

commit v3 on v2

--- a/solution.py
+++ b/solution.py
@@ -22,10 +22,10 @@
 MEMBERS = BAND // YS
 CHUNK = 2 * VB
 KLOC = 2
-DEPTH = KLOC * YS * 2 * CHUNK
+DEPTH = YS * 2 * CHUNK
 ROWS = 256
 OWNERS = ROWS // 16
-LINES = POINTS // 128
+WIDE = POINTS + 128
 
 
 def plane_matrices():
@@ -81,17 +81,24 @@
 
 
 def kernel(
-    place_ref, sym_ref, rows_ref, occ_hbm, emp_ref, fac_ref, whi_ref, wlo_ref, near_ref, far_ref,
-    occ_ref, mid_ref, xhi0_ref, xlo0_ref, xhi1_ref, xlo1_ref, spec_ref, left_ref,
-    pick0_ref, pick1_ref, pick2_ref, pick3_ref, bhi_ref, blo_ref, ahi_ref, alo_ref, idx_ref, sems,
+    place_ref, sym_ref, rows_ref, occ_hbm, emp_hbm, fac_ref, whi_hbm, wlo_hbm, near_hbm, far_hbm,
+    occ_ref, emp_ref, whi_ref, wlo_ref, mid_ref, xhi0_ref, xlo0_ref, xhi1_ref, xlo1_ref, spec_ref, left_ref,
+    pick0_ref, pick1_ref, pick2_ref, pick3_ref, bhi0_ref, blo0_ref, bhi1_ref, blo1_ref,
+    ahi0_ref, alo0_ref, ahi1_ref, alo1_ref, near_ref, far_ref, idx_ref, occ_sems, in_sems, out_sems,
 ):
     slots = ((xhi0_ref, xlo0_ref), (xhi1_ref, xlo1_ref))
     picks = (pick0_ref, pick1_ref, pick2_ref, pick3_ref)
+    rights = ((bhi0_ref, blo0_ref), (bhi1_ref, blo1_ref))
+    lefts = ((ahi0_ref, alo0_ref), (ahi1_ref, alo1_ref))
     copies = [
-        [pltpu.make_async_copy(occ_hbm.at[k, :, part], occ_ref.at[k, part], sems.at[k, part]) for part in range(2)]
+        [pltpu.make_async_copy(occ_hbm.at[k, :, part], occ_ref.at[k, part], occ_sems.at[k, part]) for part in range(2)]
         for k in range(KLOC)
     ]
-    for copy in copies[0] + copies[1]:
+    others = [
+        pltpu.make_async_copy(source, target, in_sems.at[which])
+        for which, (source, target) in enumerate(((emp_hbm, emp_ref), (whi_hbm, whi_ref), (wlo_hbm, wlo_ref)))
+    ]
+    for copy in [others[0]] + copies[0] + others[1:] + copies[1]:
         copy.start()
 
     def pairs(step, block, slot):
@@ -105,9 +112,8 @@
             base = a * PLANE + half * HALF
             o_re = occ_ref[k, 0, pl.ds(start, 16), pl.ds(base, HALF)]
             o_im = occ_ref[k, 1, pl.ds(start, 16), pl.ds(base, HALF)]
-            at = a * 2 + half
-            e_re = emp_ref[line, at : at + 1, :]
-            e_im = emp_ref[line, LINES + at : LINES + at + 1, :]
+            e_re = emp_ref[line, 0:1, pl.ds(base, HALF)]
+            e_im = emp_ref[line, 1:2, pl.ds(base, HALF)]
             return o_re * e_re + o_im * e_im, o_re * e_im - o_im * e_re
 
         for a0 in range(4):
@@ -156,25 +162,27 @@
                         part * HALF : (part + 1) * HALF, which * CHUNK : (which + 1) * CHUNK
                     ]
 
-    def columns(k, slot):
-        return pl.ds(pl.multiple_of(k * (8 * CHUNK) + slot * CHUNK, CHUNK), CHUNK)
-
-    def gather(k):
-        def pick(at, to_ref, to):
-            source = pl.multiple_of(idx_ref[k * NG + at], 8)
-            to_ref[pl.ds(to, 8), :] = spec_ref[pl.ds(source, 8), :]
+    def columns(slot):
+        return pl.ds(slot * CHUNK, CHUNK)
+
+    def pick(k, at, to_ref, to):
+        source = pl.multiple_of(idx_ref[k * NG + at], 8)
+        to_ref[pl.ds(to, 8), :] = spec_ref[pl.ds(source, 8), :]
+
+    def gather_left(k):
+        ahi_ref, alo_ref = lefts[k]
 
         def left(step, carry):
             row = pl.multiple_of(step * 16, 16)
             for lane in range(16):
-                pick(rows_ref[step * 2 + lane // 8] + lane % 8, left_ref, lane * 8)
+                pick(k, rows_ref[step * 2 + lane // 8] + lane % 8, left_ref, lane * 8)
             for chunk in range(YS):
-                factor = fac_ref[pl.ds(k * YS + chunk, 1), :]
+                factor = fac_ref[k * YS + chunk : k * YS + chunk + 1, :]
                 re = left_ref[pl.ds(2 * chunk, 16, stride=8), :] * factor
                 im = left_ref[pl.ds(2 * chunk + 1, 16, stride=8), :] * factor
                 rhi, rlo = split(re)
                 ihi, ilo = split(im)
-                first, second = columns(k, 2 * chunk), columns(k, 2 * chunk + 1)
+                first, second = columns(2 * chunk), columns(2 * chunk + 1)
                 ahi_ref[pl.ds(row, 16), first] = rhi
                 alo_ref[pl.ds(row, 16), first] = rlo
                 ahi_ref[pl.ds(row, 16), second] = ihi
@@ -187,18 +195,28 @@
 
         lax.fori_loop(0, ROWS // 16, left, 0)
 
+    def gather(k):
+        bhi_ref, blo_ref = rights[k]
+        gather_left(k)
+
         def right(step, carry):
             for which, pick_ref in enumerate(picks):
                 row = pl.multiple_of(step * (16 * len(picks)) + which * 16, 16)
                 for lane in range(16):
-                    pick(row + lane, pick_ref, lane * 8)
+                    pick(k, row + lane, pick_ref, lane * 8)
                 for slot in range(8):
                     high, low = split(pick_ref[pl.ds(slot, 16, stride=8), :])
-                    bhi_ref[pl.ds(row, 16), columns(k, slot)] = high
-                    blo_ref[pl.ds(row, 16), columns(k, slot)] = low
+                    bhi_ref[pl.ds(row, 16), columns(slot)] = high
+                    blo_ref[pl.ds(row, 16), columns(slot)] = low
             return carry
 
         lax.fori_loop(0, NG // (16 * len(picks)), right, 0)
+
+    def product(k, at):
+        (ahi_ref, alo_ref), (bhi_ref, blo_ref) = lefts[k], rights[k]
+        bhi = bhi_ref[at, :]
+        ahi = ahi_ref[...]
+        return dot_t(ahi, bhi) + dot_t(ahi, blo_ref[at, :]) + dot_t(alo_ref[...], bhi)
 
     def first(block, carry):
         pairs(0, block, 0)
@@ -220,7 +238,7 @@
             planes(KLOC * YS - 1, block * 4 + part, 1)
         return carry
 
-    for copy in copies[0]:
+    for copy in copies[0] + others:
         copy.wait()
     lax.fori_loop(0, 8, first, 0)
 
@@ -245,51 +263,66 @@
     lax.fori_loop(0, 2, last, 0)
     gather(1)
 
+    def places_of(tile):
+        return pl.ds(pl.multiple_of(tile * 256, 256), 256)
+
+    def sent(tile):
+        return [
+            pltpu.make_async_copy(
+                source.at[:, :, :, places_of(tile)], target.at[:, :, :, places_of(tile)], out_sems.at[tile, which]
+            )
+            for which, (source, target) in enumerate(((near_ref, near_hbm), (far_ref, far_hbm)))
+        ]
+
     def one_column(tile, carry):
-        at = pl.ds(pl.multiple_of(tile * 256, 256), 256)
-        bhi = bhi_ref[at, :]
-        blo = blo_ref[at, :]
-        ahi = ahi_ref[...]
-        out = dot_t(ahi, bhi) + dot_t(ahi, blo) + dot_t(alo_ref[...], bhi)
+        out = product(0, places_of(tile)) + product(1, places_of(tile))
         for part in range(2):
             for to in range(OWNERS):
                 row = part * ROWS + to * 8
-                near_ref[to, part, :, at] = out[row : row + 8]
-                far_ref[to, part, :, at] = out[row + ROWS // 2 : row + ROWS // 2 + 8]
+                near_ref[to, part, :, places_of(tile)] = out[row : row + 8]
+                far_ref[to, part, :, places_of(tile)] = out[row + ROWS // 2 : row + ROWS // 2 + 8]
+        for copy in sent(tile):
+            copy.start()
         return carry
 
+    def done(tile, carry):
+        for copy in sent(tile):
+            copy.wait()
+        return carry
+
     lax.fori_loop(0, NG // 256, one_column, 0)
+    lax.fori_loop(0, NG // 256, done, 0)
 
 
 def partial_rows(places, sym_map, rows, occ, emp, factor):
     whi, wlo = plane_matrices()
     vmem = pl.BlockSpec(memory_space=pltpu.VMEM)
     smem = pl.BlockSpec(memory_space=pltpu.SMEM)
+    hbm = pl.BlockSpec(memory_space=pl.ANY)
     part = jax.ShapeDtypeStruct((OWNERS, 2, 8, NG), jnp.float32)
     return pl.pallas_call(
         kernel,
         out_shape=(part, part),
-        in_specs=[smem, smem, smem, pl.BlockSpec(memory_space=pl.ANY), vmem, vmem, vmem, vmem],
-        out_specs=(vmem, vmem),
+        in_specs=[smem, smem, smem, hbm, hbm, vmem, hbm, hbm],
+        out_specs=(hbm, hbm),
         scratch_shapes=[
             pltpu.VMEM((KLOC, 2, VB, POINTS), jnp.float32),
+            pltpu.VMEM((KLOC * YS * 2, 2, WIDE), jnp.float32),
+            pltpu.VMEM((2, PLANE, PLANE), jnp.bfloat16),
+            pltpu.VMEM((2, PLANE, PLANE), jnp.bfloat16),
             pltpu.VMEM((2, 4, 4, 2, 16, HALF), jnp.float32),
-            pltpu.VMEM((2, GRID * CHUNK, PLANE), jnp.bfloat16),
-            pltpu.VMEM((2, GRID * CHUNK, PLANE), jnp.bfloat16),
-            pltpu.VMEM((2, GRID * CHUNK, PLANE), jnp.bfloat16),
-            pltpu.VMEM((2, GRID * CHUNK, PLANE), jnp.bfloat16),
-            pltpu.VMEM((POINTS * 8, CHUNK), jnp.float32),
-            pltpu.VMEM((16 * 8, CHUNK), jnp.float32),
-            pltpu.VMEM((16 * 8, CHUNK), jnp.float32),
-            pltpu.VMEM((16 * 8, CHUNK), jnp.float32),
-            pltpu.VMEM((16 * 8, CHUNK), jnp.float32),
-            pltpu.VMEM((16 * 8, CHUNK), jnp.float32),
-            pltpu.VMEM((NG, DEPTH), jnp.bfloat16),
-            pltpu.VMEM((NG, DEPTH), jnp.bfloat16),
-            pltpu.VMEM((2 * ROWS, DEPTH), jnp.bfloat16),
-            pltpu.VMEM((2 * ROWS, DEPTH), jnp.bfloat16),
+        ]
+        + [pltpu.VMEM((2, GRID * CHUNK, PLANE), jnp.bfloat16)] * 4
+        + [pltpu.VMEM((POINTS * 8, CHUNK), jnp.float32)]
+        + [pltpu.VMEM((16 * 8, CHUNK), jnp.float32)] * 5
+        + [pltpu.VMEM((NG, DEPTH), jnp.bfloat16)] * 4
+        + [pltpu.VMEM((2 * ROWS, DEPTH), jnp.bfloat16)] * 4
+        + [pltpu.VMEM((OWNERS, 2, 8, NG), jnp.float32)] * 2
+        + [
             pltpu.SMEM((KLOC * NG,), jnp.int32),
             pltpu.SemaphoreType.DMA((KLOC, 2)),
+            pltpu.SemaphoreType.DMA((3,)),
+            pltpu.SemaphoreType.DMA((NG // 256, 2)),
         ],
         compiler_params=pltpu.CompilerParams(vmem_limit_bytes=62 * 2**20),
         cost_estimate=pl.CostEstimate(flops=40 * 10**9, bytes_accessed=10 * 2**20, transcendentals=0),
@@ -307,11 +340,11 @@
     y = lax.axis_index("y")
     member = lax.axis_index(("x_lo", "z"))
 
-    energy = jnp.broadcast_to(emp_energy[:, :, None, None], (KLOC, 2, 8, 128))
-    lines = jnp.concatenate([emp_orb.reshape(KLOC, 2, 2 * LINES, 128), energy], axis=2)
+    energy = jnp.broadcast_to(emp_energy[:, :, None, None], (KLOC, 2, 2, 128))
+    lines = jnp.concatenate([emp_orb, energy], axis=3)
     own = jnp.stack([lines[1], shifted(lines[0], KA_AXES, -1)])
     emp = jnp.concatenate([own] + [shifted(own, "y", -step) for step in range(1, YS)], axis=1)
-    emp = emp.reshape(KLOC * YS * 2, 2 * LINES + 8, 128)
+    emp = emp.reshape(KLOC * YS * 2, 2, WIDE)
 
     kpoint = ka * KLOC + jnp.arange(KLOC, dtype=jnp.int32)
     wrapped = (kpoint + 1 >= KA * KLOC).astype(jnp.int32)
@@ -325,7 +358,7 @@
     owner = (y + jnp.arange(YS, dtype=jnp.int32)) % YS
     bands = owner[:, None] * (2 * MEMBERS) + member * 2 + jnp.arange(2, dtype=jnp.int32)[None, :]
     live = (bands[None] < count[target][:, None, None]).astype(jnp.float32)
-    gap = emp[:, 2 * LINES, 0].reshape(KLOC, YS, 2)[..., None] - occ_energy[:, None, None, :]
+    gap = emp[:, 0, POINTS].reshape(KLOC, YS, 2)[..., None] - occ_energy[:, None, None, :]
     strength = (scale * weights[kpoint].astype(jnp.float32))[:, None, None, None]
     factor = (strength * live[..., None] / gap).reshape(KLOC * YS, CHUNK)
 

time: 118 us -> 116 us (0.983)
  Pallas kernels: 58.1 us -> 56.8 us
    pallas_call x1, Pallas kernels: 58.1 us -> 56.8 us  [partial_rows(): pl.pallas_call(kernel, out_shape=(part, part), in_specs=[smem, smem, smem...]
  transfers between devices with their start and end apart: 17 -> 17, of which waited for: 7 -> 9; matrix products, arithmetic and copies ran while one was open for 6% -> 6% of each run, Pallas kernels for 0% -> 0%
where the time goes in v3:
time: 116 us
  Pallas kernels  56.8 us (49%)
  starting transfers between devices  29.8 us (26%)
  waiting for transfers between devices  15.3 us (13%)
  other arithmetic  7.87 us (7%)
  local copies, waits for them, and re-layouts  5.39 us (5%)
    pallas_call x1, Pallas kernels, partial_rows(): pl.pallas_call(kernel, out_shape=(part, part), in_specs=[smem, smem, smem...  56.8 us
    ppermute x17, starting transfers between devices, shifted(): lax.ppermute(value, axis, [(index, (index + by) % size) for index in rang...  29.8 us
    ppermute x17, waiting for transfers between devices, shifted(): lax.ppermute(value, axis, [(index, (index + by) % size) for index in rang...  15.3 us
  transfers between devices with their start and end apart: 17, of which 9 were waited for; matrix products, arithmetic and copies ran while one was open for 6% of the time, Pallas kernels for 0%

profile of v3, /device:TPU:0, one launch (start us, length us, event | category | flops | bytes accessed | tf_op | source)
XLA Modules:
  0.0 116.1 jit_solution(5809370661237494660)
XLA Ops:
  0.0 0.0 copy-start
  0.0 0.8 broadcast_in_dim.4
  0.8 0.9 fusion.4
  1.7 2.6 %collective-permute-start = (f32[2,2,4224]{2,1,0:T(2,128)S(1)}, f32[2,2,4224]{2,1,0:T(2,128)S(1)}, u32[]{:S(2)}, u32[]{:S(2)}) collective-permute-start(f32[2,2,4224]{2,1,0:T(2,128)S(1)} %get-tuple-element.22), channel_id=1, source_target_pairs={{0,96},{32,0},{64,32},{96,64},{1,97},{33,1},{65,33},{97,65},{2,98}... | collective-permute-start | bytes 202760 | tf_op jit(solution)/shard_map/ppermute | solution.py:334
  4.4 1.3 %reduce_sum.9 = s32[]{:T(128)} reduce(s32[8]{0:T(128)} %param.16, s32[]{:T(128)} %constant.151.clone.1), dimensions={0}, to_apply=%region_0.1 | reduce | flops 7 | bytes 40 | tf_op jit(solution)/shard_map/reduce_sum | solution.py:356
  6.4 0.1 iota_add_fusion
  6.5 1.3 %gather_fusion.1 = s32[2]{0:T(128)S(1)} fusion(s32[8]{0:T(128)} %param.16, s32[1024]{0:T(1024)S(1)} %pad_clamp_fusion), kind=kCustom, calls=%fused_computation.1 | custom fusion | bytes 24 | tf_op jit(solution)/shard_map/gather | solution.py:362
  7.8 1.3 %fusion.15.place_ref = s32[2048]{0:T(1024)} fusion(s32[2048]{0:T(1024)} %param.14), kind=kLoop, calls=%fused_computation.57 | loop fusion | flops 139264 | bytes 16384 | tf_op jit(solution)/shard_map/mul | solution.py:354
  9.1 0.6 gather_fusion
  9.8 0.1 compare_select_fusion
  9.8 0.1 add_add_fusion
  9.9 0.1 broadcast_add_fusion
  10.0 0.0 collective-permute-done
  10.0 0.1 pad_maximum_fusion.1
  10.1 1.6 %collective-permute-start.3 = (f32[2,2,2,4224]{3,2,1,0:T(2,128)S(1)}, f32[2,2,2,4224]{3,2,1,0:T(2,128)S(1)}, u32[]{:S(2)}, u32[]{:S(2)}) collective-permute-start(f32[2,2,2,4224]{3,2,1,0:T(2,128)S(1)} %pad_maximum_fusion.1), channel_id=1, source_target_pairs={{0,8},{8,16},{16,24},{24,0},{1,9},{9,17},{17,25},{25,1},{2,10},{10... | collective-permute-start | bytes 405512 | tf_op jit(solution)/shard_map/ppermute | solution.py:334
  11.7 2.9 %collective-permute-start.2 = (f32[2,2,2,4224]{3,2,1,0:T(2,128)S(1)}, f32[2,2,2,4224]{3,2,1,0:T(2,128)S(1)}, u32[]{:S(2)}, u32[]{:S(2)}) collective-permute-start(f32[2,2,2,4224]{3,2,1,0:T(2,128)S(1)} %pad_maximum_fusion.1), channel_id=1, source_target_pairs={{0,16},{8,24},{16,0},{24,8},{1,17},{9,25},{17,1},{25,9},{2,18},{10... | collective-permute-start | bytes 405512 | tf_op jit(solution)/shard_map/ppermute | solution.py:334
  14.6 1.3 %collective-permute-start.1 = (f32[2,2,2,4224]{3,2,1,0:T(2,128)S(1)}, f32[2,2,2,4224]{3,2,1,0:T(2,128)S(1)}, u32[]{:S(2)}, u32[]{:S(2)}) collective-permute-start(f32[2,2,2,4224]{3,2,1,0:T(2,128)S(1)} %pad_maximum_fusion.1), channel_id=1, source_target_pairs={{0,24},{8,0},{16,8},{24,16},{1,25},{9,1},{17,9},{25,17},{2,26},{10... | collective-permute-start | bytes 405512 | tf_op jit(solution)/shard_map/ppermute | solution.py:334
  16.0 0.1 add.349
  16.0 1.3 %copy.26 = s32[1,16,2,128]{3,1,2,0:T(8,128)} copy(s32[1,16,2,128]{3,2,1,0:T(2,128)} %bitcast.78) | data formatting | bytes 32768
  17.4 0.6 pad_add_fusion.rows_ref
  18.0 0.0 collective-permute-done.3
  18.0 1.0 collective-permute-done.2
  19.0 0.6 collective-permute-done.1
  19.6 0.2 pad_maximum_fusion
  19.9 0.2 slice_reduce_fusion
  20.1 0.1 sub.50
  20.2 0.0 copy-done.2
  20.2 0.1 subtract_divide_fusion
  20.3 0.7 div.76.fac_ref
  20.9 0.0 copy-done.1
  20.9 56.8 %shard_map.100 = (f32[16,2,8,2048]{3,2,1,0:T(8,128)}, f32[16,2,8,2048]{3,2,1,0:T(8,128)}) custom-call(s32[2048]{0:T(1024)} %fusion.15.place_ref, s32[4096]{0:T(1024)} %bitcast.79, s32[34]{0:T(128)} %pad_add_fusion.rows_ref, f32[2,64,2,4096]{3,2,1,0:T(2,128)} %occ_hbm.1, f32[16,2,4224]{2,1,0:T(2,128)} %bitcast.75, f32[8,128]{1,0:T(8,128)} %div.76.fac_ref, ...), custom_call_target="tpu_custom_call" | custom-call | flops 40000000000 | bytes 10485760 | tf_op jit(solution)/shard_map/pallas_call | solution.py:303
  77.7 0.1 collective-permute-start.4
  77.8 4.4 %collective-permute-done.4 = f32[16,2,8,2048]{3,2,1,0:T(8,128)S(1)} collective-permute-done((f32[16,2,8,2048]{3,2,1,0:T(8,128)}, f32[16,2,8,2048]{3,2,1,0:T(8,128)S(1)}, u32[]{:S(2)}, u32[]{:S(2)}) %collective-permute-start.4) | collective-permute-done | bytes 2097184 | tf_op jit(solution)/shard_map/ppermute | solution.py:334
  82.2 1.9 %add.368 = f32[16,2,8,2048]{3,2,1,0:T(8,128)S(1)} add(f32[16,2,8,2048]{3,2,1,0:T(8,128)} %get-tuple-element.7, f32[16,2,8,2048]{3,2,1,0:T(8,128)S(1)} %collective-permute-done.4) | non-fusion elementwise | flops 524288 | bytes 6291456 | tf_op jit(solution)/shard_map/add | solution.py:376
  84.1 0.1 slice_bitcast_fusion.1
  84.2 0.1 copy_bitcast_fusion
  84.3 2.5 %collective-permute-start.12 = (f32[4,8,2048]{2,1,0:T(8,128)S(1)}, f32[4,8,2048]{2,1,0:T(8,128)S(1)}, u32[]{:S(2)}, u32[]{:S(2)}) collective-permute-start(f32[4,8,2048]{2,1,0:T(8,128)S(1)} %get-tuple-element.9), channel_id=1, source_target_pairs={{0,64},{4,68},{64,0},{68,4},{1,65},{5,69},{65,1},{69,5},{2,66},{6,... | collective-permute-start | bytes 786440 | tf_op jit(solution)/shard_map/ppermute | solution.py:334
  86.8 0.6 collective-permute-start.11
  87.4 2.7 %collective-permute-start.13 = (f32[4,8,2048]{2,1,0:T(8,128)S(1)}, f32[4,8,2048]{2,1,0:T(8,128)S(1)}, u32[]{:S(2)}, u32[]{:S(2)}) collective-permute-start(f32[4,8,2048]{2,1,0:T(8,128)S(1)} %get-tuple-element.11), channel_id=1, source_target_pairs={{0,68},{4,0},{64,4},{68,64},{1,69},{5,1},{65,5},{69,65},{2,70},{6,... | collective-permute-start | bytes 786440 | tf_op jit(solution)/shard_map/ppermute | solution.py:334
  90.0 0.1 slice_bitcast_fusion.5
  90.1 3.9 %collective-permute-start.6 = (f32[4,8,2048]{2,1,0:T(8,128)S(1)}, f32[4,8,2048]{2,1,0:T(8,128)S(1)}, u32[]{:S(2)}, u32[]{:S(2)}) collective-permute-start(f32[4,8,2048]{2,1,0:T(8,128)S(1)} %get-tuple-element.12), channel_id=1, source_target_pairs={{0,2},{1,3},{2,0},{3,1},{4,6},{5,7},{6,4},{7,5},{8,10},{9,11},{10,... | collective-permute-start | bytes 786440 | tf_op jit(solution)/shard_map/ppermute | solution.py:334
  94.0 0.7 collective-permute-start.7
  94.7 0.3 collective-permute-done.12
  95.0 1.9 %collective-permute-start.5 = (f32[4,8,2048]{2,1,0:T(8,128)S(1)}, f32[4,8,2048]{2,1,0:T(8,128)S(1)}, u32[]{:S(2)}, u32[]{:S(2)}) collective-permute-start(f32[4,8,2048]{2,1,0:T(8,128)S(1)} %get-tuple-element.14), channel_id=1, source_target_pairs={{0,1},{1,2},{2,3},{3,0},{4,5},{5,6},{6,7},{7,4},{8,9},{9,10},{10,1... | collective-permute-start | bytes 786440 | tf_op jit(solution)/shard_map/ppermute | solution.py:334
  97.0 2.8 %collective-permute-done.11 = f32[4,8,2048]{2,1,0:T(8,128)S(1)} collective-permute-done((f32[4,8,2048]{2,1,0:T(8,128)S(1)}, f32[4,8,2048]{2,1,0:T(8,128)S(1)}, u32[]{:S(2)}, u32[]{:S(2)}) %collective-permute-start.11) | collective-permute-done | bytes 262176 | tf_op jit(solution)/shard_map/ppermute | solution.py:334
  99.8 0.0 collective-permute-done.13
  99.8 0.1 fusion.1
  99.9 4.0 %collective-permute-start.15 = (f32[8,2048]{1,0:T(8,128)S(1)}, f32[8,2048]{1,0:T(8,128)S(1)}, u32[]{:S(2)}, u32[]{:S(2)}) collective-permute-start(f32[8,2048]{1,0:T(8,128)S(1)} %get-tuple-element.18), channel_id=1, source_target_pairs={{0,2},{1,3},{2,0},{3,1},{4,6},{5,7},{6,4},{7,5},{8,10},{9,11},{10,... | collective-permute-start | bytes 196616 | tf_op jit(solution)/shard_map/ppermute | solution.py:334
  103.9 0.7 collective-permute-start.16
  104.6 0.0 collective-permute-done.6
  104.6 1.3 %collective-permute-start.14 = (f32[8,2048]{1,0:T(8,128)S(1)}, f32[8,2048]{1,0:T(8,128)S(1)}, u32[]{:S(2)}, u32[]{:S(2)}) collective-permute-start(f32[8,2048]{1,0:T(8,128)S(1)} %get-tuple-element.20), channel_id=1, source_target_pairs={{0,1},{1,2},{2,3},{3,0},{4,5},{5,6},{6,7},{7,4},{8,9},{9,10},{10,1... | collective-permute-start | bytes 196616 | tf_op jit(solution)/shard_map/ppermute | solution.py:334
  105.9 1.0 collective-permute-done.7
  106.9 0.0 collective-permute-done.5
  106.9 0.1 fusion.3
  107.0 0.9 collective-permute-start.9
  107.8 1.9 %collective-permute-start.10 = (f32[8,2048]{1,0:T(8,128)S(1)}, f32[8,2048]{1,0:T(8,128)S(1)}, u32[]{:S(2)}, u32[]{:S(2)}) collective-permute-start(f32[8,2048]{1,0:T(8,128)S(1)} %get-tuple-element.16), channel_id=1, source_target_pairs={{0,68},{4,0},{64,4},{68,64},{1,69},{5,1},{65,5},{69,65},{2,70},{6,... | collective-permute-start | bytes 196616 | tf_op jit(solution)/shard_map/ppermute | solution.py:334
  109.7 0.0 collective-permute-done.15
  109.7 0.1 collective-permute-start.8
  109.9 0.0 collective-permute-done.16
  109.9 0.2 collective-permute-done.14
  110.2 2.8 %collective-permute-done.9 = f32[8,2048]{1,0:T(8,128)S(1)} collective-permute-done((f32[8,2048]{1,0:T(8,128)S(1)}, f32[8,2048]{1,0:T(8,128)S(1)}, u32[]{:S(2)}, u32[]{:S(2)}) %collective-permute-start.9) | collective-permute-done | bytes 65568 | tf_op jit(solution)/shard_map/ppermute | solution.py:334
  112.9 0.0 collective-permute-done.10
  112.9 2.3 %collective-permute-done.8 = f32[8,2048]{1,0:T(8,128)S(1)} collective-permute-done((f32[8,2048]{1,0:T(8,128)S(1)}, f32[8,2048]{1,0:T(8,128)S(1)}, u32[]{:S(2)}, u32[]{:S(2)}) %collective-permute-start.8) | collective-permute-done | bytes 65568 | tf_op jit(solution)/shard_map/ppermute | solution.py:334
  115.3 0.8 maximum_bitcast_fusion
  (18 shorter events, 0.3 us)
Async XLA Ops:
  0.0 9.1 %copy-start = (s32[8]{0:T(128)S(1)}, s32[8]{0:T(128)}, u32[]{:S(2)}) copy-start(s32[8]{0:T(128)} %param.17) | copy-start | bytes 100
  0.0 20.2 %copy-start.2 = (f32[2,64]{1,0:T(2,128)S(1)}, f32[2,64]{1,0:T(2,128)}, u32[]{:S(2)}) copy-start(f32[2,64]{1,0:T(2,128)} %param.11) | copy-start | bytes 1540
  1.7 8.3 %collective-permute-start = (f32[2,2,4224]{2,1,0:T(2,128)S(1)}, f32[2,2,4224]{2,1,0:T(2,128)S(1)}, u32[]{:S(2)}, u32[]{:S(2)}) collective-permute-start(f32[2,2,4224]{2,1,0:T(2,128)S(1)} %get-tuple-element.22), channel_id=1, source_target_pairs={{0,96},{32,0},{64,32},{96,64},{1,97},{33,1},{65,33},{97,65},{2,98}... | collective-permute-start | bytes 202760 | tf_op jit(solution)/shard_map/ppermute | solution.py:334
  10.1 8.0 %collective-permute-start.3 = (f32[2,2,2,4224]{3,2,1,0:T(2,128)S(1)}, f32[2,2,2,4224]{3,2,1,0:T(2,128)S(1)}, u32[]{:S(2)}, u32[]{:S(2)}) collective-permute-start(f32[2,2,2,4224]{3,2,1,0:T(2,128)S(1)} %pad_maximum_fusion.1), channel_id=1, source_target_pairs={{0,8},{8,16},{16,24},{24,0},{1,9},{9,17},{17,25},{25,1},{2,10},{10... | collective-permute-start | bytes 405512 | tf_op jit(solution)/shard_map/ppermute | solution.py:334
  11.7 7.3 %collective-permute-start.2 = (f32[2,2,2,4224]{3,2,1,0:T(2,128)S(1)}, f32[2,2,2,4224]{3,2,1,0:T(2,128)S(1)}, u32[]{:S(2)}, u32[]{:S(2)}) collective-permute-start(f32[2,2,2,4224]{3,2,1,0:T(2,128)S(1)} %pad_maximum_fusion.1), channel_id=1, source_target_pairs={{0,16},{8,24},{16,0},{24,8},{1,17},{9,25},{17,1},{25,9},{2,18},{10... | collective-permute-start | bytes 405512 | tf_op jit(solution)/shard_map/ppermute | solution.py:334
  14.6 5.0 %collective-permute-start.1 = (f32[2,2,2,4224]{3,2,1,0:T(2,128)S(1)}, f32[2,2,2,4224]{3,2,1,0:T(2,128)S(1)}, u32[]{:S(2)}, u32[]{:S(2)}) collective-permute-start(f32[2,2,2,4224]{3,2,1,0:T(2,128)S(1)} %pad_maximum_fusion.1), channel_id=1, source_target_pairs={{0,24},{8,0},{16,8},{24,16},{1,25},{9,1},{17,9},{25,17},{2,26},{10... | collective-permute-start | bytes 405512 | tf_op jit(solution)/shard_map/ppermute | solution.py:334
  19.9 1.1 copy-start.1
  77.7 4.5 %collective-permute-start.4 = (f32[16,2,8,2048]{3,2,1,0:T(8,128)}, f32[16,2,8,2048]{3,2,1,0:T(8,128)S(1)}, u32[]{:S(2)}, u32[]{:S(2)}) collective-permute-start(f32[16,2,8,2048]{3,2,1,0:T(8,128)} %get-tuple-element.8), channel_id=1, source_target_pairs={{0,32},{32,0},{1,33},{33,1},{2,34},{34,2},{3,35},{35,3},{4,36},{36... | collective-permute-start | bytes 6291464 | tf_op jit(solution)/shard_map/ppermute | solution.py:334
  84.3 10.8 %collective-permute-start.12 = (f32[4,8,2048]{2,1,0:T(8,128)S(1)}, f32[4,8,2048]{2,1,0:T(8,128)S(1)}, u32[]{:S(2)}, u32[]{:S(2)}) collective-permute-start(f32[4,8,2048]{2,1,0:T(8,128)S(1)} %get-tuple-element.9), channel_id=1, source_target_pairs={{0,64},{4,68},{64,0},{68,4},{1,65},{5,69},{65,1},{69,5},{2,66},{6,... | collective-permute-start | bytes 786440 | tf_op jit(solution)/shard_map/ppermute | solution.py:334
  86.8 13.0 %collective-permute-start.11 = (f32[4,8,2048]{2,1,0:T(8,128)S(1)}, f32[4,8,2048]{2,1,0:T(8,128)S(1)}, u32[]{:S(2)}, u32[]{:S(2)}) collective-permute-start(f32[4,8,2048]{2,1,0:T(8,128)S(1)} %get-tuple-element.10), channel_id=1, source_target_pairs={{0,4},{4,64},{64,68},{68,0},{1,5},{5,65},{65,69},{69,1},{2,6},{6,6... | collective-permute-start | bytes 786440 | tf_op jit(solution)/shard_map/ppermute | solution.py:334
  87.4 12.5 %collective-permute-start.13 = (f32[4,8,2048]{2,1,0:T(8,128)S(1)}, f32[4,8,2048]{2,1,0:T(8,128)S(1)}, u32[]{:S(2)}, u32[]{:S(2)}) collective-permute-start(f32[4,8,2048]{2,1,0:T(8,128)S(1)} %get-tuple-element.11), channel_id=1, source_target_pairs={{0,68},{4,0},{64,4},{68,64},{1,69},{5,1},{65,5},{69,65},{2,70},{6,... | collective-permute-start | bytes 786440 | tf_op jit(solution)/shard_map/ppermute | solution.py:334
  90.1 14.5 %collective-permute-start.6 = (f32[4,8,2048]{2,1,0:T(8,128)S(1)}, f32[4,8,2048]{2,1,0:T(8,128)S(1)}, u32[]{:S(2)}, u32[]{:S(2)}) collective-permute-start(f32[4,8,2048]{2,1,0:T(8,128)S(1)} %get-tuple-element.12), channel_id=1, source_target_pairs={{0,2},{1,3},{2,0},{3,1},{4,6},{5,7},{6,4},{7,5},{8,10},{9,11},{10,... | collective-permute-start | bytes 786440 | tf_op jit(solution)/shard_map/ppermute | solution.py:334
  94.0 12.8 %collective-permute-start.7 = (f32[4,8,2048]{2,1,0:T(8,128)S(1)}, f32[4,8,2048]{2,1,0:T(8,128)S(1)}, u32[]{:S(2)}, u32[]{:S(2)}) collective-permute-start(f32[4,8,2048]{2,1,0:T(8,128)S(1)} %get-tuple-element.13), channel_id=1, source_target_pairs={{0,3},{1,0},{2,1},{3,2},{4,7},{5,4},{6,5},{7,6},{8,11},{9,8},{10,9... | collective-permute-start | bytes 786440 | tf_op jit(solution)/shard_map/ppermute | solution.py:334
  95.0 11.8 %collective-permute-start.5 = (f32[4,8,2048]{2,1,0:T(8,128)S(1)}, f32[4,8,2048]{2,1,0:T(8,128)S(1)}, u32[]{:S(2)}, u32[]{:S(2)}) collective-permute-start(f32[4,8,2048]{2,1,0:T(8,128)S(1)} %get-tuple-element.14), channel_id=1, source_target_pairs={{0,1},{1,2},{2,3},{3,0},{4,5},{5,6},{6,7},{7,4},{8,9},{9,10},{10,1... | collective-permute-start | bytes 786440 | tf_op jit(solution)/shard_map/ppermute | solution.py:334
  99.9 9.8 %collective-permute-start.15 = (f32[8,2048]{1,0:T(8,128)S(1)}, f32[8,2048]{1,0:T(8,128)S(1)}, u32[]{:S(2)}, u32[]{:S(2)}) collective-permute-start(f32[8,2048]{1,0:T(8,128)S(1)} %get-tuple-element.18), channel_id=1, source_target_pairs={{0,2},{1,3},{2,0},{3,1},{4,6},{5,7},{6,4},{7,5},{8,10},{9,11},{10,... | collective-permute-start | bytes 196616 | tf_op jit(solution)/shard_map/ppermute | solution.py:334
  103.9 6.0 %collective-permute-start.16 = (f32[8,2048]{1,0:T(8,128)S(1)}, f32[8,2048]{1,0:T(8,128)S(1)}, u32[]{:S(2)}, u32[]{:S(2)}) collective-permute-start(f32[8,2048]{1,0:T(8,128)S(1)} %get-tuple-element.19), channel_id=1, source_target_pairs={{0,3},{1,0},{2,1},{3,2},{4,7},{5,4},{6,5},{7,6},{8,11},{9,8},{10,9... | collective-permute-start | bytes 196616 | tf_op jit(solution)/shard_map/ppermute | solution.py:334
  104.6 5.5 %collective-permute-start.14 = (f32[8,2048]{1,0:T(8,128)S(1)}, f32[8,2048]{1,0:T(8,128)S(1)}, u32[]{:S(2)}, u32[]{:S(2)}) collective-permute-start(f32[8,2048]{1,0:T(8,128)S(1)} %get-tuple-element.20), channel_id=1, source_target_pairs={{0,1},{1,2},{2,3},{3,0},{4,5},{5,6},{6,7},{7,4},{8,9},{9,10},{10,1... | collective-permute-start | bytes 196616 | tf_op jit(solution)/shard_map/ppermute | solution.py:334
  107.0 6.0 %collective-permute-start.9 = (f32[8,2048]{1,0:T(8,128)S(1)}, f32[8,2048]{1,0:T(8,128)S(1)}, u32[]{:S(2)}, u32[]{:S(2)}) collective-permute-start(f32[8,2048]{1,0:T(8,128)S(1)} %get-tuple-element.15), channel_id=1, source_target_pairs={{0,64},{4,68},{64,0},{68,4},{1,65},{5,69},{65,1},{69,5},{2,66},{6,... | collective-permute-start | bytes 196616 | tf_op jit(solution)/shard_map/ppermute | solution.py:334
  107.8 5.1 %collective-permute-start.10 = (f32[8,2048]{1,0:T(8,128)S(1)}, f32[8,2048]{1,0:T(8,128)S(1)}, u32[]{:S(2)}, u32[]{:S(2)}) collective-permute-start(f32[8,2048]{1,0:T(8,128)S(1)} %get-tuple-element.16), channel_id=1, source_target_pairs={{0,68},{4,0},{64,4},{68,64},{1,69},{5,1},{65,5},{69,65},{2,70},{6,... | collective-permute-start | bytes 196616 | tf_op jit(solution)/shard_map/ppermute | solution.py:334
  109.7 5.5 %collective-permute-start.8 = (f32[8,2048]{1,0:T(8,128)S(1)}, f32[8,2048]{1,0:T(8,128)S(1)}, u32[]{:S(2)}, u32[]{:S(2)}) collective-permute-start(f32[8,2048]{1,0:T(8,128)S(1)} %get-tuple-element.17), channel_id=1, source_target_pairs={{0,4},{4,64},{64,68},{68,0},{1,5},{5,65},{65,69},{69,1},{2,6},{6,6... | collective-permute-start | bytes 196616 | tf_op jit(solution)/shard_map/ppermute | solution.py:334

commit v4 on v3

--- a/solution.py
+++ b/solution.py
@@ -81,24 +81,28 @@
 
 
 def kernel(
-    place_ref, sym_ref, rows_ref, occ_hbm, emp_hbm, fac_ref, whi_hbm, wlo_hbm, near_hbm, far_hbm,
+    place_ref, sym_ref, rows_ref, occ_hbm, own_hbm, one_hbm, two_hbm, three_hbm, weight_ref, level_ref, whi_hbm, wlo_hbm, near_hbm, far_hbm,
     occ_ref, emp_ref, whi_ref, wlo_ref, mid_ref, xhi0_ref, xlo0_ref, xhi1_ref, xlo1_ref, spec_ref, left_ref,
-    pick0_ref, pick1_ref, pick2_ref, pick3_ref, bhi0_ref, blo0_ref, bhi1_ref, blo1_ref,
-    ahi0_ref, alo0_ref, ahi1_ref, alo1_ref, near_ref, far_ref, idx_ref, occ_sems, in_sems, out_sems,
+    pick0_ref, pick1_ref, pick2_ref, pick3_ref, pick4_ref, pick5_ref, pick6_ref, pick7_ref, bhi0_ref, blo0_ref, bhi1_ref, blo1_ref,
+    ahi0_ref, alo0_ref, ahi1_ref, alo1_ref, near_ref, far_ref, fac_ref, idx_ref, occ_sems, in_sems, out_sems,
 ):
     slots = ((xhi0_ref, xlo0_ref), (xhi1_ref, xlo1_ref))
-    picks = (pick0_ref, pick1_ref, pick2_ref, pick3_ref)
+    picks = (pick0_ref, pick1_ref, pick2_ref, pick3_ref, pick4_ref, pick5_ref, pick6_ref, pick7_ref)
     rights = ((bhi0_ref, blo0_ref), (bhi1_ref, blo1_ref))
     lefts = ((ahi0_ref, alo0_ref), (ahi1_ref, alo1_ref))
     copies = [
         [pltpu.make_async_copy(occ_hbm.at[k, :, part], occ_ref.at[k, part], occ_sems.at[k, part]) for part in range(2)]
         for k in range(KLOC)
     ]
-    others = [
+    lines = [
+        pltpu.make_async_copy(source, emp_ref.at[:, step], in_sems.at[2 + step])
+        for step, source in enumerate((own_hbm, one_hbm, two_hbm, three_hbm))
+    ]
+    others = lines + [
         pltpu.make_async_copy(source, target, in_sems.at[which])
-        for which, (source, target) in enumerate(((emp_hbm, emp_ref), (whi_hbm, whi_ref), (wlo_hbm, wlo_ref)))
+        for which, (source, target) in enumerate(((whi_hbm, whi_ref), (wlo_hbm, wlo_ref)))
     ]
-    for copy in [others[0]] + copies[0] + others[1:] + copies[1]:
+    for copy in lines + copies[0] + others[YS:] + copies[1]:
         copy.start()
 
     def pairs(step, block, slot):
@@ -106,14 +110,14 @@
         k = step // YS
         band = block // (VB // 16)
         start = pl.multiple_of((block % (VB // 16)) * 16, 16)
-        line = step * 2 + band
+        chunk = step % YS
 
         def pair(a, half):
             base = a * PLANE + half * HALF
             o_re = occ_ref[k, 0, pl.ds(start, 16), pl.ds(base, HALF)]
             o_im = occ_ref[k, 1, pl.ds(start, 16), pl.ds(base, HALF)]
-            e_re = emp_ref[line, 0:1, pl.ds(base, HALF)]
-            e_im = emp_ref[line, 1:2, pl.ds(base, HALF)]
+            e_re = emp_ref[k, chunk, band, 0:1, pl.ds(base, HALF)]
+            e_im = emp_ref[k, chunk, band, 1:2, pl.ds(base, HALF)]
             return o_re * e_re + o_im * e_im, o_re * e_im - o_im * e_re
 
         for a0 in range(4):
@@ -171,13 +175,18 @@
 
     def gather_left(k):
         ahi_ref, alo_ref = lefts[k]
+        lane = lax.broadcasted_iota(jnp.int32, (1, CHUNK), 1)
+        for chunk in range(YS):
+            levels = [emp_ref[k, chunk, band, 0:1, POINTS : POINTS + CHUNK] for band in range(2)]
+            gap = jnp.where(lane < VB, levels[0], levels[1]) - level_ref[k : k + 1, :]
+            fac_ref[chunk : chunk + 1, :] = weight_ref[k * YS + chunk : k * YS + chunk + 1, :] / gap
 
         def left(step, carry):
             row = pl.multiple_of(step * 16, 16)
             for lane in range(16):
                 pick(k, rows_ref[step * 2 + lane // 8] + lane % 8, left_ref, lane * 8)
             for chunk in range(YS):
-                factor = fac_ref[k * YS + chunk : k * YS + chunk + 1, :]
+                factor = fac_ref[chunk : chunk + 1, :]
                 re = left_ref[pl.ds(2 * chunk, 16, stride=8), :] * factor
                 im = left_ref[pl.ds(2 * chunk + 1, 16, stride=8), :] * factor
                 rhi, rlo = split(re)
@@ -274,7 +283,7 @@
             for which, (source, target) in enumerate(((near_ref, near_hbm), (far_ref, far_hbm)))
         ]
 
-    def one_column(tile, carry):
+    def one_column(tile):
         out = product(0, places_of(tile)) + product(1, places_of(tile))
         for part in range(2):
             for to in range(OWNERS):
@@ -283,6 +292,10 @@
                 far_ref[to, part, :, places_of(tile)] = out[row + ROWS // 2 : row + ROWS // 2 + 8]
         for copy in sent(tile):
             copy.start()
+
+    def columns_of(turn, carry):
+        for part in range(2):
+            one_column(turn * 2 + part)
         return carry
 
     def done(tile, carry):
@@ -290,11 +303,11 @@
             copy.wait()
         return carry
 
-    lax.fori_loop(0, NG // 256, one_column, 0)
+    lax.fori_loop(0, NG // 256 // 2, columns_of, 0)
     lax.fori_loop(0, NG // 256, done, 0)
 
 
-def partial_rows(places, sym_map, rows, occ, emp, factor):
+def partial_rows(places, sym_map, rows, occ, emp, strength, level):
     whi, wlo = plane_matrices()
     vmem = pl.BlockSpec(memory_space=pltpu.VMEM)
     smem = pl.BlockSpec(memory_space=pltpu.SMEM)
@@ -303,30 +316,31 @@
     return pl.pallas_call(
         kernel,
         out_shape=(part, part),
-        in_specs=[smem, smem, smem, hbm, hbm, vmem, hbm, hbm],
+        in_specs=[smem, smem, smem] + [hbm] * 5 + [vmem, vmem, hbm, hbm],
         out_specs=(hbm, hbm),
         scratch_shapes=[
             pltpu.VMEM((KLOC, 2, VB, POINTS), jnp.float32),
-            pltpu.VMEM((KLOC * YS * 2, 2, WIDE), jnp.float32),
+            pltpu.VMEM((KLOC, YS, 2, 2, WIDE), jnp.float32),
             pltpu.VMEM((2, PLANE, PLANE), jnp.bfloat16),
             pltpu.VMEM((2, PLANE, PLANE), jnp.bfloat16),
             pltpu.VMEM((2, 4, 4, 2, 16, HALF), jnp.float32),
         ]
         + [pltpu.VMEM((2, GRID * CHUNK, PLANE), jnp.bfloat16)] * 4
         + [pltpu.VMEM((POINTS * 8, CHUNK), jnp.float32)]
-        + [pltpu.VMEM((16 * 8, CHUNK), jnp.float32)] * 5
+        + [pltpu.VMEM((16 * 8, CHUNK), jnp.float32)] * 9
         + [pltpu.VMEM((NG, DEPTH), jnp.bfloat16)] * 4
         + [pltpu.VMEM((2 * ROWS, DEPTH), jnp.bfloat16)] * 4
         + [pltpu.VMEM((OWNERS, 2, 8, NG), jnp.float32)] * 2
         + [
+            pltpu.VMEM((8, CHUNK), jnp.float32),
             pltpu.SMEM((KLOC * NG,), jnp.int32),
             pltpu.SemaphoreType.DMA((KLOC, 2)),
-            pltpu.SemaphoreType.DMA((3,)),
+            pltpu.SemaphoreType.DMA((2 + YS,)),
             pltpu.SemaphoreType.DMA((NG // 256, 2)),
         ],
         compiler_params=pltpu.CompilerParams(vmem_limit_bytes=62 * 2**20),
         cost_estimate=pl.CostEstimate(flops=40 * 10**9, bytes_accessed=10 * 2**20, transcendentals=0),
-    )(places, sym_map, rows, occ, emp, factor, jnp.asarray(whi), jnp.asarray(wlo))
+    )(places, sym_map, rows, occ, *emp, strength, level, jnp.asarray(whi), jnp.asarray(wlo))
 
 
 def shifted(value, axis, by):
@@ -340,11 +354,11 @@
     y = lax.axis_index("y")
     member = lax.axis_index(("x_lo", "z"))
 
-    energy = jnp.broadcast_to(emp_energy[:, :, None, None], (KLOC, 2, 2, 128))
-    lines = jnp.concatenate([emp_orb, energy], axis=3)
+    spread = jnp.pad(emp_orb, ((0, 0), (0, 0), (0, 0), (0, WIDE - POINTS)))
+    lane = lax.broadcasted_iota(jnp.int32, spread.shape, 3)
+    lines = jnp.where(lane < POINTS, spread, emp_energy[:, :, None, None])
     own = jnp.stack([lines[1], shifted(lines[0], KA_AXES, -1)])
-    emp = jnp.concatenate([own] + [shifted(own, "y", -step) for step in range(1, YS)], axis=1)
-    emp = emp.reshape(KLOC * YS * 2, 2, WIDE)
+    emp = [own] + [shifted(own, "y", -step) for step in range(1, YS)]
 
     kpoint = ka * KLOC + jnp.arange(KLOC, dtype=jnp.int32)
     wrapped = (kpoint + 1 >= KA * KLOC).astype(jnp.int32)
@@ -358,9 +372,9 @@
     owner = (y + jnp.arange(YS, dtype=jnp.int32)) % YS
     bands = owner[:, None] * (2 * MEMBERS) + member * 2 + jnp.arange(2, dtype=jnp.int32)[None, :]
     live = (bands[None] < count[target][:, None, None]).astype(jnp.float32)
-    gap = emp[:, 0, POINTS].reshape(KLOC, YS, 2)[..., None] - occ_energy[:, None, None, :]
     strength = (scale * weights[kpoint].astype(jnp.float32))[:, None, None, None]
-    factor = (strength * live[..., None] / gap).reshape(KLOC * YS, CHUNK)
+    strength = jnp.broadcast_to(strength * live[..., None], (KLOC, YS, 2, VB)).reshape(KLOC * YS, CHUNK)
+    level = jnp.concatenate([occ_energy, occ_energy], axis=1)
 
     near_core = jnp.arange(2, dtype=jnp.int32)[:, None, None]
     x = lax.axis_index(("x_hi", "x_lo"))
@@ -371,7 +385,7 @@
     rows = (to_ka * 256 + y * 64 + (to_x % 2) * 32 + to_z * 8).reshape(32)
     rows = jnp.concatenate([rows, wrapped * (PLANE * 8)])
 
-    near, far = partial_rows(places, sym_map.reshape(KLOC * NG), rows.astype(jnp.int32), occ_orb, emp, factor)
+    near, far = partial_rows(places, sym_map.reshape(KLOC * NG), rows.astype(jnp.int32), occ_orb, emp, strength, level)
 
     both = near + shifted(far, "core", 1)
     both = both.reshape(4, 4, 2, 8, NG)

time: 116 us -> 115 us (level)
  waiting for transfers between devices: 15.3 us -> 12.9 us
    ppermute x17, waiting for transfers between devices: 15.3 us -> 12.9 us  [shifted(): lax.ppermute(value, axis, [(index, (index + by) % size) for index in rang...]
  transfers between devices with their start and end apart: 17 -> 17, of which waited for: 9 -> 6; matrix products, arithmetic and copies ran while one was open for 6% -> 8% of each run, Pallas kernels for 0% -> 0%
where the time goes in v4:
time: 115 us; the launch traced here: 114 us
  Pallas kernels  56.1 us (49%)
  starting transfers between devices  30.3 us (26%)
  waiting for transfers between devices  12.9 us (11%)
  other arithmetic  8.98 us (8%)
  local copies, waits for them, and re-layouts  5.14 us (4%)
    pallas_call x1, Pallas kernels, partial_rows(): pl.pallas_call(kernel, out_shape=(part, part), in_specs=[smem, smem, smem...  56.1 us
    ppermute x17, starting transfers between devices, shifted(): lax.ppermute(value, axis, [(index, (index + by) % size) for index in rang...  30.3 us
    ppermute x17, waiting for transfers between devices, shifted(): lax.ppermute(value, axis, [(index, (index + by) % size) for index in rang...  12.9 us
  transfers between devices with their start and end apart: 17, of which 6 were waited for; matrix products, arithmetic and copies ran while one was open for 8% of the time, Pallas kernels for 0%

profile of v4, /device:TPU:0, one launch (start us, length us, event | category | flops | bytes accessed | tf_op | source)
XLA Modules:
  0.0 114.3 jit_solution(13345665276304149010)
XLA Ops:
  0.0 0.0 copy-start
  0.0 1.0 pad_select_fusion
  1.1 2.6 %collective-permute-start = (f32[2,2,4224]{2,1,0:T(2,128)S(1)}, f32[2,2,4224]{2,1,0:T(2,128)S(1)}, u32[]{:S(2)}, u32[]{:S(2)}) collective-permute-start(f32[2,2,4224]{2,1,0:T(2,128)S(1)} %get-tuple-element.22), channel_id=1, source_target_pairs={{0,96},{32,0},{64,32},{96,64},{1,97},{33,1},{65,33},{97,65},{2,98}... | collective-permute-start | bytes 202760 | tf_op jit(solution)/shard_map/ppermute | solution.py:348
  3.7 1.3 %reduce_sum.9 = s32[]{:T(128)} reduce(s32[8]{0:T(128)} %param.16, s32[]{:T(128)} %constant.153.clone.1), dimensions={0}, to_apply=%region_0.1 | reduce | flops 7 | bytes 40 | tf_op jit(solution)/shard_map/reduce_sum | solution.py:370
  5.7 0.1 iota_add_fusion
  5.8 0.1 add_add_fusion
  5.9 0.1 broadcast_add_fusion
  6.0 0.1 add.351
  6.1 1.3 %gather_fusion.1 = s32[2]{0:T(128)S(1)} fusion(s32[8]{0:T(128)} %param.16, s32[1024]{0:T(1024)S(1)} %pad_clamp_fusion), kind=kCustom, calls=%fused_computation.1 | custom fusion | bytes 24 | tf_op jit(solution)/shard_map/gather | solution.py:375
  7.4 1.3 %fusion.13.place_ref = s32[2048]{0:T(1024)} fusion(s32[2048]{0:T(1024)} %param.14), kind=kLoop, calls=%fused_computation.54 | loop fusion | flops 139264 | bytes 16384 | tf_op jit(solution)/shard_map/mul | solution.py:368
  8.7 0.0 copy-done
  8.7 0.6 gather_fusion
  9.3 0.1 compare_select_fusion
  9.4 0.0 collective-permute-done
  9.4 0.1 pad_maximum_fusion.own_hbm
  9.5 1.6 %collective-permute-start.3 = (f32[2,2,2,4224]{3,2,1,0:T(2,128)S(1)}, f32[2,2,2,4224]{3,2,1,0:T(2,128)S(1)}, u32[]{:S(2)}, u32[]{:S(2)}) collective-permute-start(f32[2,2,2,4224]{3,2,1,0:T(2,128)S(1)} %pad_maximum_fusion.own_hbm), channel_id=1, source_target_pairs={{0,8},{8,16},{16,24},{24,0},{1,9},{9,17},{17,25},{25,1},{2,10},{10... | collective-permute-start | bytes 405512 | tf_op jit(solution)/shard_map/ppermute | solution.py:348
  11.1 2.9 %collective-permute-start.2 = (f32[2,2,2,4224]{3,2,1,0:T(2,128)S(1)}, f32[2,2,2,4224]{3,2,1,0:T(2,128)S(1)}, u32[]{:S(2)}, u32[]{:S(2)}) collective-permute-start(f32[2,2,2,4224]{3,2,1,0:T(2,128)S(1)} %pad_maximum_fusion.own_hbm), channel_id=1, source_target_pairs={{0,16},{8,24},{16,0},{24,8},{1,17},{9,25},{17,1},{25,9},{2,18},{10... | collective-permute-start | bytes 405512 | tf_op jit(solution)/shard_map/ppermute | solution.py:348
  14.1 1.3 %collective-permute-start.1 = (f32[2,2,2,4224]{3,2,1,0:T(2,128)S(1)}, f32[2,2,2,4224]{3,2,1,0:T(2,128)S(1)}, u32[]{:S(2)}, u32[]{:S(2)}) collective-permute-start(f32[2,2,2,4224]{3,2,1,0:T(2,128)S(1)} %pad_maximum_fusion.own_hbm), channel_id=1, source_target_pairs={{0,24},{8,0},{16,8},{24,16},{1,25},{9,1},{17,9},{25,17},{2,26},{10... | collective-permute-start | bytes 405512 | tf_op jit(solution)/shard_map/ppermute | solution.py:348
  15.4 0.6 pad_add_fusion.rows_ref
  16.0 0.1 broadcast_in_dim.13
  16.0 0.7 reshape.284.weight_ref
  16.7 1.3 %copy.26 = s32[1,16,2,128]{3,1,2,0:T(8,128)} copy(s32[1,16,2,128]{3,2,1,0:T(2,128)} %bitcast.74) | data formatting | bytes 32768
  18.0 1.4 %pad_maximum_fusion.1.level_ref = f32[2,128]{1,0:T(2,128)} fusion(f32[2,64]{1,0:T(2,128)} %param.11), kind=kLoop, calls=%fused_computation.90 | loop fusion | flops 256 | bytes 1536 | tf_op jit(solution)/shard_map/concatenate | solution.py:377
  19.5 0.0 collective-permute-done.3.three_hbm
  19.5 0.0 collective-permute-done.2.two_hbm
  19.5 0.0 copy-start.3
  19.5 0.0 collective-permute-done.1.one_hbm
  19.5 0.6 copy-done.2
  20.1 0.1 copy-done.3
  20.2 0.1 copy-done.4
  20.2 56.1 %shard_map.100 = (f32[16,2,8,2048]{3,2,1,0:T(8,128)}, f32[16,2,8,2048]{3,2,1,0:T(8,128)}) custom-call(s32[2048]{0:T(1024)} %fusion.13.place_ref, s32[4096]{0:T(1024)} %bitcast.75, s32[34]{0:T(128)} %pad_add_fusion.rows_ref, f32[2,64,2,4096]{3,2,1,0:T(2,128)} %occ_hbm.1, f32[2,2,2,4224]{3,2,1,0:T(2,128)} %copy-done.1, f32[2,2,2,4224]{3,2,1,0:T(2,128)} %copy-done.4, ...), custom_call_target="tpu_custom_call" | custom-call | flops 40000000000 | bytes 10485760 | tf_op jit(solution)/shard_map/pallas_call | solution.py:316
  76.3 0.1 collective-permute-start.4
  76.4 4.4 %collective-permute-done.4 = f32[16,2,8,2048]{3,2,1,0:T(8,128)S(1)} collective-permute-done((f32[16,2,8,2048]{3,2,1,0:T(8,128)}, f32[16,2,8,2048]{3,2,1,0:T(8,128)S(1)}, u32[]{:S(2)}, u32[]{:S(2)}) %collective-permute-start.4) | collective-permute-done | bytes 2097184 | tf_op jit(solution)/shard_map/ppermute | solution.py:348
  80.8 1.9 %add.370 = f32[16,2,8,2048]{3,2,1,0:T(8,128)S(1)} add(f32[16,2,8,2048]{3,2,1,0:T(8,128)} %get-tuple-element.7, f32[16,2,8,2048]{3,2,1,0:T(8,128)S(1)} %collective-permute-done.4) | non-fusion elementwise | flops 524288 | bytes 6291456 | tf_op jit(solution)/shard_map/add | solution.py:390
  82.7 0.1 slice_bitcast_fusion.1
  82.8 0.1 copy_bitcast_fusion
  82.9 2.0 %collective-permute-start.12 = (f32[4,8,2048]{2,1,0:T(8,128)S(1)}, f32[4,8,2048]{2,1,0:T(8,128)S(1)}, u32[]{:S(2)}, u32[]{:S(2)}) collective-permute-start(f32[4,8,2048]{2,1,0:T(8,128)S(1)} %get-tuple-element.9), channel_id=1, source_target_pairs={{0,64},{4,68},{64,0},{68,4},{1,65},{5,69},{65,1},{69,5},{2,66},{6,... | collective-permute-start | bytes 786440 | tf_op jit(solution)/shard_map/ppermute | solution.py:348
  84.9 0.6 collective-permute-start.11
  85.5 2.6 %collective-permute-start.13 = (f32[4,8,2048]{2,1,0:T(8,128)S(1)}, f32[4,8,2048]{2,1,0:T(8,128)S(1)}, u32[]{:S(2)}, u32[]{:S(2)}) collective-permute-start(f32[4,8,2048]{2,1,0:T(8,128)S(1)} %get-tuple-element.11), channel_id=1, source_target_pairs={{0,68},{4,0},{64,4},{68,64},{1,69},{5,1},{65,5},{69,65},{2,70},{6,... | collective-permute-start | bytes 786440 | tf_op jit(solution)/shard_map/ppermute | solution.py:348
  88.1 0.1 slice_bitcast_fusion.5
  88.2 4.0 %collective-permute-start.6 = (f32[4,8,2048]{2,1,0:T(8,128)S(1)}, f32[4,8,2048]{2,1,0:T(8,128)S(1)}, u32[]{:S(2)}, u32[]{:S(2)}) collective-permute-start(f32[4,8,2048]{2,1,0:T(8,128)S(1)} %get-tuple-element.12), channel_id=1, source_target_pairs={{0,2},{1,3},{2,0},{3,1},{4,6},{5,7},{6,4},{7,5},{8,10},{9,11},{10,... | collective-permute-start | bytes 786440 | tf_op jit(solution)/shard_map/ppermute | solution.py:348
  92.2 0.7 collective-permute-start.7
  92.9 0.8 collective-permute-done.12
  93.7 1.9 %collective-permute-start.5 = (f32[4,8,2048]{2,1,0:T(8,128)S(1)}, f32[4,8,2048]{2,1,0:T(8,128)S(1)}, u32[]{:S(2)}, u32[]{:S(2)}) collective-permute-start(f32[4,8,2048]{2,1,0:T(8,128)S(1)} %get-tuple-element.14), channel_id=1, source_target_pairs={{0,1},{1,2},{2,3},{3,0},{4,5},{5,6},{6,7},{7,4},{8,9},{9,10},{10,1... | collective-permute-start | bytes 786440 | tf_op jit(solution)/shard_map/ppermute | solution.py:348
  95.6 2.8 %collective-permute-done.11 = f32[4,8,2048]{2,1,0:T(8,128)S(1)} collective-permute-done((f32[4,8,2048]{2,1,0:T(8,128)S(1)}, f32[4,8,2048]{2,1,0:T(8,128)S(1)}, u32[]{:S(2)}, u32[]{:S(2)}) %collective-permute-start.11) | collective-permute-done | bytes 262176 | tf_op jit(solution)/shard_map/ppermute | solution.py:348
  98.4 0.0 collective-permute-done.13
  98.4 0.1 fusion.1
  98.5 4.0 %collective-permute-start.15 = (f32[8,2048]{1,0:T(8,128)S(1)}, f32[8,2048]{1,0:T(8,128)S(1)}, u32[]{:S(2)}, u32[]{:S(2)}) collective-permute-start(f32[8,2048]{1,0:T(8,128)S(1)} %get-tuple-element.18), channel_id=1, source_target_pairs={{0,2},{1,3},{2,0},{3,1},{4,6},{5,7},{6,4},{7,5},{8,10},{9,11},{10,... | collective-permute-start | bytes 196616 | tf_op jit(solution)/shard_map/ppermute | solution.py:348
  102.5 0.7 collective-permute-start.16
  103.2 0.0 collective-permute-done.6
  103.2 1.3 %collective-permute-start.14 = (f32[8,2048]{1,0:T(8,128)S(1)}, f32[8,2048]{1,0:T(8,128)S(1)}, u32[]{:S(2)}, u32[]{:S(2)}) collective-permute-start(f32[8,2048]{1,0:T(8,128)S(1)} %get-tuple-element.20), channel_id=1, source_target_pairs={{0,1},{1,2},{2,3},{3,0},{4,5},{5,6},{6,7},{7,4},{8,9},{9,10},{10,1... | collective-permute-start | bytes 196616 | tf_op jit(solution)/shard_map/ppermute | solution.py:348
  104.5 0.0 collective-permute-done.7
  104.5 0.0 collective-permute-done.5
  104.5 0.1 fusion.3
  104.6 1.8 %collective-permute-start.9 = (f32[8,2048]{1,0:T(8,128)S(1)}, f32[8,2048]{1,0:T(8,128)S(1)}, u32[]{:S(2)}, u32[]{:S(2)}) collective-permute-start(f32[8,2048]{1,0:T(8,128)S(1)} %get-tuple-element.15), channel_id=1, source_target_pairs={{0,64},{4,68},{64,0},{68,4},{1,65},{5,69},{65,1},{69,5},{2,66},{6,... | collective-permute-start | bytes 196616 | tf_op jit(solution)/shard_map/ppermute | solution.py:348
  106.5 1.5 %collective-permute-start.10 = (f32[8,2048]{1,0:T(8,128)S(1)}, f32[8,2048]{1,0:T(8,128)S(1)}, u32[]{:S(2)}, u32[]{:S(2)}) collective-permute-start(f32[8,2048]{1,0:T(8,128)S(1)} %get-tuple-element.16), channel_id=1, source_target_pairs={{0,68},{4,0},{64,4},{68,64},{1,69},{5,1},{65,5},{69,65},{2,70},{6,... | collective-permute-start | bytes 196616 | tf_op jit(solution)/shard_map/ppermute | solution.py:348
  108.0 0.0 collective-permute-done.15
  108.0 0.5 collective-permute-start.8
  108.5 0.0 collective-permute-done.16
  108.5 0.2 collective-permute-done.14
  108.8 2.2 %collective-permute-done.9 = f32[8,2048]{1,0:T(8,128)S(1)} collective-permute-done((f32[8,2048]{1,0:T(8,128)S(1)}, f32[8,2048]{1,0:T(8,128)S(1)}, u32[]{:S(2)}, u32[]{:S(2)}) %collective-permute-start.9) | collective-permute-done | bytes 65568 | tf_op jit(solution)/shard_map/ppermute | solution.py:348
  111.0 0.0 collective-permute-done.10
  111.0 2.5 %collective-permute-done.8 = f32[8,2048]{1,0:T(8,128)S(1)} collective-permute-done((f32[8,2048]{1,0:T(8,128)S(1)}, f32[8,2048]{1,0:T(8,128)S(1)}, u32[]{:S(2)}, u32[]{:S(2)}) %collective-permute-start.8) | collective-permute-done | bytes 65568 | tf_op jit(solution)/shard_map/ppermute | solution.py:348
  113.5 0.8 maximum_bitcast_fusion
  (21 shorter events, 0.3 us)
Async XLA Ops:
  0.0 8.7 %copy-start = (s32[8]{0:T(128)S(1)}, s32[8]{0:T(128)}, u32[]{:S(2)}) copy-start(s32[8]{0:T(128)} %param.17) | copy-start | bytes 100
  1.1 8.4 %collective-permute-start = (f32[2,2,4224]{2,1,0:T(2,128)S(1)}, f32[2,2,4224]{2,1,0:T(2,128)S(1)}, u32[]{:S(2)}, u32[]{:S(2)}) collective-permute-start(f32[2,2,4224]{2,1,0:T(2,128)S(1)} %get-tuple-element.22), channel_id=1, source_target_pairs={{0,96},{32,0},{64,32},{96,64},{1,97},{33,1},{65,33},{97,65},{2,98}... | collective-permute-start | bytes 202760 | tf_op jit(solution)/shard_map/ppermute | solution.py:348
  9.5 10.0 %copy-start.1 = (f32[2,2,2,4224]{3,2,1,0:T(2,128)}, f32[2,2,2,4224]{3,2,1,0:T(2,128)S(1)}, u32[]{:S(2)}) copy-start(f32[2,2,2,4224]{3,2,1,0:T(2,128)S(1)} %pad_maximum_fusion.own_hbm) | copy-start | bytes 405508
  9.5 10.0 %collective-permute-start.3 = (f32[2,2,2,4224]{3,2,1,0:T(2,128)S(1)}, f32[2,2,2,4224]{3,2,1,0:T(2,128)S(1)}, u32[]{:S(2)}, u32[]{:S(2)}) collective-permute-start(f32[2,2,2,4224]{3,2,1,0:T(2,128)S(1)} %pad_maximum_fusion.own_hbm), channel_id=1, source_target_pairs={{0,8},{8,16},{16,24},{24,0},{1,9},{9,17},{17,25},{25,1},{2,10},{10... | collective-permute-start | bytes 405512 | tf_op jit(solution)/shard_map/ppermute | solution.py:348
  11.1 8.3 %collective-permute-start.2 = (f32[2,2,2,4224]{3,2,1,0:T(2,128)S(1)}, f32[2,2,2,4224]{3,2,1,0:T(2,128)S(1)}, u32[]{:S(2)}, u32[]{:S(2)}) collective-permute-start(f32[2,2,2,4224]{3,2,1,0:T(2,128)S(1)} %pad_maximum_fusion.own_hbm), channel_id=1, source_target_pairs={{0,16},{8,24},{16,0},{24,8},{1,17},{9,25},{17,1},{25,9},{2,18},{10... | collective-permute-start | bytes 405512 | tf_op jit(solution)/shard_map/ppermute | solution.py:348
  14.1 5.4 %collective-permute-start.1 = (f32[2,2,2,4224]{3,2,1,0:T(2,128)S(1)}, f32[2,2,2,4224]{3,2,1,0:T(2,128)S(1)}, u32[]{:S(2)}, u32[]{:S(2)}) collective-permute-start(f32[2,2,2,4224]{3,2,1,0:T(2,128)S(1)} %pad_maximum_fusion.own_hbm), channel_id=1, source_target_pairs={{0,24},{8,0},{16,8},{24,16},{1,25},{9,1},{17,9},{25,17},{2,26},{10... | collective-permute-start | bytes 405512 | tf_op jit(solution)/shard_map/ppermute | solution.py:348
  19.5 0.7 copy-start.2
  19.5 0.7 copy-start.3
  19.5 0.7 copy-start.4
  76.3 4.5 %collective-permute-start.4 = (f32[16,2,8,2048]{3,2,1,0:T(8,128)}, f32[16,2,8,2048]{3,2,1,0:T(8,128)S(1)}, u32[]{:S(2)}, u32[]{:S(2)}) collective-permute-start(f32[16,2,8,2048]{3,2,1,0:T(8,128)} %get-tuple-element.8), channel_id=1, source_target_pairs={{0,32},{32,0},{1,33},{33,1},{2,34},{34,2},{3,35},{35,3},{4,36},{36... | collective-permute-start | bytes 6291464 | tf_op jit(solution)/shard_map/ppermute | solution.py:348
  82.9 10.8 %collective-permute-start.12 = (f32[4,8,2048]{2,1,0:T(8,128)S(1)}, f32[4,8,2048]{2,1,0:T(8,128)S(1)}, u32[]{:S(2)}, u32[]{:S(2)}) collective-permute-start(f32[4,8,2048]{2,1,0:T(8,128)S(1)} %get-tuple-element.9), channel_id=1, source_target_pairs={{0,64},{4,68},{64,0},{68,4},{1,65},{5,69},{65,1},{69,5},{2,66},{6,... | collective-permute-start | bytes 786440 | tf_op jit(solution)/shard_map/ppermute | solution.py:348
  84.9 13.5 %collective-permute-start.11 = (f32[4,8,2048]{2,1,0:T(8,128)S(1)}, f32[4,8,2048]{2,1,0:T(8,128)S(1)}, u32[]{:S(2)}, u32[]{:S(2)}) collective-permute-start(f32[4,8,2048]{2,1,0:T(8,128)S(1)} %get-tuple-element.10), channel_id=1, source_target_pairs={{0,4},{4,64},{64,68},{68,0},{1,5},{5,65},{65,69},{69,1},{2,6},{6,6... | collective-permute-start | bytes 786440 | tf_op jit(solution)/shard_map/ppermute | solution.py:348
  85.5 12.9 %collective-permute-start.13 = (f32[4,8,2048]{2,1,0:T(8,128)S(1)}, f32[4,8,2048]{2,1,0:T(8,128)S(1)}, u32[]{:S(2)}, u32[]{:S(2)}) collective-permute-start(f32[4,8,2048]{2,1,0:T(8,128)S(1)} %get-tuple-element.11), channel_id=1, source_target_pairs={{0,68},{4,0},{64,4},{68,64},{1,69},{5,1},{65,5},{69,65},{2,70},{6,... | collective-permute-start | bytes 786440 | tf_op jit(solution)/shard_map/ppermute | solution.py:348
  88.2 15.0 %collective-permute-start.6 = (f32[4,8,2048]{2,1,0:T(8,128)S(1)}, f32[4,8,2048]{2,1,0:T(8,128)S(1)}, u32[]{:S(2)}, u32[]{:S(2)}) collective-permute-start(f32[4,8,2048]{2,1,0:T(8,128)S(1)} %get-tuple-element.12), channel_id=1, source_target_pairs={{0,2},{1,3},{2,0},{3,1},{4,6},{5,7},{6,4},{7,5},{8,10},{9,11},{10,... | collective-permute-start | bytes 786440 | tf_op jit(solution)/shard_map/ppermute | solution.py:348
  92.2 12.4 %collective-permute-start.7 = (f32[4,8,2048]{2,1,0:T(8,128)S(1)}, f32[4,8,2048]{2,1,0:T(8,128)S(1)}, u32[]{:S(2)}, u32[]{:S(2)}) collective-permute-start(f32[4,8,2048]{2,1,0:T(8,128)S(1)} %get-tuple-element.13), channel_id=1, source_target_pairs={{0,3},{1,0},{2,1},{3,2},{4,7},{5,4},{6,5},{7,6},{8,11},{9,8},{10,9... | collective-permute-start | bytes 786440 | tf_op jit(solution)/shard_map/ppermute | solution.py:348
  93.7 10.9 %collective-permute-start.5 = (f32[4,8,2048]{2,1,0:T(8,128)S(1)}, f32[4,8,2048]{2,1,0:T(8,128)S(1)}, u32[]{:S(2)}, u32[]{:S(2)}) collective-permute-start(f32[4,8,2048]{2,1,0:T(8,128)S(1)} %get-tuple-element.14), channel_id=1, source_target_pairs={{0,1},{1,2},{2,3},{3,0},{4,5},{5,6},{6,7},{7,4},{8,9},{9,10},{10,1... | collective-permute-start | bytes 786440 | tf_op jit(solution)/shard_map/ppermute | solution.py:348
  98.5 9.5 %collective-permute-start.15 = (f32[8,2048]{1,0:T(8,128)S(1)}, f32[8,2048]{1,0:T(8,128)S(1)}, u32[]{:S(2)}, u32[]{:S(2)}) collective-permute-start(f32[8,2048]{1,0:T(8,128)S(1)} %get-tuple-element.18), channel_id=1, source_target_pairs={{0,2},{1,3},{2,0},{3,1},{4,6},{5,7},{6,4},{7,5},{8,10},{9,11},{10,... | collective-permute-start | bytes 196616 | tf_op jit(solution)/shard_map/ppermute | solution.py:348
  102.5 6.0 %collective-permute-start.16 = (f32[8,2048]{1,0:T(8,128)S(1)}, f32[8,2048]{1,0:T(8,128)S(1)}, u32[]{:S(2)}, u32[]{:S(2)}) collective-permute-start(f32[8,2048]{1,0:T(8,128)S(1)} %get-tuple-element.19), channel_id=1, source_target_pairs={{0,3},{1,0},{2,1},{3,2},{4,7},{5,4},{6,5},{7,6},{8,11},{9,8},{10,9... | collective-permute-start | bytes 196616 | tf_op jit(solution)/shard_map/ppermute | solution.py:348
  103.2 5.5 %collective-permute-start.14 = (f32[8,2048]{1,0:T(8,128)S(1)}, f32[8,2048]{1,0:T(8,128)S(1)}, u32[]{:S(2)}, u32[]{:S(2)}) collective-permute-start(f32[8,2048]{1,0:T(8,128)S(1)} %get-tuple-element.20), channel_id=1, source_target_pairs={{0,1},{1,2},{2,3},{3,0},{4,5},{5,6},{6,7},{7,4},{8,9},{9,10},{10,1... | collective-permute-start | bytes 196616 | tf_op jit(solution)/shard_map/ppermute | solution.py:348
  104.6 6.3 %collective-permute-start.9 = (f32[8,2048]{1,0:T(8,128)S(1)}, f32[8,2048]{1,0:T(8,128)S(1)}, u32[]{:S(2)}, u32[]{:S(2)}) collective-permute-start(f32[8,2048]{1,0:T(8,128)S(1)} %get-tuple-element.15), channel_id=1, source_target_pairs={{0,64},{4,68},{64,0},{68,4},{1,65},{5,69},{65,1},{69,5},{2,66},{6,... | collective-permute-start | bytes 196616 | tf_op jit(solution)/shard_map/ppermute | solution.py:348
  106.5 4.5 %collective-permute-start.10 = (f32[8,2048]{1,0:T(8,128)S(1)}, f32[8,2048]{1,0:T(8,128)S(1)}, u32[]{:S(2)}, u32[]{:S(2)}) collective-permute-start(f32[8,2048]{1,0:T(8,128)S(1)} %get-tuple-element.16), channel_id=1, source_target_pairs={{0,68},{4,0},{64,4},{68,64},{1,69},{5,1},{65,5},{69,65},{2,70},{6,... | collective-permute-start | bytes 196616 | tf_op jit(solution)/shard_map/ppermute | solution.py:348
  108.0 5.5 %collective-permute-start.8 = (f32[8,2048]{1,0:T(8,128)S(1)}, f32[8,2048]{1,0:T(8,128)S(1)}, u32[]{:S(2)}, u32[]{:S(2)}) collective-permute-start(f32[8,2048]{1,0:T(8,128)S(1)} %get-tuple-element.17), channel_id=1, source_target_pairs={{0,4},{4,64},{64,68},{68,0},{1,5},{5,65},{65,69},{69,1},{2,6},{6,6... | collective-permute-start | bytes 196616 | tf_op jit(solution)/shard_map/ppermute | solution.py:348

commit v5 on v4

--- a/solution.py
+++ b/solution.py
@@ -326,8 +326,8 @@
             pltpu.VMEM((2, 4, 4, 2, 16, HALF), jnp.float32),
         ]
         + [pltpu.VMEM((2, GRID * CHUNK, PLANE), jnp.bfloat16)] * 4
-        + [pltpu.VMEM((POINTS * 8, CHUNK), jnp.float32)]
-        + [pltpu.VMEM((16 * 8, CHUNK), jnp.float32)] * 9
+        + [pltpu.VMEM((POINTS * 8 + 8, CHUNK), jnp.float32)]
+        + [pltpu.VMEM((16 * 8 + 8, CHUNK), jnp.float32)] * 9
         + [pltpu.VMEM((NG, DEPTH), jnp.bfloat16)] * 4
         + [pltpu.VMEM((2 * ROWS, DEPTH), jnp.bfloat16)] * 4
         + [pltpu.VMEM((OWNERS, 2, 8, NG), jnp.float32)] * 2

time: 115 us -> 115 us (level)
  no operation moved by 1% of the time
where the time goes in v5:
time: 115 us; the launch traced here: 114 us
  Pallas kernels  56.1 us (49%)
  starting transfers between devices  30.3 us (26%)
  waiting for transfers between devices  12.9 us (11%)
  other arithmetic  8.98 us (8%)
  local copies, waits for them, and re-layouts  5.14 us (4%)
    pallas_call x1, Pallas kernels, partial_rows(): pl.pallas_call(kernel, out_shape=(part, part), in_specs=[smem, smem, smem...  56.1 us
    ppermute x17, starting transfers between devices, shifted(): lax.ppermute(value, axis, [(index, (index + by) % size) for index in rang...  30.3 us
    ppermute x17, waiting for transfers between devices, shifted(): lax.ppermute(value, axis, [(index, (index + by) % size) for index in rang...  12.9 us
  transfers between devices with their start and end apart: 17, of which 6 were waited for; matrix products, arithmetic and copies ran while one was open for 8% of the time, Pallas kernels for 0%

profile of v5, /device:TPU:0, one launch (start us, length us, event | category | flops | bytes accessed | tf_op | source)
XLA Modules:
  0.0 114.3 jit_solution(9292433804928408321)
XLA Ops:
  0.0 0.0 copy-start
  0.0 1.0 pad_select_fusion
  1.1 2.6 %collective-permute-start = (f32[2,2,4224]{2,1,0:T(2,128)S(1)}, f32[2,2,4224]{2,1,0:T(2,128)S(1)}, u32[]{:S(2)}, u32[]{:S(2)}) collective-permute-start(f32[2,2,4224]{2,1,0:T(2,128)S(1)} %get-tuple-element.22), channel_id=1, source_target_pairs={{0,96},{32,0},{64,32},{96,64},{1,97},{33,1},{65,33},{97,65},{2,98}... | collective-permute-start | bytes 202760 | tf_op jit(solution)/shard_map/ppermute | solution.py:348
  3.7 1.3 %reduce_sum.9 = s32[]{:T(128)} reduce(s32[8]{0:T(128)} %param.16, s32[]{:T(128)} %constant.153.clone.1), dimensions={0}, to_apply=%region_0.1 | reduce | flops 7 | bytes 40 | tf_op jit(solution)/shard_map/reduce_sum | solution.py:370
  5.7 0.1 iota_add_fusion
  5.8 0.1 add_add_fusion
  5.9 0.1 broadcast_add_fusion
  6.0 0.1 add.351
  6.1 1.3 %gather_fusion.1 = s32[2]{0:T(128)S(1)} fusion(s32[8]{0:T(128)} %param.16, s32[1024]{0:T(1024)S(1)} %pad_clamp_fusion), kind=kCustom, calls=%fused_computation.1 | custom fusion | bytes 24 | tf_op jit(solution)/shard_map/gather | solution.py:375
  7.4 1.3 %fusion.13.place_ref = s32[2048]{0:T(1024)} fusion(s32[2048]{0:T(1024)} %param.14), kind=kLoop, calls=%fused_computation.54 | loop fusion | flops 139264 | bytes 16384 | tf_op jit(solution)/shard_map/mul | solution.py:368
  8.7 0.0 copy-done
  8.7 0.6 gather_fusion
  9.3 0.1 compare_select_fusion
  9.4 0.0 collective-permute-done
  9.4 0.1 pad_maximum_fusion.own_hbm
  9.5 1.6 %collective-permute-start.3 = (f32[2,2,2,4224]{3,2,1,0:T(2,128)S(1)}, f32[2,2,2,4224]{3,2,1,0:T(2,128)S(1)}, u32[]{:S(2)}, u32[]{:S(2)}) collective-permute-start(f32[2,2,2,4224]{3,2,1,0:T(2,128)S(1)} %pad_maximum_fusion.own_hbm), channel_id=1, source_target_pairs={{0,8},{8,16},{16,24},{24,0},{1,9},{9,17},{17,25},{25,1},{2,10},{10... | collective-permute-start | bytes 405512 | tf_op jit(solution)/shard_map/ppermute | solution.py:348
  11.1 2.9 %collective-permute-start.2 = (f32[2,2,2,4224]{3,2,1,0:T(2,128)S(1)}, f32[2,2,2,4224]{3,2,1,0:T(2,128)S(1)}, u32[]{:S(2)}, u32[]{:S(2)}) collective-permute-start(f32[2,2,2,4224]{3,2,1,0:T(2,128)S(1)} %pad_maximum_fusion.own_hbm), channel_id=1, source_target_pairs={{0,16},{8,24},{16,0},{24,8},{1,17},{9,25},{17,1},{25,9},{2,18},{10... | collective-permute-start | bytes 405512 | tf_op jit(solution)/shard_map/ppermute | solution.py:348
  14.1 1.3 %collective-permute-start.1 = (f32[2,2,2,4224]{3,2,1,0:T(2,128)S(1)}, f32[2,2,2,4224]{3,2,1,0:T(2,128)S(1)}, u32[]{:S(2)}, u32[]{:S(2)}) collective-permute-start(f32[2,2,2,4224]{3,2,1,0:T(2,128)S(1)} %pad_maximum_fusion.own_hbm), channel_id=1, source_target_pairs={{0,24},{8,0},{16,8},{24,16},{1,25},{9,1},{17,9},{25,17},{2,26},{10... | collective-permute-start | bytes 405512 | tf_op jit(solution)/shard_map/ppermute | solution.py:348
  15.4 0.6 pad_add_fusion.rows_ref
  16.0 0.1 broadcast_in_dim.13
  16.0 0.7 reshape.284.weight_ref
  16.7 1.3 %copy.26 = s32[1,16,2,128]{3,1,2,0:T(8,128)} copy(s32[1,16,2,128]{3,2,1,0:T(2,128)} %bitcast.74) | data formatting | bytes 32768
  18.0 1.4 %pad_maximum_fusion.1.level_ref = f32[2,128]{1,0:T(2,128)} fusion(f32[2,64]{1,0:T(2,128)} %param.11), kind=kLoop, calls=%fused_computation.90 | loop fusion | flops 256 | bytes 1536 | tf_op jit(solution)/shard_map/concatenate | solution.py:377
  19.5 0.0 collective-permute-done.3.three_hbm
  19.5 0.0 collective-permute-done.2.two_hbm
  19.5 0.0 copy-start.3
  19.5 0.0 collective-permute-done.1.one_hbm
  19.5 0.6 copy-done.2
  20.1 0.1 copy-done.3
  20.2 0.1 copy-done.4
  20.2 56.1 %shard_map.100 = (f32[16,2,8,2048]{3,2,1,0:T(8,128)}, f32[16,2,8,2048]{3,2,1,0:T(8,128)}) custom-call(s32[2048]{0:T(1024)} %fusion.13.place_ref, s32[4096]{0:T(1024)} %bitcast.75, s32[34]{0:T(128)} %pad_add_fusion.rows_ref, f32[2,64,2,4096]{3,2,1,0:T(2,128)} %occ_hbm.1, f32[2,2,2,4224]{3,2,1,0:T(2,128)} %copy-done.1, f32[2,2,2,4224]{3,2,1,0:T(2,128)} %copy-done.4, ...), custom_call_target="tpu_custom_call" | custom-call | flops 40000000000 | bytes 10485760 | tf_op jit(solution)/shard_map/pallas_call | solution.py:316
  76.3 0.1 collective-permute-start.4
  76.4 4.4 %collective-permute-done.4 = f32[16,2,8,2048]{3,2,1,0:T(8,128)S(1)} collective-permute-done((f32[16,2,8,2048]{3,2,1,0:T(8,128)}, f32[16,2,8,2048]{3,2,1,0:T(8,128)S(1)}, u32[]{:S(2)}, u32[]{:S(2)}) %collective-permute-start.4) | collective-permute-done | bytes 2097184 | tf_op jit(solution)/shard_map/ppermute | solution.py:348
  80.8 1.9 %add.370 = f32[16,2,8,2048]{3,2,1,0:T(8,128)S(1)} add(f32[16,2,8,2048]{3,2,1,0:T(8,128)} %get-tuple-element.7, f32[16,2,8,2048]{3,2,1,0:T(8,128)S(1)} %collective-permute-done.4) | non-fusion elementwise | flops 524288 | bytes 6291456 | tf_op jit(solution)/shard_map/add | solution.py:390
  82.7 0.1 slice_bitcast_fusion.1
  82.8 0.1 copy_bitcast_fusion
  82.9 2.0 %collective-permute-start.12 = (f32[4,8,2048]{2,1,0:T(8,128)S(1)}, f32[4,8,2048]{2,1,0:T(8,128)S(1)}, u32[]{:S(2)}, u32[]{:S(2)}) collective-permute-start(f32[4,8,2048]{2,1,0:T(8,128)S(1)} %get-tuple-element.9), channel_id=1, source_target_pairs={{0,64},{4,68},{64,0},{68,4},{1,65},{5,69},{65,1},{69,5},{2,66},{6,... | collective-permute-start | bytes 786440 | tf_op jit(solution)/shard_map/ppermute | solution.py:348
  84.9 0.6 collective-permute-start.11
  85.5 2.6 %collective-permute-start.13 = (f32[4,8,2048]{2,1,0:T(8,128)S(1)}, f32[4,8,2048]{2,1,0:T(8,128)S(1)}, u32[]{:S(2)}, u32[]{:S(2)}) collective-permute-start(f32[4,8,2048]{2,1,0:T(8,128)S(1)} %get-tuple-element.11), channel_id=1, source_target_pairs={{0,68},{4,0},{64,4},{68,64},{1,69},{5,1},{65,5},{69,65},{2,70},{6,... | collective-permute-start | bytes 786440 | tf_op jit(solution)/shard_map/ppermute | solution.py:348
  88.1 0.1 slice_bitcast_fusion.5
  88.2 4.0 %collective-permute-start.6 = (f32[4,8,2048]{2,1,0:T(8,128)S(1)}, f32[4,8,2048]{2,1,0:T(8,128)S(1)}, u32[]{:S(2)}, u32[]{:S(2)}) collective-permute-start(f32[4,8,2048]{2,1,0:T(8,128)S(1)} %get-tuple-element.12), channel_id=1, source_target_pairs={{0,2},{1,3},{2,0},{3,1},{4,6},{5,7},{6,4},{7,5},{8,10},{9,11},{10,... | collective-permute-start | bytes 786440 | tf_op jit(solution)/shard_map/ppermute | solution.py:348
  92.2 0.7 collective-permute-start.7
  92.9 0.8 collective-permute-done.12
  93.6 1.9 %collective-permute-start.5 = (f32[4,8,2048]{2,1,0:T(8,128)S(1)}, f32[4,8,2048]{2,1,0:T(8,128)S(1)}, u32[]{:S(2)}, u32[]{:S(2)}) collective-permute-start(f32[4,8,2048]{2,1,0:T(8,128)S(1)} %get-tuple-element.14), channel_id=1, source_target_pairs={{0,1},{1,2},{2,3},{3,0},{4,5},{5,6},{6,7},{7,4},{8,9},{9,10},{10,1... | collective-permute-start | bytes 786440 | tf_op jit(solution)/shard_map/ppermute | solution.py:348
  95.6 2.8 %collective-permute-done.11 = f32[4,8,2048]{2,1,0:T(8,128)S(1)} collective-permute-done((f32[4,8,2048]{2,1,0:T(8,128)S(1)}, f32[4,8,2048]{2,1,0:T(8,128)S(1)}, u32[]{:S(2)}, u32[]{:S(2)}) %collective-permute-start.11) | collective-permute-done | bytes 262176 | tf_op jit(solution)/shard_map/ppermute | solution.py:348
  98.4 0.0 collective-permute-done.13
  98.4 0.1 fusion.1
  98.5 4.0 %collective-permute-start.15 = (f32[8,2048]{1,0:T(8,128)S(1)}, f32[8,2048]{1,0:T(8,128)S(1)}, u32[]{:S(2)}, u32[]{:S(2)}) collective-permute-start(f32[8,2048]{1,0:T(8,128)S(1)} %get-tuple-element.18), channel_id=1, source_target_pairs={{0,2},{1,3},{2,0},{3,1},{4,6},{5,7},{6,4},{7,5},{8,10},{9,11},{10,... | collective-permute-start | bytes 196616 | tf_op jit(solution)/shard_map/ppermute | solution.py:348
  102.5 0.7 collective-permute-start.16
  103.2 0.0 collective-permute-done.6
  103.2 1.3 %collective-permute-start.14 = (f32[8,2048]{1,0:T(8,128)S(1)}, f32[8,2048]{1,0:T(8,128)S(1)}, u32[]{:S(2)}, u32[]{:S(2)}) collective-permute-start(f32[8,2048]{1,0:T(8,128)S(1)} %get-tuple-element.20), channel_id=1, source_target_pairs={{0,1},{1,2},{2,3},{3,0},{4,5},{5,6},{6,7},{7,4},{8,9},{9,10},{10,1... | collective-permute-start | bytes 196616 | tf_op jit(solution)/shard_map/ppermute | solution.py:348
  104.5 0.0 collective-permute-done.7
  104.5 0.0 collective-permute-done.5
  104.5 0.1 fusion.3
  104.6 1.8 %collective-permute-start.9 = (f32[8,2048]{1,0:T(8,128)S(1)}, f32[8,2048]{1,0:T(8,128)S(1)}, u32[]{:S(2)}, u32[]{:S(2)}) collective-permute-start(f32[8,2048]{1,0:T(8,128)S(1)} %get-tuple-element.15), channel_id=1, source_target_pairs={{0,64},{4,68},{64,0},{68,4},{1,65},{5,69},{65,1},{69,5},{2,66},{6,... | collective-permute-start | bytes 196616 | tf_op jit(solution)/shard_map/ppermute | solution.py:348
  106.5 1.5 %collective-permute-start.10 = (f32[8,2048]{1,0:T(8,128)S(1)}, f32[8,2048]{1,0:T(8,128)S(1)}, u32[]{:S(2)}, u32[]{:S(2)}) collective-permute-start(f32[8,2048]{1,0:T(8,128)S(1)} %get-tuple-element.16), channel_id=1, source_target_pairs={{0,68},{4,0},{64,4},{68,64},{1,69},{5,1},{65,5},{69,65},{2,70},{6,... | collective-permute-start | bytes 196616 | tf_op jit(solution)/shard_map/ppermute | solution.py:348
  108.0 0.0 collective-permute-done.15
  108.0 0.5 collective-permute-start.8
  108.5 0.0 collective-permute-done.16
  108.5 0.2 collective-permute-done.14
  108.8 2.2 %collective-permute-done.9 = f32[8,2048]{1,0:T(8,128)S(1)} collective-permute-done((f32[8,2048]{1,0:T(8,128)S(1)}, f32[8,2048]{1,0:T(8,128)S(1)}, u32[]{:S(2)}, u32[]{:S(2)}) %collective-permute-start.9) | collective-permute-done | bytes 65568 | tf_op jit(solution)/shard_map/ppermute | solution.py:348
  111.0 0.0 collective-permute-done.10
  111.0 2.5 %collective-permute-done.8 = f32[8,2048]{1,0:T(8,128)S(1)} collective-permute-done((f32[8,2048]{1,0:T(8,128)S(1)}, f32[8,2048]{1,0:T(8,128)S(1)}, u32[]{:S(2)}, u32[]{:S(2)}) %collective-permute-start.8) | collective-permute-done | bytes 65568 | tf_op jit(solution)/shard_map/ppermute | solution.py:348
  113.5 0.8 maximum_bitcast_fusion
  (21 shorter events, 0.3 us)
Async XLA Ops:
  0.0 8.7 %copy-start = (s32[8]{0:T(128)S(1)}, s32[8]{0:T(128)}, u32[]{:S(2)}) copy-start(s32[8]{0:T(128)} %param.17) | copy-start | bytes 100
  1.1 8.4 %collective-permute-start = (f32[2,2,4224]{2,1,0:T(2,128)S(1)}, f32[2,2,4224]{2,1,0:T(2,128)S(1)}, u32[]{:S(2)}, u32[]{:S(2)}) collective-permute-start(f32[2,2,4224]{2,1,0:T(2,128)S(1)} %get-tuple-element.22), channel_id=1, source_target_pairs={{0,96},{32,0},{64,32},{96,64},{1,97},{33,1},{65,33},{97,65},{2,98}... | collective-permute-start | bytes 202760 | tf_op jit(solution)/shard_map/ppermute | solution.py:348
  9.5 10.0 %copy-start.1 = (f32[2,2,2,4224]{3,2,1,0:T(2,128)}, f32[2,2,2,4224]{3,2,1,0:T(2,128)S(1)}, u32[]{:S(2)}) copy-start(f32[2,2,2,4224]{3,2,1,0:T(2,128)S(1)} %pad_maximum_fusion.own_hbm) | copy-start | bytes 405508
  9.5 10.0 %collective-permute-start.3 = (f32[2,2,2,4224]{3,2,1,0:T(2,128)S(1)}, f32[2,2,2,4224]{3,2,1,0:T(2,128)S(1)}, u32[]{:S(2)}, u32[]{:S(2)}) collective-permute-start(f32[2,2,2,4224]{3,2,1,0:T(2,128)S(1)} %pad_maximum_fusion.own_hbm), channel_id=1, source_target_pairs={{0,8},{8,16},{16,24},{24,0},{1,9},{9,17},{17,25},{25,1},{2,10},{10... | collective-permute-start | bytes 405512 | tf_op jit(solution)/shard_map/ppermute | solution.py:348
  11.1 8.3 %collective-permute-start.2 = (f32[2,2,2,4224]{3,2,1,0:T(2,128)S(1)}, f32[2,2,2,4224]{3,2,1,0:T(2,128)S(1)}, u32[]{:S(2)}, u32[]{:S(2)}) collective-permute-start(f32[2,2,2,4224]{3,2,1,0:T(2,128)S(1)} %pad_maximum_fusion.own_hbm), channel_id=1, source_target_pairs={{0,16},{8,24},{16,0},{24,8},{1,17},{9,25},{17,1},{25,9},{2,18},{10... | collective-permute-start | bytes 405512 | tf_op jit(solution)/shard_map/ppermute | solution.py:348
  14.1 5.4 %collective-permute-start.1 = (f32[2,2,2,4224]{3,2,1,0:T(2,128)S(1)}, f32[2,2,2,4224]{3,2,1,0:T(2,128)S(1)}, u32[]{:S(2)}, u32[]{:S(2)}) collective-permute-start(f32[2,2,2,4224]{3,2,1,0:T(2,128)S(1)} %pad_maximum_fusion.own_hbm), channel_id=1, source_target_pairs={{0,24},{8,0},{16,8},{24,16},{1,25},{9,1},{17,9},{25,17},{2,26},{10... | collective-permute-start | bytes 405512 | tf_op jit(solution)/shard_map/ppermute | solution.py:348
  19.5 0.7 copy-start.2
  19.5 0.7 copy-start.3
  19.5 0.7 copy-start.4
  76.3 4.5 %collective-permute-start.4 = (f32[16,2,8,2048]{3,2,1,0:T(8,128)}, f32[16,2,8,2048]{3,2,1,0:T(8,128)S(1)}, u32[]{:S(2)}, u32[]{:S(2)}) collective-permute-start(f32[16,2,8,2048]{3,2,1,0:T(8,128)} %get-tuple-element.8), channel_id=1, source_target_pairs={{0,32},{32,0},{1,33},{33,1},{2,34},{34,2},{3,35},{35,3},{4,36},{36... | collective-permute-start | bytes 6291464 | tf_op jit(solution)/shard_map/ppermute | solution.py:348
  82.9 10.8 %collective-permute-start.12 = (f32[4,8,2048]{2,1,0:T(8,128)S(1)}, f32[4,8,2048]{2,1,0:T(8,128)S(1)}, u32[]{:S(2)}, u32[]{:S(2)}) collective-permute-start(f32[4,8,2048]{2,1,0:T(8,128)S(1)} %get-tuple-element.9), channel_id=1, source_target_pairs={{0,64},{4,68},{64,0},{68,4},{1,65},{5,69},{65,1},{69,5},{2,66},{6,... | collective-permute-start | bytes 786440 | tf_op jit(solution)/shard_map/ppermute | solution.py:348
  84.9 13.5 %collective-permute-start.11 = (f32[4,8,2048]{2,1,0:T(8,128)S(1)}, f32[4,8,2048]{2,1,0:T(8,128)S(1)}, u32[]{:S(2)}, u32[]{:S(2)}) collective-permute-start(f32[4,8,2048]{2,1,0:T(8,128)S(1)} %get-tuple-element.10), channel_id=1, source_target_pairs={{0,4},{4,64},{64,68},{68,0},{1,5},{5,65},{65,69},{69,1},{2,6},{6,6... | collective-permute-start | bytes 786440 | tf_op jit(solution)/shard_map/ppermute | solution.py:348
  85.5 12.9 %collective-permute-start.13 = (f32[4,8,2048]{2,1,0:T(8,128)S(1)}, f32[4,8,2048]{2,1,0:T(8,128)S(1)}, u32[]{:S(2)}, u32[]{:S(2)}) collective-permute-start(f32[4,8,2048]{2,1,0:T(8,128)S(1)} %get-tuple-element.11), channel_id=1, source_target_pairs={{0,68},{4,0},{64,4},{68,64},{1,69},{5,1},{65,5},{69,65},{2,70},{6,... | collective-permute-start | bytes 786440 | tf_op jit(solution)/shard_map/ppermute | solution.py:348
  88.2 15.0 %collective-permute-start.6 = (f32[4,8,2048]{2,1,0:T(8,128)S(1)}, f32[4,8,2048]{2,1,0:T(8,128)S(1)}, u32[]{:S(2)}, u32[]{:S(2)}) collective-permute-start(f32[4,8,2048]{2,1,0:T(8,128)S(1)} %get-tuple-element.12), channel_id=1, source_target_pairs={{0,2},{1,3},{2,0},{3,1},{4,6},{5,7},{6,4},{7,5},{8,10},{9,11},{10,... | collective-permute-start | bytes 786440 | tf_op jit(solution)/shard_map/ppermute | solution.py:348
  92.2 12.4 %collective-permute-start.7 = (f32[4,8,2048]{2,1,0:T(8,128)S(1)}, f32[4,8,2048]{2,1,0:T(8,128)S(1)}, u32[]{:S(2)}, u32[]{:S(2)}) collective-permute-start(f32[4,8,2048]{2,1,0:T(8,128)S(1)} %get-tuple-element.13), channel_id=1, source_target_pairs={{0,3},{1,0},{2,1},{3,2},{4,7},{5,4},{6,5},{7,6},{8,11},{9,8},{10,9... | collective-permute-start | bytes 786440 | tf_op jit(solution)/shard_map/ppermute | solution.py:348
  93.6 10.9 %collective-permute-start.5 = (f32[4,8,2048]{2,1,0:T(8,128)S(1)}, f32[4,8,2048]{2,1,0:T(8,128)S(1)}, u32[]{:S(2)}, u32[]{:S(2)}) collective-permute-start(f32[4,8,2048]{2,1,0:T(8,128)S(1)} %get-tuple-element.14), channel_id=1, source_target_pairs={{0,1},{1,2},{2,3},{3,0},{4,5},{5,6},{6,7},{7,4},{8,9},{9,10},{10,1... | collective-permute-start | bytes 786440 | tf_op jit(solution)/shard_map/ppermute | solution.py:348
  98.5 9.5 %collective-permute-start.15 = (f32[8,2048]{1,0:T(8,128)S(1)}, f32[8,2048]{1,0:T(8,128)S(1)}, u32[]{:S(2)}, u32[]{:S(2)}) collective-permute-start(f32[8,2048]{1,0:T(8,128)S(1)} %get-tuple-element.18), channel_id=1, source_target_pairs={{0,2},{1,3},{2,0},{3,1},{4,6},{5,7},{6,4},{7,5},{8,10},{9,11},{10,... | collective-permute-start | bytes 196616 | tf_op jit(solution)/shard_map/ppermute | solution.py:348
  102.5 6.0 %collective-permute-start.16 = (f32[8,2048]{1,0:T(8,128)S(1)}, f32[8,2048]{1,0:T(8,128)S(1)}, u32[]{:S(2)}, u32[]{:S(2)}) collective-permute-start(f32[8,2048]{1,0:T(8,128)S(1)} %get-tuple-element.19), channel_id=1, source_target_pairs={{0,3},{1,0},{2,1},{3,2},{4,7},{5,4},{6,5},{7,6},{8,11},{9,8},{10,9... | collective-permute-start | bytes 196616 | tf_op jit(solution)/shard_map/ppermute | solution.py:348
  103.2 5.5 %collective-permute-start.14 = (f32[8,2048]{1,0:T(8,128)S(1)}, f32[8,2048]{1,0:T(8,128)S(1)}, u32[]{:S(2)}, u32[]{:S(2)}) collective-permute-start(f32[8,2048]{1,0:T(8,128)S(1)} %get-tuple-element.20), channel_id=1, source_target_pairs={{0,1},{1,2},{2,3},{3,0},{4,5},{5,6},{6,7},{7,4},{8,9},{9,10},{10,1... | collective-permute-start | bytes 196616 | tf_op jit(solution)/shard_map/ppermute | solution.py:348
  104.6 6.3 %collective-permute-start.9 = (f32[8,2048]{1,0:T(8,128)S(1)}, f32[8,2048]{1,0:T(8,128)S(1)}, u32[]{:S(2)}, u32[]{:S(2)}) collective-permute-start(f32[8,2048]{1,0:T(8,128)S(1)} %get-tuple-element.15), channel_id=1, source_target_pairs={{0,64},{4,68},{64,0},{68,4},{1,65},{5,69},{65,1},{69,5},{2,66},{6,... | collective-permute-start | bytes 196616 | tf_op jit(solution)/shard_map/ppermute | solution.py:348
  106.5 4.5 %collective-permute-start.10 = (f32[8,2048]{1,0:T(8,128)S(1)}, f32[8,2048]{1,0:T(8,128)S(1)}, u32[]{:S(2)}, u32[]{:S(2)}) collective-permute-start(f32[8,2048]{1,0:T(8,128)S(1)} %get-tuple-element.16), channel_id=1, source_target_pairs={{0,68},{4,0},{64,4},{68,64},{1,69},{5,1},{65,5},{69,65},{2,70},{6,... | collective-permute-start | bytes 196616 | tf_op jit(solution)/shard_map/ppermute | solution.py:348
  108.0 5.5 %collective-permute-start.8 = (f32[8,2048]{1,0:T(8,128)S(1)}, f32[8,2048]{1,0:T(8,128)S(1)}, u32[]{:S(2)}, u32[]{:S(2)}) collective-permute-start(f32[8,2048]{1,0:T(8,128)S(1)} %get-tuple-element.17), channel_id=1, source_target_pairs={{0,4},{4,64},{64,68},{68,0},{1,5},{5,65},{65,69},{69,1},{2,6},{6,6... | collective-permute-start | bytes 196616 | tf_op jit(solution)/shard_map/ppermute | solution.py:348

commit v6 on v5

--- a/solution.py
+++ b/solution.py
@@ -202,7 +202,7 @@
                 alo_ref[pl.ds(ROWS + row, 16), second] = rlo
             return carry
 
-        lax.fori_loop(0, ROWS // 16, left, 0)
+        lax.fori_loop(0, ROWS // 16, left, 0, unroll=2)
 
     def gather(k):
         bhi_ref, blo_ref = rights[k]
@@ -249,7 +249,7 @@
 
     for copy in copies[0] + others:
         copy.wait()
-    lax.fori_loop(0, 8, first, 0)
+    lax.fori_loop(0, 8, first, 0, unroll=2)
 
     def two(turn, carry):
         both(2 * turn + 1, 1)

time: 115 us -> 114 us (level)
  no operation moved by 1% of the time
where the time goes in v6:
time: 114 us
  Pallas kernels  55.9 us (49%)
  starting transfers between devices  30.3 us (27%)
  waiting for transfers between devices  12.9 us (11%)
  other arithmetic  8.98 us (8%)
  local copies, waits for them, and re-layouts  5.14 us (5%)
    pallas_call x1, Pallas kernels, partial_rows(): pl.pallas_call(kernel, out_shape=(part, part), in_specs=[smem, smem, smem...  55.9 us
    ppermute x17, starting transfers between devices, shifted(): lax.ppermute(value, axis, [(index, (index + by) % size) for index in rang...  30.3 us
    ppermute x17, waiting for transfers between devices, shifted(): lax.ppermute(value, axis, [(index, (index + by) % size) for index in rang...  12.9 us
  transfers between devices with their start and end apart: 17, of which 6 were waited for; matrix products, arithmetic and copies ran while one was open for 8% of the time, Pallas kernels for 0%

profile of v6, /device:TPU:0, one launch (start us, length us, event | category | flops | bytes accessed | tf_op | source)
XLA Modules:
  0.0 114.1 jit_solution(9328780699514704638)
XLA Ops:
  0.0 0.0 copy-start
  0.0 1.0 pad_select_fusion
  1.1 2.6 %collective-permute-start = (f32[2,2,4224]{2,1,0:T(2,128)S(1)}, f32[2,2,4224]{2,1,0:T(2,128)S(1)}, u32[]{:S(2)}, u32[]{:S(2)}) collective-permute-start(f32[2,2,4224]{2,1,0:T(2,128)S(1)} %get-tuple-element.22), channel_id=1, source_target_pairs={{0,96},{32,0},{64,32},{96,64},{1,97},{33,1},{65,33},{97,65},{2,98}... | collective-permute-start | bytes 202760 | tf_op jit(solution)/shard_map/ppermute | solution.py:348
  3.7 1.3 %reduce_sum.9 = s32[]{:T(128)} reduce(s32[8]{0:T(128)} %param.16, s32[]{:T(128)} %constant.153.clone.1), dimensions={0}, to_apply=%region_0.1 | reduce | flops 7 | bytes 40 | tf_op jit(solution)/shard_map/reduce_sum | solution.py:370
  5.7 0.1 iota_add_fusion
  5.8 0.1 add_add_fusion
  5.9 0.1 broadcast_add_fusion
  6.0 0.1 add.351
  6.1 1.3 %gather_fusion.1 = s32[2]{0:T(128)S(1)} fusion(s32[8]{0:T(128)} %param.16, s32[1024]{0:T(1024)S(1)} %pad_clamp_fusion), kind=kCustom, calls=%fused_computation.1 | custom fusion | bytes 24 | tf_op jit(solution)/shard_map/gather | solution.py:375
  7.4 1.3 %fusion.13.place_ref = s32[2048]{0:T(1024)} fusion(s32[2048]{0:T(1024)} %param.14), kind=kLoop, calls=%fused_computation.54 | loop fusion | flops 139264 | bytes 16384 | tf_op jit(solution)/shard_map/mul | solution.py:368
  8.7 0.0 copy-done
  8.7 0.6 gather_fusion
  9.3 0.1 compare_select_fusion
  9.4 0.0 collective-permute-done
  9.4 0.1 pad_maximum_fusion.own_hbm
  9.5 1.6 %collective-permute-start.3 = (f32[2,2,2,4224]{3,2,1,0:T(2,128)S(1)}, f32[2,2,2,4224]{3,2,1,0:T(2,128)S(1)}, u32[]{:S(2)}, u32[]{:S(2)}) collective-permute-start(f32[2,2,2,4224]{3,2,1,0:T(2,128)S(1)} %pad_maximum_fusion.own_hbm), channel_id=1, source_target_pairs={{0,8},{8,16},{16,24},{24,0},{1,9},{9,17},{17,25},{25,1},{2,10},{10... | collective-permute-start | bytes 405512 | tf_op jit(solution)/shard_map/ppermute | solution.py:348
  11.1 2.9 %collective-permute-start.2 = (f32[2,2,2,4224]{3,2,1,0:T(2,128)S(1)}, f32[2,2,2,4224]{3,2,1,0:T(2,128)S(1)}, u32[]{:S(2)}, u32[]{:S(2)}) collective-permute-start(f32[2,2,2,4224]{3,2,1,0:T(2,128)S(1)} %pad_maximum_fusion.own_hbm), channel_id=1, source_target_pairs={{0,16},{8,24},{16,0},{24,8},{1,17},{9,25},{17,1},{25,9},{2,18},{10... | collective-permute-start | bytes 405512 | tf_op jit(solution)/shard_map/ppermute | solution.py:348
  14.1 1.3 %collective-permute-start.1 = (f32[2,2,2,4224]{3,2,1,0:T(2,128)S(1)}, f32[2,2,2,4224]{3,2,1,0:T(2,128)S(1)}, u32[]{:S(2)}, u32[]{:S(2)}) collective-permute-start(f32[2,2,2,4224]{3,2,1,0:T(2,128)S(1)} %pad_maximum_fusion.own_hbm), channel_id=1, source_target_pairs={{0,24},{8,0},{16,8},{24,16},{1,25},{9,1},{17,9},{25,17},{2,26},{10... | collective-permute-start | bytes 405512 | tf_op jit(solution)/shard_map/ppermute | solution.py:348
  15.4 0.6 pad_add_fusion.rows_ref
  16.0 0.1 broadcast_in_dim.13
  16.0 0.7 reshape.284.weight_ref
  16.7 1.3 %copy.26 = s32[1,16,2,128]{3,1,2,0:T(8,128)} copy(s32[1,16,2,128]{3,2,1,0:T(2,128)} %bitcast.74) | data formatting | bytes 32768
  18.0 1.4 %pad_maximum_fusion.1.level_ref = f32[2,128]{1,0:T(2,128)} fusion(f32[2,64]{1,0:T(2,128)} %param.11), kind=kLoop, calls=%fused_computation.90 | loop fusion | flops 256 | bytes 1536 | tf_op jit(solution)/shard_map/concatenate | solution.py:377
  19.5 0.0 collective-permute-done.3.three_hbm
  19.5 0.0 collective-permute-done.2.two_hbm
  19.5 0.0 copy-start.3
  19.5 0.0 collective-permute-done.1.one_hbm
  19.5 0.6 copy-done.2
  20.1 0.1 copy-done.3
  20.2 0.1 copy-done.4
  20.2 55.9 %shard_map.100 = (f32[16,2,8,2048]{3,2,1,0:T(8,128)}, f32[16,2,8,2048]{3,2,1,0:T(8,128)}) custom-call(s32[2048]{0:T(1024)} %fusion.13.place_ref, s32[4096]{0:T(1024)} %bitcast.75, s32[34]{0:T(128)} %pad_add_fusion.rows_ref, f32[2,64,2,4096]{3,2,1,0:T(2,128)} %occ_hbm.1, f32[2,2,2,4224]{3,2,1,0:T(2,128)} %copy-done.1, f32[2,2,2,4224]{3,2,1,0:T(2,128)} %copy-done.4, ...), custom_call_target="tpu_custom_call" | custom-call | flops 40000000000 | bytes 10485760 | tf_op jit(solution)/shard_map/pallas_call | solution.py:316
  76.1 0.1 collective-permute-start.4
  76.2 4.4 %collective-permute-done.4 = f32[16,2,8,2048]{3,2,1,0:T(8,128)S(1)} collective-permute-done((f32[16,2,8,2048]{3,2,1,0:T(8,128)}, f32[16,2,8,2048]{3,2,1,0:T(8,128)S(1)}, u32[]{:S(2)}, u32[]{:S(2)}) %collective-permute-start.4) | collective-permute-done | bytes 2097184 | tf_op jit(solution)/shard_map/ppermute | solution.py:348
  80.6 1.9 %add.370 = f32[16,2,8,2048]{3,2,1,0:T(8,128)S(1)} add(f32[16,2,8,2048]{3,2,1,0:T(8,128)} %get-tuple-element.7, f32[16,2,8,2048]{3,2,1,0:T(8,128)S(1)} %collective-permute-done.4) | non-fusion elementwise | flops 524288 | bytes 6291456 | tf_op jit(solution)/shard_map/add | solution.py:390
  82.5 0.1 slice_bitcast_fusion.1
  82.6 0.1 copy_bitcast_fusion
  82.6 2.0 %collective-permute-start.12 = (f32[4,8,2048]{2,1,0:T(8,128)S(1)}, f32[4,8,2048]{2,1,0:T(8,128)S(1)}, u32[]{:S(2)}, u32[]{:S(2)}) collective-permute-start(f32[4,8,2048]{2,1,0:T(8,128)S(1)} %get-tuple-element.9), channel_id=1, source_target_pairs={{0,64},{4,68},{64,0},{68,4},{1,65},{5,69},{65,1},{69,5},{2,66},{6,... | collective-permute-start | bytes 786440 | tf_op jit(solution)/shard_map/ppermute | solution.py:348
  84.7 0.6 collective-permute-start.11
  85.3 2.6 %collective-permute-start.13 = (f32[4,8,2048]{2,1,0:T(8,128)S(1)}, f32[4,8,2048]{2,1,0:T(8,128)S(1)}, u32[]{:S(2)}, u32[]{:S(2)}) collective-permute-start(f32[4,8,2048]{2,1,0:T(8,128)S(1)} %get-tuple-element.11), channel_id=1, source_target_pairs={{0,68},{4,0},{64,4},{68,64},{1,69},{5,1},{65,5},{69,65},{2,70},{6,... | collective-permute-start | bytes 786440 | tf_op jit(solution)/shard_map/ppermute | solution.py:348
  87.9 0.1 slice_bitcast_fusion.5
  88.0 4.0 %collective-permute-start.6 = (f32[4,8,2048]{2,1,0:T(8,128)S(1)}, f32[4,8,2048]{2,1,0:T(8,128)S(1)}, u32[]{:S(2)}, u32[]{:S(2)}) collective-permute-start(f32[4,8,2048]{2,1,0:T(8,128)S(1)} %get-tuple-element.12), channel_id=1, source_target_pairs={{0,2},{1,3},{2,0},{3,1},{4,6},{5,7},{6,4},{7,5},{8,10},{9,11},{10,... | collective-permute-start | bytes 786440 | tf_op jit(solution)/shard_map/ppermute | solution.py:348
  91.9 0.7 collective-permute-start.7
  92.6 0.8 collective-permute-done.12
  93.4 1.9 %collective-permute-start.5 = (f32[4,8,2048]{2,1,0:T(8,128)S(1)}, f32[4,8,2048]{2,1,0:T(8,128)S(1)}, u32[]{:S(2)}, u32[]{:S(2)}) collective-permute-start(f32[4,8,2048]{2,1,0:T(8,128)S(1)} %get-tuple-element.14), channel_id=1, source_target_pairs={{0,1},{1,2},{2,3},{3,0},{4,5},{5,6},{6,7},{7,4},{8,9},{9,10},{10,1... | collective-permute-start | bytes 786440 | tf_op jit(solution)/shard_map/ppermute | solution.py:348
  95.3 2.9 %collective-permute-done.11 = f32[4,8,2048]{2,1,0:T(8,128)S(1)} collective-permute-done((f32[4,8,2048]{2,1,0:T(8,128)S(1)}, f32[4,8,2048]{2,1,0:T(8,128)S(1)}, u32[]{:S(2)}, u32[]{:S(2)}) %collective-permute-start.11) | collective-permute-done | bytes 262176 | tf_op jit(solution)/shard_map/ppermute | solution.py:348
  98.2 0.0 collective-permute-done.13
  98.2 0.1 fusion.1
  98.3 4.0 %collective-permute-start.15 = (f32[8,2048]{1,0:T(8,128)S(1)}, f32[8,2048]{1,0:T(8,128)S(1)}, u32[]{:S(2)}, u32[]{:S(2)}) collective-permute-start(f32[8,2048]{1,0:T(8,128)S(1)} %get-tuple-element.18), channel_id=1, source_target_pairs={{0,2},{1,3},{2,0},{3,1},{4,6},{5,7},{6,4},{7,5},{8,10},{9,11},{10,... | collective-permute-start | bytes 196616 | tf_op jit(solution)/shard_map/ppermute | solution.py:348
  102.2 0.7 collective-permute-start.16
  103.0 0.0 collective-permute-done.6
  103.0 1.3 %collective-permute-start.14 = (f32[8,2048]{1,0:T(8,128)S(1)}, f32[8,2048]{1,0:T(8,128)S(1)}, u32[]{:S(2)}, u32[]{:S(2)}) collective-permute-start(f32[8,2048]{1,0:T(8,128)S(1)} %get-tuple-element.20), channel_id=1, source_target_pairs={{0,1},{1,2},{2,3},{3,0},{4,5},{5,6},{6,7},{7,4},{8,9},{9,10},{10,1... | collective-permute-start | bytes 196616 | tf_op jit(solution)/shard_map/ppermute | solution.py:348
  104.3 0.0 collective-permute-done.7
  104.3 0.0 collective-permute-done.5
  104.3 0.1 fusion.3
  104.4 1.8 %collective-permute-start.9 = (f32[8,2048]{1,0:T(8,128)S(1)}, f32[8,2048]{1,0:T(8,128)S(1)}, u32[]{:S(2)}, u32[]{:S(2)}) collective-permute-start(f32[8,2048]{1,0:T(8,128)S(1)} %get-tuple-element.15), channel_id=1, source_target_pairs={{0,64},{4,68},{64,0},{68,4},{1,65},{5,69},{65,1},{69,5},{2,66},{6,... | collective-permute-start | bytes 196616 | tf_op jit(solution)/shard_map/ppermute | solution.py:348
  106.2 1.5 %collective-permute-start.10 = (f32[8,2048]{1,0:T(8,128)S(1)}, f32[8,2048]{1,0:T(8,128)S(1)}, u32[]{:S(2)}, u32[]{:S(2)}) collective-permute-start(f32[8,2048]{1,0:T(8,128)S(1)} %get-tuple-element.16), channel_id=1, source_target_pairs={{0,68},{4,0},{64,4},{68,64},{1,69},{5,1},{65,5},{69,65},{2,70},{6,... | collective-permute-start | bytes 196616 | tf_op jit(solution)/shard_map/ppermute | solution.py:348
  107.7 0.0 collective-permute-done.15
  107.7 0.5 collective-permute-start.8
  108.3 0.0 collective-permute-done.16
  108.3 0.2 collective-permute-done.14
  108.5 2.2 %collective-permute-done.9 = f32[8,2048]{1,0:T(8,128)S(1)} collective-permute-done((f32[8,2048]{1,0:T(8,128)S(1)}, f32[8,2048]{1,0:T(8,128)S(1)}, u32[]{:S(2)}, u32[]{:S(2)}) %collective-permute-start.9) | collective-permute-done | bytes 65568 | tf_op jit(solution)/shard_map/ppermute | solution.py:348
  110.7 0.0 collective-permute-done.10
  110.7 2.5 %collective-permute-done.8 = f32[8,2048]{1,0:T(8,128)S(1)} collective-permute-done((f32[8,2048]{1,0:T(8,128)S(1)}, f32[8,2048]{1,0:T(8,128)S(1)}, u32[]{:S(2)}, u32[]{:S(2)}) %collective-permute-start.8) | collective-permute-done | bytes 65568 | tf_op jit(solution)/shard_map/ppermute | solution.py:348
  113.3 0.8 maximum_bitcast_fusion
  (21 shorter events, 0.3 us)
Async XLA Ops:
  0.0 8.7 %copy-start = (s32[8]{0:T(128)S(1)}, s32[8]{0:T(128)}, u32[]{:S(2)}) copy-start(s32[8]{0:T(128)} %param.17) | copy-start | bytes 100
  1.1 8.4 %collective-permute-start = (f32[2,2,4224]{2,1,0:T(2,128)S(1)}, f32[2,2,4224]{2,1,0:T(2,128)S(1)}, u32[]{:S(2)}, u32[]{:S(2)}) collective-permute-start(f32[2,2,4224]{2,1,0:T(2,128)S(1)} %get-tuple-element.22), channel_id=1, source_target_pairs={{0,96},{32,0},{64,32},{96,64},{1,97},{33,1},{65,33},{97,65},{2,98}... | collective-permute-start | bytes 202760 | tf_op jit(solution)/shard_map/ppermute | solution.py:348
  9.5 10.0 %copy-start.1 = (f32[2,2,2,4224]{3,2,1,0:T(2,128)}, f32[2,2,2,4224]{3,2,1,0:T(2,128)S(1)}, u32[]{:S(2)}) copy-start(f32[2,2,2,4224]{3,2,1,0:T(2,128)S(1)} %pad_maximum_fusion.own_hbm) | copy-start | bytes 405508
  9.5 10.0 %collective-permute-start.3 = (f32[2,2,2,4224]{3,2,1,0:T(2,128)S(1)}, f32[2,2,2,4224]{3,2,1,0:T(2,128)S(1)}, u32[]{:S(2)}, u32[]{:S(2)}) collective-permute-start(f32[2,2,2,4224]{3,2,1,0:T(2,128)S(1)} %pad_maximum_fusion.own_hbm), channel_id=1, source_target_pairs={{0,8},{8,16},{16,24},{24,0},{1,9},{9,17},{17,25},{25,1},{2,10},{10... | collective-permute-start | bytes 405512 | tf_op jit(solution)/shard_map/ppermute | solution.py:348
  11.1 8.3 %collective-permute-start.2 = (f32[2,2,2,4224]{3,2,1,0:T(2,128)S(1)}, f32[2,2,2,4224]{3,2,1,0:T(2,128)S(1)}, u32[]{:S(2)}, u32[]{:S(2)}) collective-permute-start(f32[2,2,2,4224]{3,2,1,0:T(2,128)S(1)} %pad_maximum_fusion.own_hbm), channel_id=1, source_target_pairs={{0,16},{8,24},{16,0},{24,8},{1,17},{9,25},{17,1},{25,9},{2,18},{10... | collective-permute-start | bytes 405512 | tf_op jit(solution)/shard_map/ppermute | solution.py:348
  14.1 5.4 %collective-permute-start.1 = (f32[2,2,2,4224]{3,2,1,0:T(2,128)S(1)}, f32[2,2,2,4224]{3,2,1,0:T(2,128)S(1)}, u32[]{:S(2)}, u32[]{:S(2)}) collective-permute-start(f32[2,2,2,4224]{3,2,1,0:T(2,128)S(1)} %pad_maximum_fusion.own_hbm), channel_id=1, source_target_pairs={{0,24},{8,0},{16,8},{24,16},{1,25},{9,1},{17,9},{25,17},{2,26},{10... | collective-permute-start | bytes 405512 | tf_op jit(solution)/shard_map/ppermute | solution.py:348
  19.5 0.7 copy-start.2
  19.5 0.7 copy-start.3
  19.5 0.7 copy-start.4
  76.1 4.5 %collective-permute-start.4 = (f32[16,2,8,2048]{3,2,1,0:T(8,128)}, f32[16,2,8,2048]{3,2,1,0:T(8,128)S(1)}, u32[]{:S(2)}, u32[]{:S(2)}) collective-permute-start(f32[16,2,8,2048]{3,2,1,0:T(8,128)} %get-tuple-element.8), channel_id=1, source_target_pairs={{0,32},{32,0},{1,33},{33,1},{2,34},{34,2},{3,35},{35,3},{4,36},{36... | collective-permute-start | bytes 6291464 | tf_op jit(solution)/shard_map/ppermute | solution.py:348
  82.6 10.8 %collective-permute-start.12 = (f32[4,8,2048]{2,1,0:T(8,128)S(1)}, f32[4,8,2048]{2,1,0:T(8,128)S(1)}, u32[]{:S(2)}, u32[]{:S(2)}) collective-permute-start(f32[4,8,2048]{2,1,0:T(8,128)S(1)} %get-tuple-element.9), channel_id=1, source_target_pairs={{0,64},{4,68},{64,0},{68,4},{1,65},{5,69},{65,1},{69,5},{2,66},{6,... | collective-permute-start | bytes 786440 | tf_op jit(solution)/shard_map/ppermute | solution.py:348
  84.7 13.5 %collective-permute-start.11 = (f32[4,8,2048]{2,1,0:T(8,128)S(1)}, f32[4,8,2048]{2,1,0:T(8,128)S(1)}, u32[]{:S(2)}, u32[]{:S(2)}) collective-permute-start(f32[4,8,2048]{2,1,0:T(8,128)S(1)} %get-tuple-element.10), channel_id=1, source_target_pairs={{0,4},{4,64},{64,68},{68,0},{1,5},{5,65},{65,69},{69,1},{2,6},{6,6... | collective-permute-start | bytes 786440 | tf_op jit(solution)/shard_map/ppermute | solution.py:348
  85.3 12.9 %collective-permute-start.13 = (f32[4,8,2048]{2,1,0:T(8,128)S(1)}, f32[4,8,2048]{2,1,0:T(8,128)S(1)}, u32[]{:S(2)}, u32[]{:S(2)}) collective-permute-start(f32[4,8,2048]{2,1,0:T(8,128)S(1)} %get-tuple-element.11), channel_id=1, source_target_pairs={{0,68},{4,0},{64,4},{68,64},{1,69},{5,1},{65,5},{69,65},{2,70},{6,... | collective-permute-start | bytes 786440 | tf_op jit(solution)/shard_map/ppermute | solution.py:348
  88.0 15.0 %collective-permute-start.6 = (f32[4,8,2048]{2,1,0:T(8,128)S(1)}, f32[4,8,2048]{2,1,0:T(8,128)S(1)}, u32[]{:S(2)}, u32[]{:S(2)}) collective-permute-start(f32[4,8,2048]{2,1,0:T(8,128)S(1)} %get-tuple-element.12), channel_id=1, source_target_pairs={{0,2},{1,3},{2,0},{3,1},{4,6},{5,7},{6,4},{7,5},{8,10},{9,11},{10,... | collective-permute-start | bytes 786440 | tf_op jit(solution)/shard_map/ppermute | solution.py:348
  91.9 12.4 %collective-permute-start.7 = (f32[4,8,2048]{2,1,0:T(8,128)S(1)}, f32[4,8,2048]{2,1,0:T(8,128)S(1)}, u32[]{:S(2)}, u32[]{:S(2)}) collective-permute-start(f32[4,8,2048]{2,1,0:T(8,128)S(1)} %get-tuple-element.13), channel_id=1, source_target_pairs={{0,3},{1,0},{2,1},{3,2},{4,7},{5,4},{6,5},{7,6},{8,11},{9,8},{10,9... | collective-permute-start | bytes 786440 | tf_op jit(solution)/shard_map/ppermute | solution.py:348
  93.4 10.9 %collective-permute-start.5 = (f32[4,8,2048]{2,1,0:T(8,128)S(1)}, f32[4,8,2048]{2,1,0:T(8,128)S(1)}, u32[]{:S(2)}, u32[]{:S(2)}) collective-permute-start(f32[4,8,2048]{2,1,0:T(8,128)S(1)} %get-tuple-element.14), channel_id=1, source_target_pairs={{0,1},{1,2},{2,3},{3,0},{4,5},{5,6},{6,7},{7,4},{8,9},{9,10},{10,1... | collective-permute-start | bytes 786440 | tf_op jit(solution)/shard_map/ppermute | solution.py:348
  98.3 9.5 %collective-permute-start.15 = (f32[8,2048]{1,0:T(8,128)S(1)}, f32[8,2048]{1,0:T(8,128)S(1)}, u32[]{:S(2)}, u32[]{:S(2)}) collective-permute-start(f32[8,2048]{1,0:T(8,128)S(1)} %get-tuple-element.18), channel_id=1, source_target_pairs={{0,2},{1,3},{2,0},{3,1},{4,6},{5,7},{6,4},{7,5},{8,10},{9,11},{10,... | collective-permute-start | bytes 196616 | tf_op jit(solution)/shard_map/ppermute | solution.py:348
  102.2 6.0 %collective-permute-start.16 = (f32[8,2048]{1,0:T(8,128)S(1)}, f32[8,2048]{1,0:T(8,128)S(1)}, u32[]{:S(2)}, u32[]{:S(2)}) collective-permute-start(f32[8,2048]{1,0:T(8,128)S(1)} %get-tuple-element.19), channel_id=1, source_target_pairs={{0,3},{1,0},{2,1},{3,2},{4,7},{5,4},{6,5},{7,6},{8,11},{9,8},{10,9... | collective-permute-start | bytes 196616 | tf_op jit(solution)/shard_map/ppermute | solution.py:348
  103.0 5.5 %collective-permute-start.14 = (f32[8,2048]{1,0:T(8,128)S(1)}, f32[8,2048]{1,0:T(8,128)S(1)}, u32[]{:S(2)}, u32[]{:S(2)}) collective-permute-start(f32[8,2048]{1,0:T(8,128)S(1)} %get-tuple-element.20), channel_id=1, source_target_pairs={{0,1},{1,2},{2,3},{3,0},{4,5},{5,6},{6,7},{7,4},{8,9},{9,10},{10,1... | collective-permute-start | bytes 196616 | tf_op jit(solution)/shard_map/ppermute | solution.py:348
  104.4 6.3 %collective-permute-start.9 = (f32[8,2048]{1,0:T(8,128)S(1)}, f32[8,2048]{1,0:T(8,128)S(1)}, u32[]{:S(2)}, u32[]{:S(2)}) collective-permute-start(f32[8,2048]{1,0:T(8,128)S(1)} %get-tuple-element.15), channel_id=1, source_target_pairs={{0,64},{4,68},{64,0},{68,4},{1,65},{5,69},{65,1},{69,5},{2,66},{6,... | collective-permute-start | bytes 196616 | tf_op jit(solution)/shard_map/ppermute | solution.py:348
  106.2 4.5 %collective-permute-start.10 = (f32[8,2048]{1,0:T(8,128)S(1)}, f32[8,2048]{1,0:T(8,128)S(1)}, u32[]{:S(2)}, u32[]{:S(2)}) collective-permute-start(f32[8,2048]{1,0:T(8,128)S(1)} %get-tuple-element.16), channel_id=1, source_target_pairs={{0,68},{4,0},{64,4},{68,64},{1,69},{5,1},{65,5},{69,65},{2,70},{6,... | collective-permute-start | bytes 196616 | tf_op jit(solution)/shard_map/ppermute | solution.py:348
  107.7 5.5 %collective-permute-start.8 = (f32[8,2048]{1,0:T(8,128)S(1)}, f32[8,2048]{1,0:T(8,128)S(1)}, u32[]{:S(2)}, u32[]{:S(2)}) collective-permute-start(f32[8,2048]{1,0:T(8,128)S(1)} %get-tuple-element.17), channel_id=1, source_target_pairs={{0,4},{4,64},{64,68},{68,0},{1,5},{5,65},{65,69},{69,1},{2,6},{6,6... | collective-permute-start | bytes 196616 | tf_op jit(solution)/shard_map/ppermute | solution.py:348
